TPU v7x, 512 devices: a whole 4x8x8 slice. The times are simulated.
512 devices in a mesh: row: 16 (over y, core), col: 32 (over x, z).
Axes of the slice: x: 4, y: 8, z: 8, core: 2. Of those that a mesh axis runs over, the one named last changes fastest.
Arguments:
- w_cycle: bfloat16 [1536, 24576], P('row', 'col'), may hold values from -0.109375 to 0.109375
- amplitudes: bfloat16 [192, 192, 128, 128], P('col', None, 'row'), may hold values from -6 to 6
- occ_count: int32 [8], replicated, may hold values from 1 to 24, 120 in all
- virt_count: int32 [8], replicated, may hold values from 1 to 128, 680 in all
- target: int32 [1], replicated, may hold values from 0 to 7
Outputs:
- cycle: bfloat16 [1536, 24576], P('col', 'row')
Inputs may be any that keep to these rules, and one draw needn't show every extreme that they name: `occ_count`: in stored slot order; they sum to 120, and some irrep has exactly 24. `virt_count`: in stored slot order; they sum to 680, and some irrep has exactly 128.
All inputs are finite; a program needn't handle non-finite values.
Results may differ from a plain program's by a relative error of at most 0.019.
Values may be sent and summed in bfloat16 or wider, within the bound.
No kernel may reach another device: no remote copies, remote signals or barrier semaphores. Data moves between devices by JAX's collectives and lax.ppermute only.
A program may use at most 64 MiB of HBM per device.

v0:
```python
import jax
import jax.numpy as jnp
from jax import lax
from jax.sharding import PartitionSpec as P

IRREPS = 8
OCAP = 24
VCAP = 128
IW = 12
KO = 192


def pair_valid(occ_count, virt_count, target):
    slot_ids = jnp.arange(IRREPS * OCAP, dtype=jnp.int32)
    irrep_of = slot_ids // OCAP
    labels = jnp.arange(IRREPS, dtype=jnp.int32)
    pick_occ = (irrep_of[:, None] == labels[None, :]).astype(jnp.int32)
    occupied = jnp.sum(pick_occ * occ_count[None, :], axis=1)
    partner = jnp.bitwise_xor(irrep_of, target[0])
    pick_virt = (partner[:, None] == labels[None, :]).astype(jnp.int32)
    virtual = jnp.sum(pick_virt * virt_count[None, :], axis=1)
    column = jnp.arange(VCAP, dtype=jnp.int32)
    valid_pairs = (slot_ids % OCAP < occupied)[:, None] & (column[None, :] < virtual[:, None])
    return valid_pairs.astype(jnp.float32)


def per_device(w_cycle, amplitudes, occ_count, virt_count, target):
    valid_pairs = pair_valid(occ_count, virt_count, target)
    k_local = amplitudes.shape[0]
    col_index = lax.axis_index("col")
    row_index = lax.axis_index("row")
    k_valid = lax.dynamic_slice_in_dim(valid_pairs, col_index * k_local, k_local, 0)
    k_mask = k_valid[:, :, None, None].astype(jnp.bfloat16)
    landed = lax.all_to_all(amplitudes, "row", split_axis=1, concat_axis=2, tiled=True)
    arrived = jnp.transpose(landed, (0, 2, 1, 3))
    arrived = arrived * k_mask
    j_local = arrived.shape[2]
    amp_matrix = arrived.reshape(k_local * VCAP, j_local * VCAP)
    rows_out = w_cycle.shape[0] * lax.axis_size("row") // lax.axis_size("col")
    partial_value = jnp.dot(
        lax.all_gather(w_cycle, "row", axis=0, tiled=True),
        amp_matrix,
        preferred_element_type=jnp.float32,
    )
    summed = lax.psum_scatter(
        partial_value.astype(jnp.bfloat16), "col", scatter_dimension=0, tiled=True
    ).astype(jnp.float32)
    jb_local = amp_matrix.shape[1]
    row_mask = lax.dynamic_slice_in_dim(
        valid_pairs[:IW].reshape(IW * VCAP), col_index * rows_out, rows_out, 0
    )
    col_mask = lax.dynamic_slice_in_dim(
        valid_pairs.reshape(KO * VCAP), row_index * jb_local, jb_local, 0
    )
    return (summed * row_mask[:, None] * col_mask[None, :]).astype(jnp.bfloat16)


def solution(mesh):
    placed = (P("row", "col"), P("col", None, "row", None), P(), P(), P())
    return jax.shard_map(
        per_device, mesh=mesh, in_specs=placed, out_specs=P("col", "row"), check_vma=False
    )
```

profile of v0, /device:TPU:1, one launch (start us, length us, event | category | flops | bytes accessed | tf_op | source)
XLA Modules:
  0.0 340.8 jit_solution(11883909307189451363)
XLA Ops:
  6.5 3.5 %copy.22 = bf16[6,192,8,128]{3,2,0,1:T(8,128)(2,1)} copy(bf16[6,192,8,128]{3,2,1,0:T(8,128)(2,1)} %param.6) | data formatting | bytes 4718592 | tf_op args[1]
  10.0 0.0 copy-start
  10.0 0.0 copy-start.1
  10.0 10.5 %all-to-all-start = ((bf16[6,192,8,128]{3,2,0,1:T(8,128)(2,1)}), bf16[6,192,8,128]{3,2,0,1:T(8,128)(2,1)S(1)}, u32[]{:S(2)}, u32[]{:S(2)}) async-start(bf16[6,192,8,128]{3,2,0,1:T(8,128)(2,1)} %copy.22), calls=%async_computation | async-start | bytes 4718592 | tf_op jit(solution)/shard_map/all_to_all | solution.py:34
  20.5 0.0 all-gather.2.cloned.1.call-start
  20.6 0.7 all-gather.2.cloned.1.call-update
  21.3 0.0 reduce-scatter.4.cloned.1.call-start
  22.0 0.0 copy-done
  22.0 0.1 select_reduce_fusion
  22.1 0.0 copy-done.1
  22.1 0.1 select_reduce_fusion.1
  22.2 0.1 fusion.6
  22.4 62.1 %all-to-all-done = bf16[6,192,8,128]{3,2,0,1:T(8,128)(2,1)S(1)} async-done(((bf16[6,192,8,128]{3,2,0,1:T(8,128)(2,1)}), bf16[6,192,8,128]{3,2,0,1:T(8,128)(2,1)S(1)}, u32[]{:S(2)}, u32[]{:S(2)}) %all-to-all-start) | async-done | bytes 2359328 | tf_op jit(solution)/shard_map/all_to_all | solution.py:34
  84.5 0.4 fusion.3
  84.9 1.6 copy.25
  86.5 4.3 %all-gather.2.cloned.1.call-done = bf16[1536,768]{1,0:T(8,128)(2,1)} async-done(((bf16[96,768]{1,0:T(8,128)(2,1)}), bf16[1536,768]{1,0:T(8,128)(2,1)}) %all-gather.2.cloned.1.call-update) | async-done | bytes 2359312 | tf_op jit(solution)/shard_map/all_gather | solution.py:41
  90.8 7.3 %fusion = bf16[1536,1536]{0,1:T(8,128)(2,1)} fusion(bf16[1536,768]{1,0:T(8,128)(2,1)} %all-gather.2.cloned.1.call-done, bf16[96,8,12,128]{3,2,1,0:T(8,128)(2,1)S(1)} %bitcast.25), kind=kOutput, calls=%fused_computation.1 | convolution fusion | flops 3626237952 | bytes 9437184 | tf_op jit(solution)/shard_map/dot_general | solution.py:40
  98.1 6.7 %copy.28 = bf16[1536,1536]{1,0:T(8,128)(2,1)} copy(bf16[1536,1536]{0,1:T(8,128)(2,1)} %fusion) | data formatting | bytes 9437184
  104.8 0.0 reduce-scatter.4.cloned.1.call-update
  104.8 0.1 dynamic_slice.11
  104.9 0.1 dynamic_slice.10
  105.0 227.3 %reduce-scatter.4.cloned.1.call-done = bf16[48,1536]{1,0:T(8,128)(2,1)} async-done(((bf16[1536,1536]{1,0:T(8,128)(2,1)}), bf16[48,1536]{1,0:T(8,128)(2,1)}) %reduce-scatter.4.cloned.1.call-update) | async-done | bytes 147472 | tf_op jit(solution)/shard_map/reduce_scatter | solution.py:45
  332.3 1.7 multiply_convert_fusion
  (5 shorter events, 0.1 us)
Async XLA Ops:
  10.0 12.0 %copy-start = (s32[8]{0:T(128)S(1)}, s32[8]{0:T(128)}, u32[]{:S(2)}) copy-start(s32[8]{0:T(128)} %param.8) | copy-start | bytes 100
  10.0 12.1 %copy-start.1 = (s32[8]{0:T(128)S(1)}, s32[8]{0:T(128)}, u32[]{:S(2)}) copy-start(s32[8]{0:T(128)} %param.7) | copy-start | bytes 100
  10.0 74.4 %all-to-all-start = ((bf16[6,192,8,128]{3,2,0,1:T(8,128)(2,1)}), bf16[6,192,8,128]{3,2,0,1:T(8,128)(2,1)S(1)}, u32[]{:S(2)}, u32[]{:S(2)}) async-start(bf16[6,192,8,128]{3,2,0,1:T(8,128)(2,1)} %copy.22), calls=%async_computation | async-start | bytes 4718592 | tf_op jit(solution)/shard_map/all_to_all | solution.py:34
  20.5 70.2 %all-gather.2.cloned.1.call-start = ((), (), s32[]{:S(2)}) async-start(), calls=%async_computation.2 | async-start | bytes 2506752 | tf_op jit(solution)/shard_map/all_gather | solution.py:41
  21.3 311.0 %reduce-scatter.4.cloned.1.call-start = ((), (), s32[]{:S(2)}) async-start(), calls=%async_computation.3 | async-start | bytes 4866048 | tf_op jit(solution)/shard_map/reduce_scatter | solution.py:45
Sparse Core Ops, SparseCore 0:
  23.5 67.2 all-gather.1
  104.9 227.2 reduce-scatter.3
where the time goes:
time: 345 us; the launch traced here: 341 us
  waiting for transfers between devices  294 us (85%)
  between operations  14.1 us (4%)
  local copies, waits for them, and re-layouts  12 us (3%)
  starting transfers between devices  10.6 us (3%)
  matrix products  7.34 us (2%)
    reduce_scatter x1, waiting for transfers between devices, per_device(): lax.psum_scatter(partial_value.astype(jnp.bfloat16), 'col', scatter_dimen...  227 us
    all_to_all x1, waiting for transfers between devices, per_device(): lax.all_to_all(amplitudes, 'row', split_axis=1, concat_axis=2, tiled=True)  62.1 us
    all_to_all x1, starting transfers between devices, per_device(): lax.all_to_all(amplitudes, 'row', split_axis=1, concat_axis=2, tiled=True)  10.5 us
    unnamed x6, local copies, waits for them, and re-layouts  10.2 us
    dot_general x1, matrix products, per_device(): jnp.dot(lax.all_gather(w_cycle, 'row', axis=0, tiled=True), amp_matrix, p...  7.34 us
  transfers between devices with their start and end apart: 3, of which 3 were waited for; matrix products, arithmetic and copies ran while one was open for 1% of the time, Pallas kernels for 0%

commit v1 on v0

v1 whole, which is shorter than its diff:
```python
import jax
import jax.numpy as jnp
from jax import lax
from jax.experimental import pallas as pl
from jax.experimental.pallas import tpu as pltpu
from jax.sharding import Mesh, PartitionSpec as P

IRREPS = 8
OCAP = 24
VCAP = 128
KO = 192
ROWS = 16
TURNS = 8
BLOCK = 48
BF = jnp.bfloat16
F32 = jnp.float32


def scalars():
    return pl.BlockSpec(memory_space=pltpu.SMEM)


def deal_kernel(occ, t_ref, out_ref):
    def put(p, value):
        out_ref[lax.rem(p, ROWS), 0, lax.div(p, ROWS)] = value

    first = jnp.int32(0)
    for h in range(IRREPS):
        def one(s, carry, h=h, first=first):
            slot = h * OCAP + s
            put(first + s, jnp.concatenate([t_ref[0, slot], t_ref[1, slot]], axis=0))
            return carry

        lax.fori_loop(0, occ[h], one, 0)
        first = first + occ[h]

    def rest(p, carry):
        put(p, jnp.zeros((16, VCAP), BF))
        return carry

    lax.fori_loop(first, ROWS * TURNS, rest, 0)


def deal(amplitudes, occ_count):
    return pl.pallas_call(
        deal_kernel,
        grid=(3,),
        in_specs=[scalars(), pl.BlockSpec((2, KO, 8, VCAP), lambda i: (i, 0, 0, 0))],
        out_specs=pl.BlockSpec((ROWS, 1, TURNS, 16, VCAP), lambda i: (0, i, 0, 0, 0)),
        out_shape=jax.ShapeDtypeStruct((ROWS, 3, TURNS, 16, VCAP), BF),
        compiler_params=pltpu.CompilerParams(vmem_limit_bytes=32 << 20),
        name="deal",
    )(occ_count, amplitudes)


def order_kernel(where, occ, virt, target, w_ref, out_ref):
    kc = w_ref.shape[1]
    first_k = where[0] * 6
    irrep = first_k // OCAP
    k_base = first_k - irrep * OCAP
    n_occ = occ[irrep]
    n_virt = virt[jnp.bitwise_xor(irrep, target[0])]
    old = lax.broadcasted_iota(jnp.int32, (kc, kc), 0)
    new = lax.broadcasted_iota(jnp.int32, (kc, kc), 1)
    k, c = old // VCAP, old % VCAP
    goes = (c // 8) * 48 + k * 8 + c % 8
    keep = (goes == new) & (k + k_base < n_occ) & (c < n_virt)
    pick = jnp.where(keep, 1.0, 0.0).astype(BF)
    out_ref[...] = jnp.dot(w_ref[...], pick, preferred_element_type=F32).astype(BF)


def order(w_cycle, col, occ_count, virt_count, target):
    return pl.pallas_call(
        order_kernel,
        in_specs=[scalars()] * 4 + [pl.BlockSpec(memory_space=pltpu.VMEM)],
        out_specs=pl.BlockSpec(memory_space=pltpu.VMEM),
        out_shape=jax.ShapeDtypeStruct(w_cycle.shape, BF),
        compiler_params=pltpu.CompilerParams(vmem_limit_bytes=32 << 20),
        name="order",
    )(col, occ_count, virt_count, target, w_cycle)


def product_kernel(w_ref, t_ref, out_ref):
    depth = w_ref.shape[1]
    right = jnp.concatenate(
        [t_ref[:, 0].reshape(depth, VCAP), t_ref[:, 1].reshape(depth, VCAP)], axis=1
    )
    for x in range(4):
        part = jnp.dot(w_ref[x * 384:(x + 1) * 384, :], right, preferred_element_type=F32)
        for z in range(8):
            at = z * 192 + x * BLOCK
            out_ref[at:at + BLOCK, :] = part[z * BLOCK:(z + 1) * BLOCK].astype(BF)


def product(w_rows, landed):
    rows, depth = w_rows.shape
    width = 2 * VCAP
    return pl.pallas_call(
        product_kernel,
        grid=(TURNS // 2,),
        in_specs=[
            pl.BlockSpec((rows, depth), lambda i: (0, 0)),
            pl.BlockSpec((depth // 16, 2, 16, VCAP), lambda i: (0, i, 0, 0)),
        ],
        out_specs=pl.BlockSpec((rows, width), lambda i: (0, i)),
        out_shape=jax.ShapeDtypeStruct((rows, TURNS * VCAP), BF),
        compiler_params=pltpu.CompilerParams(vmem_limit_bytes=40 << 20),
        name="product",
    )(w_rows, landed)


def first_of(occ, irrep):
    total = jnp.int32(0)
    for h in range(IRREPS):
        total = total + jnp.where(h < irrep, occ[h], 0)
    return total


def send_kernel(where, occ, parts_ref, out_ref):
    mine = where[0]
    first = jnp.int32(0)
    for h in range(IRREPS):
        near = lax.rem(mine - first + 8 * ROWS, ROWS)
        for e in range(2):
            s = near if e == 0 else jnp.where(near < 12, near + ROWS, near)
            turn = jnp.clip((first + s) // ROWS, 0, TURNS - 1)
            at = pl.ds(pl.multiple_of(turn * VCAP, VCAP), VCAP)
            total = parts_ref[0, :, at].astype(F32)
            for x in range(1, 4):
                total = total + parts_ref[x, :, at].astype(F32)
            out_ref[2 * h + e] = total.astype(BF)
        first = first + occ[h]


def send_out(parts, row, occ_count):
    return pl.pallas_call(
        send_kernel,
        in_specs=[scalars()] * 2 + [pl.BlockSpec(memory_space=pltpu.VMEM)],
        out_specs=pl.BlockSpec(memory_space=pltpu.VMEM),
        out_shape=jax.ShapeDtypeStruct((ROWS, BLOCK, VCAP), BF),
        compiler_params=pltpu.CompilerParams(vmem_limit_bytes=32 << 20),
        name="send_out",
    )(row, occ_count, parts)


def place_kernel(where, occ, virt, target, got_ref, out_ref):
    row, col = where[0], where[1]
    irrep, half = row // 2, row % 2
    first = first_of(occ, irrep)
    n_virt = virt[jnp.bitwise_xor(irrep, target[0])]
    line = col * BLOCK + lax.broadcasted_iota(jnp.int32, (BLOCK, VCAP), 0)
    b = lax.broadcasted_iota(jnp.int32, (BLOCK, VCAP), 1)
    inside = (line // VCAP < occ[0]) & (line % VCAP < virt[target[0]]) & (b < n_virt)
    for l in range(12):
        s = half * 12 + l
        block = got_ref[lax.rem(first + s, ROWS)].astype(F32)
        keep = inside & (s < occ[irrep])
        out_ref[:, l * VCAP:(l + 1) * VCAP] = jnp.where(keep, block, 0.0).astype(BF)


def place(got, where, occ_count, virt_count, target):
    return pl.pallas_call(
        place_kernel,
        in_specs=[scalars()] * 4 + [pl.BlockSpec(memory_space=pltpu.VMEM)],
        out_specs=pl.BlockSpec(memory_space=pltpu.VMEM),
        out_shape=jax.ShapeDtypeStruct((BLOCK, 12 * VCAP), BF),
        compiler_params=pltpu.CompilerParams(vmem_limit_bytes=32 << 20),
        name="place",
    )(where, occ_count, virt_count, target, got)


def per_device(w_cycle, amplitudes, occ_count, virt_count, target):
    row = lax.axis_index("y") * 2 + lax.axis_index("core")
    col = lax.axis_index("x") * 8 + lax.axis_index("z")
    row, col = row.astype(jnp.int32), col.astype(jnp.int32)
    line = ("y", "core")
    w_rows = lax.all_gather(
        order(w_cycle, col[None], occ_count, virt_count, target), line, axis=0, tiled=True
    )
    landed = lax.all_to_all(deal(amplitudes, occ_count), line, 0, 0, tiled=True)
    landed = landed.reshape(ROWS * 3, TURNS, 16, VCAP)
    partial = product(w_rows, landed)
    by_z = lax.psum_scatter(partial, "z", scatter_dimension=0, tiled=True)
    by_x = lax.all_to_all(by_z, "x", 0, 0, tiled=True).reshape(4, BLOCK, TURNS * VCAP)
    got = lax.all_to_all(send_out(by_x, row[None], occ_count), line, 0, 0, tiled=True)
    return place(got, jnp.stack([row, col]), occ_count, virt_count, target)


def solution(mesh):
    chips = Mesh(mesh.devices.reshape(8, 2, 4, 8), ("y", "core", "x", "z"))
    row, col = ("y", "core"), ("x", "z")
    placed = (P(row, col), P(col, None, row, None), P(), P(), P())
    return jax.shard_map(
        per_device, mesh=chips, in_specs=placed, out_specs=P(col, row), check_vma=False
    )
```

time: 345 us -> 172 us (0.50); the launches traced: 341 us -> 172 us
  waiting for transfers between devices: 294 us -> 63.2 us
  blocking collectives: 0 us -> 60.2 us
  Pallas kernels: 0 us -> 12.8 us
  matrix products: 7.34 us -> 0 us
  local copies, waits for them, and re-layouts: 12 us -> 6.2 us
  starting transfers between devices: 10.6 us -> 15.3 us
    reduce_scatter x1, waiting for transfers between devices: 227 us -> 46.7 us  [per_device(): by_z = lax.psum_scatter(partial, 'z', scatter_dimension=0, tiled=True)]
    all_to_all x0 -> x1, blocking collectives: none -> 60.2 us  [per_device(): landed = lax.all_to_all(deal(amplitudes, occ_count), line, 0, 0, tiled=True)]
    all_to_all x1 -> x2, waiting for transfers between devices: 62.1 us -> 16.5 us  [the longest x1 10.2 us: per_device(): lax.all_to_all(send_out(by_x, row[None], occ_count), line, 0, 0, tiled=True)]
    pallas_call x0 -> x5, Pallas kernels: none -> 12.8 us  [the longest x1 4.39 us: product(): pl.pallas_call(product_kernel, grid=(TURNS // 2,), in_specs=[pl.BlockSpec...]
    dot_general x1 -> x0, matrix products: 7.34 us -> none  [per_device(): jnp.dot(lax.all_gather(w_cycle, 'row', axis=0, tiled=True), amp_matrix, p...]
    all_to_all x1 -> x2, starting transfers between devices: 10.5 us -> 15.3 us  [the longest x1 11.3 us: per_device(): lax.all_to_all(send_out(by_x, row[None], occ_count), line, 0, 0, tiled=True)]
    all_gather x1, waiting for transfers between devices: 4.26 us -> 0.01 us  [per_device(): lax.all_gather(order(w_cycle, col[None], occ_count, virt_count, target),...]
    unnamed x6 -> x16, local copies, waits for them, and re-layouts: 10.2 us -> 6.2 us
  transfers between devices with their start and end apart: 3 -> 4, of which waited for: 3 -> 3; matrix products, arithmetic and copies ran while one was open for 1% -> 0% of each run, Pallas kernels for 0% -> 2%
where the time goes in v1:
time: 172 us
  waiting for transfers between devices  63.2 us (37%)
  blocking collectives  60.2 us (35%)
  starting transfers between devices  15.3 us (9%)
  between operations  14.1 us (8%)
  Pallas kernels  12.8 us (7%)
  local copies, waits for them, and re-layouts  6.2 us (4%)
    all_to_all x1, blocking collectives, per_device(): landed = lax.all_to_all(deal(amplitudes, occ_count), line, 0, 0, tiled=True)  60.2 us
    reduce_scatter x1, waiting for transfers between devices, per_device(): by_z = lax.psum_scatter(partial, 'z', scatter_dimension=0, tiled=True)  46.7 us
    all_to_all x1, starting transfers between devices, per_device(): lax.all_to_all(send_out(by_x, row[None], occ_count), line, 0, 0, tiled=True)  11.3 us
    all_to_all x1, waiting for transfers between devices, per_device(): lax.all_to_all(send_out(by_x, row[None], occ_count), line, 0, 0, tiled=True)  10.2 us
    all_to_all x1, waiting for transfers between devices, per_device(): lax.all_to_all(by_z, 'x', 0, 0, tiled=True).reshape(4, BLOCK, TURNS * VCAP)  6.23 us
    unnamed x16, local copies, waits for them, and re-layouts  6.2 us
    pallas_call x1, Pallas kernels, product(): pl.pallas_call(product_kernel, grid=(TURNS // 2,), in_specs=[pl.BlockSpec...  4.39 us
    all_to_all x1, starting transfers between devices, per_device(): lax.all_to_all(by_z, 'x', 0, 0, tiled=True).reshape(4, BLOCK, TURNS * VCAP)  4.02 us
  transfers between devices with their start and end apart: 4, of which 3 were waited for; matrix products, arithmetic and copies ran while one was open for 0% of the time, Pallas kernels for 2%

profile of v1, /device:TPU:1, one launch (start us, length us, event | category | flops | bytes accessed | tf_op | source)
XLA Modules:
  0.0 171.9 jit_solution(14815057345904914413)
XLA Ops:
  6.5 0.0 all-gather.2.cloned.1.call-start
  7.2 0.0 copy-start.2
  7.2 0.9 copy-done.2
  8.1 0.0 copy-start.3
  8.1 0.7 copy-done.3
  8.8 0.0 copy-start.6
  8.8 0.7 copy-done.6
  9.4 1.8 %order.1 = bf16[96,768]{1,0:T(8,128)(2,1)} custom-call(s32[1]{0:T(128)} %bitcast.1.where, s32[8]{0:T(128)S(1)} %copy-done.3, s32[8]{0:T(128)S(1)} %copy-done.6, s32[1]{0:T(128)S(6)} %copy.6.target, bf16[96,768]{1,0:T(8,128)(2,1)S(1)} %copy-done.2), custom_call_target="tpu_custom_call" | custom-call | tf_op jit(solution)/shard_map/order/pallas_call | solution.py:73
  11.2 0.0 all-gather.2.cloned.1.call-update
  11.3 0.0 reduce-scatter.2.cloned.1.call-start
  11.3 0.0 copy-start.1
  11.3 1.7 copy-done.1
  13.0 0.0 copy-start.4
  13.0 0.7 copy-done.4
  13.6 3.9 %deal.1 = bf16[16,3,8,16,128]{4,3,2,1,0:T(8,128)(2,1)S(1)} custom-call(s32[8]{0:T(128)S(1)} %copy-done.4, bf16[6,192,8,128]{3,2,1,0:T(8,128)(2,1)S(1)} %copy-done.1), custom_call_target="tpu_custom_call" | custom-call | tf_op jit(solution)/shard_map/deal/pallas_call | solution.py:45
  17.5 60.2 %all_to_all.19 = bf16[16,3,8,16,128]{4,3,2,1,0:T(8,128)(2,1)S(1)} all-to-all(bf16[16,3,8,16,128]{4,3,2,1,0:T(8,128)(2,1)S(1)} %deal.1), channel_id=1, replica_groups=mesh['y'=8,'core'=2,'x'=4,'z'=8] {'y','core'}, dimensions={0} | all-to-all | bytes 3145728 | tf_op jit(solution)/shard_map/all_to_all | solution.py:180
  77.7 0.0 all-gather.2.cloned.1.call-done.w_ref
  77.7 0.0 copy-start
  77.7 1.7 copy-done
  79.4 4.4 %product.1 = bf16[1536,1024]{1,0:T(8,128)(2,1)} custom-call(bf16[1536,768]{1,0:T(8,128)(2,1)S(1)} %copy-done, bf16[48,8,16,128]{3,2,1,0:T(8,128)(2,1)S(1)} %bitcast.4), custom_call_target="tpu_custom_call" | custom-call | tf_op jit(solution)/shard_map/product/pallas_call | solution.py:98
  83.8 0.0 copy-start.5
  83.8 0.0 reduce-scatter.2.cloned.1.call-update
  83.8 46.7 %reduce-scatter.2.cloned.1.call-done = bf16[192,1024]{1,0:T(8,128)(2,1)} async-done(((bf16[1536,1024]{1,0:T(8,128)(2,1)}), bf16[192,1024]{1,0:T(8,128)(2,1)}) %reduce-scatter.2.cloned.1.call-update) | async-done | bytes 393232 | tf_op jit(solution)/shard_map/reduce_scatter | solution.py:183
  130.5 4.0 %all-to-all-start.1 = ((bf16[4,48,1024]{2,1,0:T(8,128)(2,1)}), bf16[4,48,1024]{2,1,0:T(8,128)(2,1)S(1)}, u32[]{:S(2)}, u32[]{:S(2)}) async-start(bf16[4,48,1024]{2,1,0:T(8,128)(2,1)} %bitcast.5), calls=%async_computation.2 | async-start | bytes 786432 | tf_op jit(solution)/shard_map/all_to_all | solution.py:184
  134.5 6.2 %all-to-all-done.1.parts_ref = bf16[4,48,1024]{2,1,0:T(8,128)(2,1)S(1)} async-done(((bf16[4,48,1024]{2,1,0:T(8,128)(2,1)}), bf16[4,48,1024]{2,1,0:T(8,128)(2,1)S(1)}, u32[]{:S(2)}, u32[]{:S(2)}) %all-to-all-start.1) | async-done | bytes 393248 | tf_op jit(solution)/shard_map/all_to_all | solution.py:184
  140.7 0.0 copy-done.5
  140.7 1.4 send_out.1
  142.2 11.3 %all-to-all-start.2 = ((bf16[16,48,128]{2,1,0:T(8,128)(2,1)}), bf16[16,48,128]{2,1,0:T(8,128)(2,1)S(1)}, u32[]{:S(2)}, u32[]{:S(2)}) async-start(bf16[16,48,128]{2,1,0:T(8,128)(2,1)} %send_out.1), calls=%async_computation.3 | async-start | bytes 393216 | tf_op jit(solution)/shard_map/all_to_all | solution.py:185
  153.4 0.1 pad_add_fusion.where
  153.5 10.2 %all-to-all-done.2.got_ref = bf16[16,48,128]{2,1,0:T(8,128)(2,1)S(1)} async-done(((bf16[16,48,128]{2,1,0:T(8,128)(2,1)}), bf16[16,48,128]{2,1,0:T(8,128)(2,1)S(1)}, u32[]{:S(2)}, u32[]{:S(2)}) %all-to-all-start.2) | async-done | bytes 196640 | tf_op jit(solution)/shard_map/all_to_all | solution.py:185
  163.8 0.0 copy-done.7
  163.8 1.3 place.1
  (1 shorter events, 0.0 us)
Async XLA Ops:
  6.5 71.2 %all-gather.2.cloned.1.call-start = ((), (), s32[]{:S(2)}) async-start(), calls=%async_computation.4 | async-start | bytes 2506752 | tf_op jit(solution)/shard_map/all_gather | solution.py:177
  7.2 0.9 copy-start.2
  8.1 0.7 copy-start.3
  8.8 0.7 copy-start.6
  11.3 119.2 %reduce-scatter.2.cloned.1.call-start = ((), (), s32[]{:S(2)}) async-start(), calls=%async_computation.5 | async-start | bytes 3538944 | tf_op jit(solution)/shard_map/reduce_scatter | solution.py:183
  11.3 1.7 copy-start.1
  13.0 0.7 copy-start.4
  77.7 1.7 copy-start
  83.8 56.9 %copy-start.5 = (s32[8]{0:T(128)S(1)}, s32[8]{0:T(128)}, u32[]{:S(2)}) copy-start(s32[8]{0:T(128)} %occ.7) | copy-start | bytes 100
  83.8 80.0 %copy-start.7 = (s32[8]{0:T(128)S(1)}, s32[8]{0:T(128)}, u32[]{:S(2)}) copy-start(s32[8]{0:T(128)} %virt.3) | copy-start | bytes 100
  130.5 10.3 %all-to-all-start.1 = ((bf16[4,48,1024]{2,1,0:T(8,128)(2,1)}), bf16[4,48,1024]{2,1,0:T(8,128)(2,1)S(1)}, u32[]{:S(2)}, u32[]{:S(2)}) async-start(bf16[4,48,1024]{2,1,0:T(8,128)(2,1)} %bitcast.5), calls=%async_computation.2 | async-start | bytes 786432 | tf_op jit(solution)/shard_map/all_to_all | solution.py:184
  142.2 21.6 %all-to-all-start.2 = ((bf16[16,48,128]{2,1,0:T(8,128)(2,1)}), bf16[16,48,128]{2,1,0:T(8,128)(2,1)S(1)}, u32[]{:S(2)}, u32[]{:S(2)}) async-start(bf16[16,48,128]{2,1,0:T(8,128)(2,1)} %send_out.1), calls=%async_computation.3 | async-start | bytes 393216 | tf_op jit(solution)/shard_map/all_to_all | solution.py:185
Sparse Core Ops, SparseCore 0:
  11.4 64.9 all-gather.1
  83.9 46.4 reduce-scatter.1

commit v2 on v1

v2 whole, which is shorter than its diff:
```python
import functools

import jax
import jax.numpy as jnp
from jax import lax
from jax.experimental import pallas as pl
from jax.experimental.pallas import tpu as pltpu
from jax.sharding import Mesh, PartitionSpec as P

IRREPS = 8
OCAP = 24
VCAP = 128
KO = 192
ROWS = 16
TURNS = 8
EARLY = 6
LATE = TURNS - EARLY
BLOCK = 48
BF = jnp.bfloat16
F32 = jnp.float32


def scalars():
    return pl.BlockSpec(memory_space=pltpu.SMEM)


def slot_table(occ, table):
    first = jnp.int32(0)
    for h in range(IRREPS):
        def one(s, carry, h=h, first=first):
            table[first + s] = h * OCAP + s
            return carry

        lax.fori_loop(0, occ[h], one, 0)
        first = first + occ[h]

    def rest(p, carry):
        table[p] = KO - 1
        return carry

    lax.fori_loop(first, ROWS * TURNS, rest, 0)


def deal_kernel(occ, t_ref, early_ref, late_ref, table):
    @pl.when(pl.program_id(0) == 0)
    def _():
        slot_table(occ, table)

    for turn in range(TURNS):
        for q in range(ROWS):
            slot = table[turn * ROWS + q]
            both = jnp.concatenate([t_ref[0, slot], t_ref[1, slot]], axis=0)
            if turn < EARLY:
                early_ref[q, 0, turn] = both
            else:
                late_ref[q, 0, turn - EARLY] = both


def deal(amplitudes, occ_count):
    def out(turns):
        return pl.BlockSpec((ROWS, 1, turns, 16, VCAP), lambda i: (0, i, 0, 0, 0))

    def shape(turns):
        return jax.ShapeDtypeStruct((ROWS, 3, turns, 16, VCAP), BF)

    return pl.pallas_call(
        deal_kernel,
        grid=(3,),
        in_specs=[scalars(), pl.BlockSpec((2, KO, 8, VCAP), lambda i: (i, 0, 0, 0))],
        out_specs=[out(EARLY), out(LATE)],
        out_shape=[shape(EARLY), shape(LATE)],
        scratch_shapes=[pltpu.SMEM((ROWS * TURNS,), jnp.int32)],
        compiler_params=pltpu.CompilerParams(vmem_limit_bytes=56 << 20),
        name="deal",
    )(occ_count, amplitudes)


def product_kernel(by_reduction, where, occ, virt, target, w_ref, t_ref, out_ref, right):
    depth, width = right.shape

    @pl.when(pl.program_id(0) == 0)
    def _():
        first_k = where[1] * 6
        irrep = first_k // OCAP
        k_base = first_k - irrep * OCAP
        n_occ = occ[irrep]
        n_virt = virt[jnp.bitwise_xor(irrep, target[0])]
        c = lax.broadcasted_iota(jnp.int32, (VCAP, VCAP), 0)
        for turn in range(width // VCAP):
            held = t_ref[:, turn].astype(F32).reshape(ROWS, 3, 2, 8, VCAP)
            for k in range(6):
                limit = jnp.where(k_base + k < n_occ, n_virt, 0)
                value = jnp.where(c < limit, held[:, k // 2, k % 2].reshape(VCAP, VCAP), 0.0)
                right[k * VCAP:(k + 1) * VCAP, turn * VCAP:(turn + 1) * VCAP] = value.astype(BF)

    part = jnp.dot(w_ref[...], right[...], preferred_element_type=F32)
    if by_reduction:
        for z in range(8):
            out_ref[z, 0] = part[z * BLOCK:(z + 1) * BLOCK].astype(BF)
    else:
        out_ref[...] = part.astype(BF)


def product(by_reduction, w_rows, landed, where, occ_count, virt_count, target):
    rows, depth = w_rows.shape
    turns = landed.shape[1]
    width = turns * VCAP
    if by_reduction:
        out_spec = pl.BlockSpec((8, 1, BLOCK, width), lambda i: (0, i, 0, 0))
        out_shape = jax.ShapeDtypeStruct((8, 4, BLOCK, width), BF)
    else:
        out_spec = pl.BlockSpec((rows // 4, width), lambda i: (i, 0))
        out_shape = jax.ShapeDtypeStruct((rows, width), BF)
    out = pl.pallas_call(
        functools.partial(product_kernel, by_reduction),
        grid=(4,),
        in_specs=[scalars()] * 4 + [
            pl.BlockSpec((rows // 4, depth), lambda i: (i, 0)),
            pl.BlockSpec((depth // 16, turns, 16, VCAP), lambda i: (0, 0, 0, 0)),
        ],
        out_specs=out_spec,
        out_shape=out_shape,
        scratch_shapes=[pltpu.VMEM((depth, width), BF)],
        compiler_params=pltpu.CompilerParams(vmem_limit_bytes=56 << 20),
        name="product_early" if by_reduction else "product_late",
    )(where, occ_count, virt_count, target, w_rows, landed)
    return out.reshape(rows, width)


def first_of(occ, irrep):
    total = jnp.int32(0)
    for h in range(IRREPS):
        total = total + jnp.where(h < irrep, occ[h], 0)
    return total


def send_kernel(where, occ, early_ref, late_ref, out_ref, total):
    for turn in range(TURNS):
        parts = early_ref if turn < EARLY else late_ref
        at = (turn if turn < EARLY else turn - EARLY) * VCAP
        added = parts[0, :, at:at + VCAP].astype(F32)
        for x in range(1, parts.shape[0]):
            added = added + parts[x, :, at:at + VCAP].astype(F32)
        total[turn] = added.astype(BF)
    mine = where[0]
    first = jnp.int32(0)
    for h in range(IRREPS):
        near = lax.rem(mine - first + 8 * ROWS, ROWS)
        for e in range(2):
            s = near if e == 0 else jnp.where(near < 12, near + ROWS, near)
            out_ref[2 * h + e] = total[jnp.clip((first + s) // ROWS, 0, TURNS - 1)]
        first = first + occ[h]


def send_out(early, late, where, occ_count):
    return pl.pallas_call(
        send_kernel,
        in_specs=[scalars()] * 2 + [pl.BlockSpec(memory_space=pltpu.VMEM)] * 2,
        out_specs=pl.BlockSpec(memory_space=pltpu.VMEM),
        out_shape=jax.ShapeDtypeStruct((ROWS, BLOCK, VCAP), BF),
        scratch_shapes=[pltpu.VMEM((TURNS, BLOCK, VCAP), BF)],
        compiler_params=pltpu.CompilerParams(vmem_limit_bytes=32 << 20),
        name="send_out",
    )(where, occ_count, early, late)


def place_kernel(where, occ, virt, target, got_ref, out_ref):
    row, col = where[0], where[1]
    irrep, half = row // 2, row % 2
    first = first_of(occ, irrep)
    n_virt = virt[jnp.bitwise_xor(irrep, target[0])]
    line = col * BLOCK + lax.broadcasted_iota(jnp.int32, (BLOCK, VCAP), 0)
    b = lax.broadcasted_iota(jnp.int32, (BLOCK, VCAP), 1)
    inside = (line // VCAP < occ[0]) & (line % VCAP < virt[target[0]]) & (b < n_virt)
    for l in range(12):
        s = half * 12 + l
        block = got_ref[lax.rem(first + s, ROWS)].astype(F32)
        keep = inside & (s < occ[irrep])
        out_ref[:, l * VCAP:(l + 1) * VCAP] = jnp.where(keep, block, 0.0).astype(BF)


def place(got, where, occ_count, virt_count, target):
    return pl.pallas_call(
        place_kernel,
        in_specs=[scalars()] * 4 + [pl.BlockSpec(memory_space=pltpu.VMEM)],
        out_specs=pl.BlockSpec(memory_space=pltpu.VMEM),
        out_shape=jax.ShapeDtypeStruct((BLOCK, 12 * VCAP), BF),
        compiler_params=pltpu.CompilerParams(vmem_limit_bytes=32 << 20),
        name="place",
    )(where, occ_count, virt_count, target, got)


def per_device(w_cycle, amplitudes, occ_count, virt_count, target):
    row = lax.axis_index("y") * 2 + lax.axis_index("core")
    col = lax.axis_index("x") * 8 + lax.axis_index("z")
    where = jnp.stack([row, col]).astype(jnp.int32)
    masks = (where, occ_count, virt_count, target)
    line = ("y", "core")
    w_rows = lax.all_gather(w_cycle, line, axis=0, tiled=True)
    early, late = deal(amplitudes, occ_count)
    early = lax.all_to_all(early, line, 0, 0, tiled=True).reshape(ROWS * 3, EARLY, 16, VCAP)
    early = product(True, w_rows, early, *masks)
    early, late = lax.optimization_barrier((early, late))
    early = lax.psum_scatter(early, "z", scatter_dimension=0, tiled=True)
    late = lax.all_to_all(late, line, 0, 0, tiled=True).reshape(ROWS * 3, LATE, 16, VCAP)
    late = product(False, w_rows, late, *masks)
    late = lax.all_to_all(late, ("x", "z"), 0, 0, tiled=True).reshape(32, BLOCK, LATE * VCAP)
    early = lax.all_to_all(early, "x", 0, 0, tiled=True).reshape(4, BLOCK, EARLY * VCAP)
    got = lax.all_to_all(send_out(early, late, where, occ_count), line, 0, 0, tiled=True)
    return place(got, *masks)


def solution(mesh):
    chips = Mesh(mesh.devices.reshape(8, 2, 4, 8), ("y", "core", "x", "z"))
    row, col = ("y", "core"), ("x", "z")
    placed = (P(row, col), P(col, None, row, None), P(), P(), P())
    return jax.shard_map(
        per_device, mesh=chips, in_specs=placed, out_specs=P(col, row), check_vma=False
    )
```

time: 172 us -> 175 us (1.017)
  blocking collectives: 60.2 us -> 83.7 us
  waiting for transfers between devices: 63.2 us -> 47.1 us
  local copies, waits for them, and re-layouts: 6.2 us -> 0.99 us
  starting transfers between devices: 15.3 us -> 10.4 us
  Pallas kernels: 12.8 us -> 17 us
    reduce_scatter x1, waiting for transfers between devices: 46.7 us -> 0.01 us  [per_device(): early = lax.psum_scatter(early, 'z', scatter_dimension=0, tiled=True)]
    all_to_all x1 -> x4, blocking collectives: 60.2 us -> 83.7 us  [the longest x1 36.4 us: per_device(): lax.all_to_all(late, ('x', 'z'), 0, 0, tiled=True)]
    all_to_all x2 -> x1, waiting for transfers between devices: 16.5 us -> 35.4 us  [per_device(): lax.all_to_all(early, line, 0, 0, tiled=True)]
    all_gather x1, waiting for transfers between devices: 0.01 us -> 10.9 us  [per_device(): w_rows = lax.all_gather(w_cycle, line, axis=0, tiled=True)]
    unnamed x16 -> x10, local copies, waits for them, and re-layouts: 6.2 us -> 0.99 us
    all_to_all x2 -> x1, starting transfers between devices: 15.3 us -> 10.4 us  [per_device(): lax.all_to_all(early, line, 0, 0, tiled=True)]
    pallas_call x2, Pallas kernels: 6.21 us -> 10.4 us  [product(): pl.pallas_call(functools.partial(product_kernel, by_reduction), grid=(4,)...]
  transfers between devices with their start and end apart: 4 -> 3, of which waited for: 3 -> 2; matrix products, arithmetic and copies ran while one was open for 0% -> 0% of each run, Pallas kernels for 2% -> 5%
where the time goes in v2:
time: 175 us; the launch traced here: 174 us
  blocking collectives  83.7 us (48%)
  waiting for transfers between devices  47.1 us (27%)
  Pallas kernels  17 us (10%)
  between operations  14.1 us (8%)
  starting transfers between devices  10.4 us (6%)
    all_to_all x1, blocking collectives, per_device(): lax.all_to_all(late, ('x', 'z'), 0, 0, tiled=True)  36.4 us
    all_to_all x1, waiting for transfers between devices, per_device(): lax.all_to_all(early, line, 0, 0, tiled=True)  35.4 us
    all_to_all x1, blocking collectives, per_device(): lax.all_to_all(late, line, 0, 0, tiled=True)  18.8 us
    all_to_all x1, blocking collectives, per_device(): lax.all_to_all(send_out(early, late, where, occ_count), line, 0, 0, tiled...  18.5 us
    all_gather x1, waiting for transfers between devices, per_device(): w_rows = lax.all_gather(w_cycle, line, axis=0, tiled=True)  10.9 us
    pallas_call x2, Pallas kernels, product(): pl.pallas_call(functools.partial(product_kernel, by_reduction), grid=(4,)...  10.4 us
    all_to_all x1, starting transfers between devices, per_device(): lax.all_to_all(early, line, 0, 0, tiled=True)  10.4 us
    all_to_all x1, blocking collectives, per_device(): lax.all_to_all(early, 'x', 0, 0, tiled=True).reshape(4, BLOCK, EARLY * VCAP)  10.1 us
  transfers between devices with their start and end apart: 3, of which 2 were waited for; matrix products, arithmetic and copies ran while one was open for 0% of the time, Pallas kernels for 5%

profile of v2, /device:TPU:1, one launch (start us, length us, event | category | flops | bytes accessed | tf_op | source)
XLA Modules:
  0.0 173.9 jit_solution(3332971641136453331)
XLA Ops:
  6.5 0.0 all-gather.2.cloned.1.call-start
  6.5 0.7 all-gather.2.cloned.1.call-update
  7.3 4.6 %deal.1 = (bf16[16,3,6,16,128]{4,3,2,1,0:T(8,128)(2,1)}, bf16[16,3,2,16,128]{4,3,2,1,0:T(8,128)(2,1)}) custom-call(s32[8]{0:T(128)} %occ.9, bf16[6,192,8,128]{3,2,1,0:T(8,128)(2,1)} %t_ref.1), custom_call_target="tpu_custom_call" | custom-call | tf_op jit(solution)/shard_map/deal/pallas_call | solution.py:66
  11.8 10.4 %all-to-all-start = ((bf16[16,3,6,16,128]{4,3,2,1,0:T(8,128)(2,1)}), bf16[16,3,6,16,128]{4,3,2,1,0:T(8,128)(2,1)S(1)}, u32[]{:S(2)}, u32[]{:S(2)}) async-start(bf16[16,3,6,16,128]{4,3,2,1,0:T(8,128)(2,1)} %get-tuple-element.9), calls=%async_computation | async-start | bytes 2359296 | tf_op jit(solution)/shard_map/all_to_all | solution.py:201
  22.2 0.0 reduce-scatter.2.cloned.1.call-start
  22.9 0.6 pad_add_fusion.where
  23.6 35.4 %all-to-all-done = bf16[16,3,6,16,128]{4,3,2,1,0:T(8,128)(2,1)S(1)} async-done(((bf16[16,3,6,16,128]{4,3,2,1,0:T(8,128)(2,1)}), bf16[16,3,6,16,128]{4,3,2,1,0:T(8,128)(2,1)S(1)}, u32[]{:S(2)}, u32[]{:S(2)}) %all-to-all-start) | async-done | bytes 1179680 | tf_op jit(solution)/shard_map/all_to_all | solution.py:201
  59.0 0.0 copy-start.3
  59.0 10.9 %all-gather.2.cloned.1.call-done.w_ref = bf16[1536,768]{1,0:T(8,128)(2,1)} async-done(((bf16[96,768]{1,0:T(8,128)(2,1)}), bf16[1536,768]{1,0:T(8,128)(2,1)}) %all-gather.2.cloned.1.call-update) | async-done | bytes 2359312 | tf_op jit(solution)/shard_map/all_gather | solution.py:199
  69.9 0.0 copy-done.3
  69.9 5.9 %product_early.1 = bf16[8,4,48,768]{3,2,1,0:T(8,128)(2,1)} custom-call(s32[2]{0:T(128)} %pad_add_fusion.where, s32[8]{0:T(128)} %occ.9, s32[8]{0:T(128)} %virt.5, s32[1]{0:T(128)S(6)} %copy.6.target, bf16[1536,768]{1,0:T(8,128)(2,1)} %all-gather.2.cloned.1.call-done.w_ref, bf16[48,6,16,128]{3,2,1,0:T(8,128)(2,1)} %bitcast.8), custom_call_target="tpu_custom_call" | custom-call | tf_op jit(solution)/shard_map/product_early/pallas_call | solution.py:114
  75.8 0.0 copy-start.4
  75.8 0.0 reduce-scatter.2.cloned.1.call-update
  75.9 1.0 copy-done.4
  76.8 18.8 %all_to_all.33 = bf16[16,3,2,16,128]{4,3,2,1,0:T(8,128)(2,1)} all-to-all(bf16[16,3,2,16,128]{4,3,2,1,0:T(8,128)(2,1)S(1)} %copy-done.4), channel_id=1, replica_groups=mesh['y'=8,'core'=2,'x'=4,'z'=8] {'y','core'}, dimensions={0} | all-to-all | bytes 786432 | tf_op jit(solution)/shard_map/all_to_all | solution.py:205
  95.6 0.0 copy-start
  95.6 0.0 copy-start.1
  95.6 4.5 %product_late.1 = bf16[1536,256]{1,0:T(8,128)(2,1)} custom-call(s32[2]{0:T(128)} %pad_add_fusion.where, s32[8]{0:T(128)} %occ.9, s32[8]{0:T(128)} %virt.5, s32[1]{0:T(128)S(6)} %copy.6.target, bf16[1536,768]{1,0:T(8,128)(2,1)} %all-gather.2.cloned.1.call-done.w_ref, bf16[48,2,16,128]{3,2,1,0:T(8,128)(2,1)} %bitcast.10), custom_call_target="tpu_custom_call" | custom-call | tf_op jit(solution)/shard_map/product_late/pallas_call | solution.py:114
  100.1 0.0 copy-start.2
  100.1 36.4 %all_to_all.34.late_ref = bf16[32,48,256]{2,1,0:T(8,128)(2,1)S(1)} all-to-all(bf16[32,48,256]{2,1,0:T(8,128)(2,1)} %bitcast.9), channel_id=1, replica_groups=mesh['y'=8,'core'=2,'x'=4,'z'=8] {'x','z'}, dimensions={0} | all-to-all | bytes 1572864 | tf_op jit(solution)/shard_map/all_to_all | solution.py:207
  136.5 0.0 reduce-scatter.2.cloned.1.call-done
  136.5 10.1 %all_to_all.35.early_ref = bf16[4,48,768]{2,1,0:T(8,128)(2,1)S(1)} all-to-all(bf16[4,48,768]{2,1,0:T(8,128)(2,1)} %bitcast.11), channel_id=1, replica_groups=mesh['y'=8,'core'=2,'x'=4,'z'=8] {'x'}, dimensions={0} | all-to-all | bytes 589824 | tf_op jit(solution)/shard_map/all_to_all | solution.py:208
  146.6 0.0 copy-done
  146.6 0.0 copy-done.1
  146.6 0.7 send_out.1
  147.3 18.5 %all_to_all.36.got_ref = bf16[16,48,128]{2,1,0:T(8,128)(2,1)S(1)} all-to-all(bf16[16,48,128]{2,1,0:T(8,128)(2,1)S(1)} %send_out.1), channel_id=1, replica_groups=mesh['y'=8,'core'=2,'x'=4,'z'=8] {'y','core'}, dimensions={0} | all-to-all | bytes 393216 | tf_op jit(solution)/shard_map/all_to_all | solution.py:209
  165.8 0.0 copy-done.2
  165.8 1.3 place.1
Async XLA Ops:
  6.5 63.4 %all-gather.2.cloned.1.call-start = ((), (), s32[]{:S(2)}) async-start(), calls=%async_computation.6 | async-start | bytes 2506752 | tf_op jit(solution)/shard_map/all_gather | solution.py:199
  11.8 47.2 %all-to-all-start = ((bf16[16,3,6,16,128]{4,3,2,1,0:T(8,128)(2,1)}), bf16[16,3,6,16,128]{4,3,2,1,0:T(8,128)(2,1)S(1)}, u32[]{:S(2)}, u32[]{:S(2)}) async-start(bf16[16,3,6,16,128]{4,3,2,1,0:T(8,128)(2,1)} %get-tuple-element.9), calls=%async_computation | async-start | bytes 2359296 | tf_op jit(solution)/shard_map/all_to_all | solution.py:201
  22.2 114.3 %reduce-scatter.2.cloned.1.call-start = ((), (), s32[]{:S(2)}) async-start(), calls=%async_computation.7 | async-start | bytes 2654208 | tf_op jit(solution)/shard_map/reduce_scatter | solution.py:204
  59.0 10.9 %copy-start.3 = (bf16[16,3,6,16,128]{4,3,2,1,0:T(8,128)(2,1)}, bf16[16,3,6,16,128]{4,3,2,1,0:T(8,128)(2,1)S(1)}, u32[]{:S(2)}) copy-start(bf16[16,3,6,16,128]{4,3,2,1,0:T(8,128)(2,1)S(1)} %all-to-all-done) | copy-start | bytes 3538948
  75.8 1.0 copy-start.4
  95.6 51.0 %copy-start = (s32[8]{0:T(128)S(1)}, s32[8]{0:T(128)}, u32[]{:S(2)}) copy-start(s32[8]{0:T(128)} %occ.9) | copy-start | bytes 100
  95.6 51.0 %copy-start.1 = (s32[2]{0:T(128)S(1)}, s32[2]{0:T(128)}, u32[]{:S(2)}) copy-start(s32[2]{0:T(128)} %pad_add_fusion.where) | copy-start | bytes 28
  100.1 65.7 %copy-start.2 = (s32[8]{0:T(128)S(1)}, s32[8]{0:T(128)}, u32[]{:S(2)}) copy-start(s32[8]{0:T(128)} %virt.5) | copy-start | bytes 100
Sparse Core Ops, SparseCore 0:
  9.5 60.4 all-gather.1
  76.0 46.9 reduce-scatter.1

commit v3 on v2

v3 whole, which is shorter than its diff:
```python
import jax
import jax.numpy as jnp
from jax import lax
from jax.experimental import pallas as pl
from jax.experimental.pallas import tpu as pltpu
from jax.sharding import Mesh, PartitionSpec as P

IRREPS = 8
OCAP = 24
VCAP = 128
KO = 192
ROWS = 16
TURNS = 8
BLOCK = 48
BF = jnp.bfloat16
F32 = jnp.float32


def scalars():
    return pl.BlockSpec(memory_space=pltpu.SMEM)


def slot_table(occ, table):
    first = jnp.int32(0)
    for h in range(IRREPS):
        def one(s, carry, h=h, first=first):
            table[first + s] = h * OCAP + s
            return carry

        lax.fori_loop(0, occ[h], one, 0)
        first = first + occ[h]

    def rest(p, carry):
        table[p] = KO - 1
        return carry

    lax.fori_loop(first, ROWS * TURNS, rest, 0)


def deal_kernel(occ, t_ref, out_ref, table):
    @pl.when(pl.program_id(0) == 0)
    def _():
        slot_table(occ, table)

    for turn in range(TURNS):
        for q in range(ROWS):
            slot = table[turn * ROWS + q]
            out_ref[q, 0, turn] = t_ref[0, slot]
            out_ref[q, 1, turn] = t_ref[1, slot]


def deal(amplitudes, occ_count):
    return pl.pallas_call(
        deal_kernel,
        grid=(3,),
        in_specs=[scalars(), pl.BlockSpec((2, KO, 8, VCAP), lambda i: (i, 0, 0, 0))],
        out_specs=pl.BlockSpec((ROWS, 2, TURNS, 8, VCAP), lambda i: (0, i, 0, 0, 0)),
        out_shape=jax.ShapeDtypeStruct((ROWS, 6, TURNS, 8, VCAP), BF),
        scratch_shapes=[pltpu.SMEM((ROWS * TURNS,), jnp.int32)],
        compiler_params=pltpu.CompilerParams(vmem_limit_bytes=56 << 20),
        name="deal",
    )(occ_count, amplitudes)


def repack_kernel(where, occ, virt, target, t_ref, out_ref):
    first_k = where[1] * 6
    irrep = first_k // OCAP
    k_base = first_k - irrep * OCAP
    n_occ = occ[irrep]
    n_virt = virt[jnp.bitwise_xor(irrep, target[0])]
    c = lax.broadcasted_iota(jnp.int32, (VCAP, VCAP), 0)
    for turn in range(t_ref.shape[1]):
        held = t_ref[:, turn].astype(F32).reshape(ROWS, 6, 8, VCAP)
        for k in range(6):
            limit = jnp.where(k_base + k < n_occ, n_virt, 0)
            value = jnp.where(c < limit, held[:, k].reshape(VCAP, VCAP), 0.0)
            out_ref[k * VCAP:(k + 1) * VCAP, turn * VCAP:(turn + 1) * VCAP] = value.astype(BF)


def repack(landed, where, occ_count, virt_count, target):
    return pl.pallas_call(
        repack_kernel,
        grid=(TURNS // 2,),
        in_specs=[scalars()] * 4 + [pl.BlockSpec((ROWS * 6, 2, 8, VCAP), lambda i: (0, i, 0, 0))],
        out_specs=pl.BlockSpec((6 * VCAP, 2 * VCAP), lambda i: (0, i)),
        out_shape=jax.ShapeDtypeStruct((6 * VCAP, TURNS * VCAP), BF),
        compiler_params=pltpu.CompilerParams(vmem_limit_bytes=56 << 20),
        name="repack",
    )(where, occ_count, virt_count, target, landed)


def product_kernel(w_ref, t_ref, out_ref):
    part = jnp.dot(w_ref[...], t_ref[...], preferred_element_type=F32)
    for z in range(8):
        out_ref[z, 0] = part[z * BLOCK:(z + 1) * BLOCK].astype(BF)


def product(w_rows, t_rows):
    rows, depth = w_rows.shape
    width = t_rows.shape[1]
    out = pl.pallas_call(
        product_kernel,
        grid=(4,),
        in_specs=[
            pl.BlockSpec((rows // 4, depth), lambda i: (i, 0)),
            pl.BlockSpec((depth, width), lambda i: (0, 0)),
        ],
        out_specs=pl.BlockSpec((8, 1, BLOCK, width), lambda i: (0, i, 0, 0)),
        out_shape=jax.ShapeDtypeStruct((8, 4, BLOCK, width), BF),
        compiler_params=pltpu.CompilerParams(vmem_limit_bytes=56 << 20),
        name="product",
    )(w_rows, t_rows)
    return out.reshape(rows, width)


def first_of(occ, irrep):
    total = jnp.int32(0)
    for h in range(IRREPS):
        total = total + jnp.where(h < irrep, occ[h], 0)
    return total


def send_kernel(where, occ, parts_ref, out_ref, total):
    for turn in range(TURNS):
        at = turn * VCAP
        added = parts_ref[0, :, at:at + VCAP].astype(F32)
        for x in range(1, 4):
            added = added + parts_ref[x, :, at:at + VCAP].astype(F32)
        total[turn] = added.astype(BF)
    mine = where[0]
    first = jnp.int32(0)
    for h in range(IRREPS):
        near = lax.rem(mine - first + 8 * ROWS, ROWS)
        for e in range(2):
            s = near if e == 0 else jnp.where(near < 12, near + ROWS, near)
            out_ref[2 * h + e] = total[jnp.clip((first + s) // ROWS, 0, TURNS - 1)]
        first = first + occ[h]


def send_out(parts, where, occ_count):
    return pl.pallas_call(
        send_kernel,
        in_specs=[scalars()] * 2 + [pl.BlockSpec(memory_space=pltpu.VMEM)],
        out_specs=pl.BlockSpec(memory_space=pltpu.VMEM),
        out_shape=jax.ShapeDtypeStruct((ROWS, BLOCK, VCAP), BF),
        scratch_shapes=[pltpu.VMEM((TURNS, BLOCK, VCAP), BF)],
        compiler_params=pltpu.CompilerParams(vmem_limit_bytes=32 << 20),
        name="send_out",
    )(where, occ_count, parts)


def place_kernel(where, occ, virt, target, got_ref, out_ref):
    row, col = where[0], where[1]
    irrep, half = row // 2, row % 2
    first = first_of(occ, irrep)
    n_virt = virt[jnp.bitwise_xor(irrep, target[0])]
    line = col * BLOCK + lax.broadcasted_iota(jnp.int32, (BLOCK, VCAP), 0)
    b = lax.broadcasted_iota(jnp.int32, (BLOCK, VCAP), 1)
    inside = (line // VCAP < occ[0]) & (line % VCAP < virt[target[0]]) & (b < n_virt)
    for l in range(12):
        s = half * 12 + l
        block = got_ref[lax.rem(first + s, ROWS)].astype(F32)
        keep = inside & (s < occ[irrep])
        out_ref[:, l * VCAP:(l + 1) * VCAP] = jnp.where(keep, block, 0.0).astype(BF)


def place(got, where, occ_count, virt_count, target):
    return pl.pallas_call(
        place_kernel,
        in_specs=[scalars()] * 4 + [pl.BlockSpec(memory_space=pltpu.VMEM)],
        out_specs=pl.BlockSpec(memory_space=pltpu.VMEM),
        out_shape=jax.ShapeDtypeStruct((BLOCK, 12 * VCAP), BF),
        compiler_params=pltpu.CompilerParams(vmem_limit_bytes=32 << 20),
        name="place",
    )(where, occ_count, virt_count, target, got)


def per_device(w_cycle, amplitudes, occ_count, virt_count, target):
    row = lax.axis_index("y") * 2 + lax.axis_index("core")
    col = lax.axis_index("x") * 8 + lax.axis_index("z")
    where = jnp.stack([row, col]).astype(jnp.int32)
    masks = (where, occ_count, virt_count, target)
    line = ("y", "core")
    w_rows = lax.all_gather(w_cycle, line, axis=0, tiled=True)
    landed = lax.all_to_all(deal(amplitudes, occ_count), line, 0, 0, tiled=True)
    t_rows = repack(landed.reshape(ROWS * 6, TURNS, 8, VCAP), *masks)
    partial = product(w_rows, t_rows)
    by_z = lax.psum_scatter(partial, "z", scatter_dimension=0, tiled=True)
    by_x = lax.all_to_all(by_z, "x", 0, 0, tiled=True).reshape(4, BLOCK, TURNS * VCAP)
    got = lax.all_to_all(send_out(by_x, where, occ_count), line, 0, 0, tiled=True)
    return place(got, *masks)


def solution(mesh):
    chips = Mesh(mesh.devices.reshape(8, 2, 4, 8), ("y", "core", "x", "z"))
    row, col = ("y", "core"), ("x", "z")
    placed = (P(row, col), P(col, None, row, None), P(), P(), P())
    return jax.shard_map(
        per_device, mesh=chips, in_specs=placed, out_specs=P(col, row), check_vma=False
    )
```

time: 175 us -> 172 us (0.983)
  blocking collectives: 83.7 us -> 31.7 us
  waiting for transfers between devices: 47.1 us -> 96.5 us
    all_to_all x4 -> x2, blocking collectives: 83.7 us -> 31.7 us  [the longest x1 21.6 us: per_device(): lax.all_to_all(send_out(by_x, where, occ_count), line, 0, 0, tiled=True)]
    reduce_scatter x1, waiting for transfers between devices: 0.01 us -> 47.9 us  [per_device(): by_z = lax.psum_scatter(partial, 'z', scatter_dimension=0, tiled=True)]
    all_to_all x1, waiting for transfers between devices: 35.4 us -> 44.5 us  [per_device(): landed = lax.all_to_all(deal(amplitudes, occ_count), line, 0, 0, tiled=True)]
    all_gather x1, waiting for transfers between devices: 10.9 us -> 3.38 us  [per_device(): w_rows = lax.all_gather(w_cycle, line, axis=0, tiled=True)]
  transfers between devices with their start and end apart: 3 -> 3, of which waited for: 2 -> 3; matrix products, arithmetic and copies ran while one was open for 0% -> 0% of each run, Pallas kernels for 5% -> 5%
where the time goes in v3:
time: 172 us; the launch traced here: 171 us
  waiting for transfers between devices  96.5 us (56%)
  blocking collectives  31.7 us (18%)
  Pallas kernels  16.7 us (10%)
  between operations  14.1 us (8%)
  starting transfers between devices  10.4 us (6%)
    reduce_scatter x1, waiting for transfers between devices, per_device(): by_z = lax.psum_scatter(partial, 'z', scatter_dimension=0, tiled=True)  47.9 us
    all_to_all x1, waiting for transfers between devices, per_device(): landed = lax.all_to_all(deal(amplitudes, occ_count), line, 0, 0, tiled=True)  44.5 us
    all_to_all x1, blocking collectives, per_device(): lax.all_to_all(send_out(by_x, where, occ_count), line, 0, 0, tiled=True)  21.6 us
    all_to_all x1, starting transfers between devices, per_device(): landed = lax.all_to_all(deal(amplitudes, occ_count), line, 0, 0, tiled=True)  10.4 us
    all_to_all x1, blocking collectives, per_device(): lax.all_to_all(by_z, 'x', 0, 0, tiled=True).reshape(4, BLOCK, TURNS * VCAP)  10.2 us
    pallas_call x1, Pallas kernels, product(): pl.pallas_call(product_kernel, grid=(4,), in_specs=[pl.BlockSpec((rows //...  6.25 us
    pallas_call x1, Pallas kernels, deal(): pl.pallas_call(deal_kernel, grid=(3,), in_specs=[scalars(), pl.BlockSpec(...  4.56 us
    pallas_call x1, Pallas kernels, repack(): pl.pallas_call(repack_kernel, grid=(TURNS // 2,), in_specs=[scalars()] *...  3.97 us
  transfers between devices with their start and end apart: 3, of which 3 were waited for; matrix products, arithmetic and copies ran while one was open for 0% of the time, Pallas kernels for 5%

profile of v3, /device:TPU:1, one launch (start us, length us, event | category | flops | bytes accessed | tf_op | source)
XLA Modules:
  0.0 171.2 jit_solution(11635494815017079036)
XLA Ops:
  6.5 0.0 all-gather.2.cloned.1.call-start
  6.5 0.7 all-gather.2.cloned.1.call-update
  7.3 4.6 %deal.1 = bf16[16,6,8,8,128]{4,3,2,1,0:T(8,128)(2,1)} custom-call(s32[8]{0:T(128)} %occ.7, bf16[6,192,8,128]{3,2,1,0:T(8,128)(2,1)} %t_ref.1), custom_call_target="tpu_custom_call" | custom-call | tf_op jit(solution)/shard_map/deal/pallas_call | solution.py:53
  11.8 10.4 %all-to-all-start = ((bf16[16,6,8,8,128]{4,3,2,1,0:T(8,128)(2,1)}), bf16[16,6,8,8,128]{4,3,2,1,0:T(8,128)(2,1)S(1)}, u32[]{:S(2)}, u32[]{:S(2)}) async-start(bf16[16,6,8,8,128]{4,3,2,1,0:T(8,128)(2,1)} %deal.1), calls=%async_computation | async-start | bytes 3145728 | tf_op jit(solution)/shard_map/all_to_all | solution.py:185
  22.2 0.0 reduce-scatter.2.cloned.1.call-start
  22.9 0.6 pad_add_fusion.where
  23.5 44.5 %all-to-all-done = bf16[16,6,8,8,128]{4,3,2,1,0:T(8,128)(2,1)S(1)} async-done(((bf16[16,6,8,8,128]{4,3,2,1,0:T(8,128)(2,1)}), bf16[16,6,8,8,128]{4,3,2,1,0:T(8,128)(2,1)S(1)}, u32[]{:S(2)}, u32[]{:S(2)}) %all-to-all-start) | async-done | bytes 1572896 | tf_op jit(solution)/shard_map/all_to_all | solution.py:185
  68.0 0.0 copy-start.3
  68.0 1.1 copy-done.3
  69.1 4.0 %repack.1.t_ref = bf16[768,1024]{1,0:T(8,128)(2,1)} custom-call(s32[2]{0:T(128)} %pad_add_fusion.where, s32[8]{0:T(128)} %occ.7, s32[8]{0:T(128)} %virt.3, s32[1]{0:T(128)S(6)} %copy.6.target, bf16[96,8,8,128]{3,2,1,0:T(8,128)(2,1)} %bitcast.6), custom_call_target="tpu_custom_call" | custom-call | tf_op jit(solution)/shard_map/repack/pallas_call | solution.py:81
  73.1 3.4 %all-gather.2.cloned.1.call-done.w_ref = bf16[1536,768]{1,0:T(8,128)(2,1)} async-done(((bf16[96,768]{1,0:T(8,128)(2,1)}), bf16[1536,768]{1,0:T(8,128)(2,1)}) %all-gather.2.cloned.1.call-update) | async-done | bytes 2359312 | tf_op jit(solution)/shard_map/all_gather | solution.py:184
  76.5 6.2 %product.1 = bf16[8,4,48,1024]{3,2,1,0:T(8,128)(2,1)} custom-call(bf16[1536,768]{1,0:T(8,128)(2,1)} %all-gather.2.cloned.1.call-done.w_ref, bf16[768,1024]{1,0:T(8,128)(2,1)} %repack.1.t_ref), custom_call_target="tpu_custom_call" | custom-call | tf_op jit(solution)/shard_map/product/pallas_call | solution.py:101
  82.7 0.0 copy-start
  82.7 0.0 copy-start.1
  82.7 0.0 copy-start.2
  82.7 0.0 reduce-scatter.2.cloned.1.call-update
  82.7 47.9 %reduce-scatter.2.cloned.1.call-done = bf16[192,1024]{1,0:T(8,128)(2,1)} async-done(((bf16[1536,1024]{1,0:T(8,128)(2,1)}), bf16[192,1024]{1,0:T(8,128)(2,1)}) %reduce-scatter.2.cloned.1.call-update) | async-done | bytes 393232 | tf_op jit(solution)/shard_map/reduce_scatter | solution.py:188
  130.7 10.2 %all_to_all.19.parts_ref = bf16[4,48,1024]{2,1,0:T(8,128)(2,1)S(1)} all-to-all(bf16[4,48,1024]{2,1,0:T(8,128)(2,1)} %bitcast.7), channel_id=1, replica_groups=mesh['y'=8,'core'=2,'x'=4,'z'=8] {'x'}, dimensions={0} | all-to-all | bytes 786432 | tf_op jit(solution)/shard_map/all_to_all | solution.py:189
  140.8 0.0 copy-done
  140.8 0.0 copy-done.1
  140.8 0.7 send_out.1
  141.5 21.6 %all_to_all.20.got_ref = bf16[16,48,128]{2,1,0:T(8,128)(2,1)S(1)} all-to-all(bf16[16,48,128]{2,1,0:T(8,128)(2,1)S(1)} %send_out.1), channel_id=1, replica_groups=mesh['y'=8,'core'=2,'x'=4,'z'=8] {'y','core'}, dimensions={0} | all-to-all | bytes 393216 | tf_op jit(solution)/shard_map/all_to_all | solution.py:190
  163.1 0.0 copy-done.2
  163.1 1.3 place.1
Async XLA Ops:
  6.5 69.9 %all-gather.2.cloned.1.call-start = ((), (), s32[]{:S(2)}) async-start(), calls=%async_computation.4 | async-start | bytes 2506752 | tf_op jit(solution)/shard_map/all_gather | solution.py:184
  11.8 56.2 %all-to-all-start = ((bf16[16,6,8,8,128]{4,3,2,1,0:T(8,128)(2,1)}), bf16[16,6,8,8,128]{4,3,2,1,0:T(8,128)(2,1)S(1)}, u32[]{:S(2)}, u32[]{:S(2)}) async-start(bf16[16,6,8,8,128]{4,3,2,1,0:T(8,128)(2,1)} %deal.1), calls=%async_computation | async-start | bytes 3145728 | tf_op jit(solution)/shard_map/all_to_all | solution.py:185
  22.2 108.5 %reduce-scatter.2.cloned.1.call-start = ((), (), s32[]{:S(2)}) async-start(), calls=%async_computation.5 | async-start | bytes 3538944 | tf_op jit(solution)/shard_map/reduce_scatter | solution.py:188
  68.0 1.1 copy-start.3
  82.7 58.1 %copy-start = (s32[8]{0:T(128)S(1)}, s32[8]{0:T(128)}, u32[]{:S(2)}) copy-start(s32[8]{0:T(128)} %occ.7) | copy-start | bytes 100
  82.7 58.1 %copy-start.1 = (s32[2]{0:T(128)S(1)}, s32[2]{0:T(128)}, u32[]{:S(2)}) copy-start(s32[2]{0:T(128)} %pad_add_fusion.where) | copy-start | bytes 28
  82.7 80.4 %copy-start.2 = (s32[8]{0:T(128)S(1)}, s32[8]{0:T(128)}, u32[]{:S(2)}) copy-start(s32[8]{0:T(128)} %virt.3) | copy-start | bytes 100
Sparse Core Ops, SparseCore 0:
  9.5 66.9 all-gather.1
  82.9 47.7 reduce-scatter.1

commit v4 on v3

v4 whole, which is shorter than its diff:
```python
import functools

import jax
import jax.numpy as jnp
from jax import lax
from jax.experimental import pallas as pl
from jax.experimental.pallas import tpu as pltpu
from jax.sharding import Mesh, PartitionSpec as P

IRREPS = 8
OCAP = 24
VCAP = 128
KO = 192
ROWS = 16
SIZES = (5, 6, 8)
STEP = 6
BLOCK = 48
BF = jnp.bfloat16
F32 = jnp.float32


def scalars():
    return pl.BlockSpec(memory_space=pltpu.SMEM)


def columns_of(occ, virt, target, irrep):
    return virt[jnp.bitwise_xor(irrep, target[0])]


def first_column(occ, virt, target, irrep):
    total = jnp.int32(0)
    for h in range(IRREPS):
        total = total + jnp.where(h < irrep, occ[h] * columns_of(occ, virt, target, h), 0)
    return total


def deal_kernel(occ, virt, target, t_ref, out_ref, held, sem):
    copies = [
        pltpu.make_async_copy(
            t_ref.at[:, h * OCAP:(h + 1) * OCAP], held.at[:, h * OCAP:(h + 1) * OCAP], sem.at[h]
        )
        for h in range(IRREPS)
    ]
    for copy in copies:
        copy.start()
    lane = lax.broadcasted_iota(jnp.int32, (48, VCAP), 1)

    def put(p, value):
        out_ref[jnp.bitwise_and(p, 15), :, lax.shift_right_logical(p, 4)] = (
            value.astype(BF).reshape(6, 8, VCAP)
        )

    current = jnp.zeros((48, VCAP), F32)
    first = jnp.int32(0)
    for h in range(IRREPS):
        copies[h].wait()
        many = occ[h]
        wide = columns_of(occ, virt, target, h)

        def some(g, current, h=h, first=first, many=many, wide=wide):
            for u in range(STEP):
                s = g * STEP + u
                at = first + jnp.minimum(s, many) * wide
                shift = jnp.bitwise_and(at, 127)
                value = held[:, h * OCAP + s].astype(F32).reshape(48, VCAP)
                value = pltpu.roll(value, shift, 1)
                current = jnp.where(lane >= shift, value, current)
                put(lax.shift_right_logical(at, 7), current)
                current = jnp.where((s < many) & (shift + wide >= VCAP), value, current)
            return current

        current = lax.fori_loop(0, (many + STEP - 1) // STEP, some, current)
        first = first + many * wide
    put(lax.shift_right_logical(first, 7), current)


def deal(turns, amplitudes, occ_count, virt_count, target):
    return pl.pallas_call(
        deal_kernel,
        in_specs=[scalars()] * 3 + [pl.BlockSpec(memory_space=pl.ANY)],
        out_specs=pl.BlockSpec(memory_space=pltpu.VMEM),
        out_shape=jax.ShapeDtypeStruct((ROWS, 6, turns, 8, VCAP), BF),
        scratch_shapes=[pltpu.VMEM((6, KO, 8, VCAP), BF), pltpu.SemaphoreType.DMA((IRREPS,))],
        compiler_params=pltpu.CompilerParams(vmem_limit_bytes=56 << 20),
        name="deal",
    )(occ_count, virt_count, target, amplitudes)


def repack_kernel(where, occ, virt, target, t_ref, out_ref):
    first_k = where[1] * 6
    irrep = first_k // OCAP
    k_base = first_k - irrep * OCAP
    n_occ = occ[irrep]
    n_virt = columns_of(occ, virt, target, irrep)
    c = lax.broadcasted_iota(jnp.int32, (VCAP, VCAP), 0)
    for turn in range(t_ref.shape[1]):
        held = t_ref[:, turn].astype(F32).reshape(ROWS, 6, 8, VCAP)
        for k in range(6):
            limit = jnp.where(k_base + k < n_occ, n_virt, 0)
            value = jnp.where(c < limit, held[:, k].reshape(VCAP, VCAP), 0.0)
            out_ref[k * VCAP:(k + 1) * VCAP, turn * VCAP:(turn + 1) * VCAP] = value.astype(BF)


def repack(landed, where, occ_count, virt_count, target):
    turns = landed.shape[1]
    return pl.pallas_call(
        repack_kernel,
        in_specs=[scalars()] * 4 + [pl.BlockSpec(memory_space=pltpu.VMEM)],
        out_specs=pl.BlockSpec(memory_space=pltpu.VMEM),
        out_shape=jax.ShapeDtypeStruct((6 * VCAP, turns * VCAP), BF),
        compiler_params=pltpu.CompilerParams(vmem_limit_bytes=24 << 20),
        name="repack",
    )(where, occ_count, virt_count, target, landed)


def product_kernel(w_ref, t_ref, out_ref, w_held, t_held, out_held, w_sem, t_sem, out_sem):
    tall = w_ref.shape[0] // 4
    t_copy = pltpu.make_async_copy(t_ref, t_held, t_sem)
    t_copy.start()
    w_copies = [
        pltpu.make_async_copy(
            w_ref.at[x * tall:(x + 1) * tall], w_held.at[x * tall:(x + 1) * tall], w_sem.at[x]
        )
        for x in range(4)
    ]
    for copy in w_copies:
        copy.start()
    t_copy.wait()
    out_copies = []
    for x in range(4):
        w_copies[x].wait()
        part = jnp.dot(
            w_held[x * tall:(x + 1) * tall, :], t_held[...], preferred_element_type=F32
        )
        for z in range(8):
            out_held[x, z] = part[z * BLOCK:(z + 1) * BLOCK].astype(BF)
        copy = pltpu.make_async_copy(out_held.at[x], out_ref.at[:, x], out_sem.at[x])
        copy.start()
        out_copies.append(copy)
    for copy in out_copies:
        copy.wait()


def product(w_rows, t_rows):
    rows, depth = w_rows.shape
    width = t_rows.shape[1]
    out = pl.pallas_call(
        product_kernel,
        in_specs=[pl.BlockSpec(memory_space=pl.ANY)] * 2,
        out_specs=pl.BlockSpec(memory_space=pl.ANY),
        out_shape=jax.ShapeDtypeStruct((8, 4, BLOCK, width), BF),
        scratch_shapes=[
            pltpu.VMEM((rows, depth), BF),
            pltpu.VMEM((depth, width), BF),
            pltpu.VMEM((4, 8, BLOCK, width), BF),
            pltpu.SemaphoreType.DMA((4,)),
            pltpu.SemaphoreType.DMA,
            pltpu.SemaphoreType.DMA((4,)),
        ],
        compiler_params=pltpu.CompilerParams(vmem_limit_bytes=56 << 20),
        name="product",
    )(w_rows, t_rows)
    return out.reshape(rows, width)


def send_kernel(where, occ, virt, target, parts_ref, out_ref, total):
    turns = total.shape[0]
    for turn in range(turns):
        at = turn * VCAP
        added = parts_ref[0, :, at:at + VCAP].astype(F32)
        for x in range(1, 4):
            added = added + parts_ref[x, :, at:at + VCAP].astype(F32)
        total[turn] = added.astype(BF)
    mine = where[0]
    first = jnp.int32(0)
    for h in range(IRREPS):
        wide = columns_of(occ, virt, target, h)
        for e in range(2):
            begin = lax.shift_right_logical(first + 12 * e * wide, 7)
            p = begin + jnp.bitwise_and(mine - begin + 16 * ROWS, 15)
            out_ref[2 * h + e] = total[jnp.minimum(lax.shift_right_logical(p, 4), turns - 1)]
        first = first + occ[h] * wide


def send_out(parts, where, occ_count, virt_count, target):
    return pl.pallas_call(
        send_kernel,
        in_specs=[scalars()] * 4 + [pl.BlockSpec(memory_space=pltpu.VMEM)],
        out_specs=pl.BlockSpec(memory_space=pltpu.VMEM),
        out_shape=jax.ShapeDtypeStruct((ROWS, BLOCK, VCAP), BF),
        scratch_shapes=[pltpu.VMEM((parts.shape[2] // VCAP, BLOCK, VCAP), BF)],
        compiler_params=pltpu.CompilerParams(vmem_limit_bytes=24 << 20),
        name="send_out",
    )(where, occ_count, virt_count, target, parts)


def place_kernel(where, occ, virt, target, got_ref, out_ref):
    row, col = where[0], where[1]
    irrep, half = row // 2, row % 2
    first = first_column(occ, virt, target, irrep)
    wide = columns_of(occ, virt, target, irrep)
    line = col * BLOCK + lax.broadcasted_iota(jnp.int32, (BLOCK, VCAP), 0)
    b = lax.broadcasted_iota(jnp.int32, (BLOCK, VCAP), 1)
    inside = (line // VCAP < occ[0]) & (line % VCAP < virt[target[0]]) & (b < wide)
    for l in range(12):
        s = half * 12 + l
        at = first + s * wide
        p = lax.shift_right_logical(at, 7)
        shift = jnp.bitwise_and(at, 127)
        here = got_ref[jnp.bitwise_and(p, 15)].astype(F32)
        after = got_ref[jnp.bitwise_and(p + 1, 15)].astype(F32)
        block = jnp.where(b >= shift, here, after)
        block = pltpu.roll(block, jnp.bitwise_and(VCAP - shift, 127), 1)
        keep = inside & (s < occ[irrep])
        out_ref[:, l * VCAP:(l + 1) * VCAP] = jnp.where(keep, block, 0.0).astype(BF)


def place(got, where, occ_count, virt_count, target):
    return pl.pallas_call(
        place_kernel,
        in_specs=[scalars()] * 4 + [pl.BlockSpec(memory_space=pltpu.VMEM)],
        out_specs=pl.BlockSpec(memory_space=pltpu.VMEM),
        out_shape=jax.ShapeDtypeStruct((BLOCK, 12 * VCAP), BF),
        compiler_params=pltpu.CompilerParams(vmem_limit_bytes=32 << 20),
        name="place",
    )(where, occ_count, virt_count, target, got)


def contract(turns, where, w_cycle, amplitudes, occ_count, virt_count, target):
    masks = (where, occ_count, virt_count, target)
    line = ("y", "core")
    w_rows = lax.all_gather(w_cycle, line, axis=0, tiled=True)
    dealt = deal(turns, amplitudes, occ_count, virt_count, target)
    landed = lax.all_to_all(dealt, line, 0, 0, tiled=True)
    t_rows = repack(landed.reshape(ROWS * 6, turns, 8, VCAP), *masks)
    partial = product(w_rows, t_rows)
    by_z = lax.psum_scatter(partial, "z", scatter_dimension=0, tiled=True)
    by_x = lax.all_to_all(by_z, "x", 0, 0, tiled=True).reshape(4, BLOCK, turns * VCAP)
    got = lax.all_to_all(send_out(by_x, *masks), line, 0, 0, tiled=True)
    return place(got, *masks)


def per_device(w_cycle, amplitudes, occ_count, virt_count, target):
    row = lax.axis_index("y") * 2 + lax.axis_index("core")
    col = lax.axis_index("x") * 8 + lax.axis_index("z")
    where = jnp.stack([row, col]).astype(jnp.int32)
    irreps = jnp.arange(IRREPS, dtype=jnp.int32)
    meets = jnp.bitwise_xor(irreps, target)[:, None] == irreps[None, :]
    pairs = jnp.sum(jnp.where(meets, occ_count[:, None] * virt_count[None, :], 0))
    case = sum((pairs > (ROWS * turns - 1) * VCAP).astype(jnp.int32) for turns in SIZES[:-1])
    return lax.switch(
        case,
        [functools.partial(contract, turns) for turns in SIZES],
        where, w_cycle, amplitudes, occ_count, virt_count, target,
    )


def solution(mesh):
    chips = Mesh(mesh.devices.reshape(8, 2, 4, 8), ("y", "core", "x", "z"))
    row, col = ("y", "core"), ("x", "z")
    placed = (P(row, col), P(col, None, row, None), P(), P(), P())
    return jax.shard_map(
        per_device, mesh=chips, in_specs=placed, out_specs=P(col, row), check_vma=False
    )
```

time: 172 us -> 159 us (0.924)
  waiting for transfers between devices: 96.5 us -> 47 us
  blocking collectives: 31.7 us -> 77.1 us
  starting transfers between devices: 10.4 us -> 0.08 us
    all_to_all x2 -> x3, blocking collectives: 31.7 us -> 77.1 us  [the longest x1 44.7 us: contract(): landed = lax.all_to_all(dealt, line, 0, 0, tiled=True)]
    all_to_all x1 -> x0, waiting for transfers between devices: 44.5 us -> none  [per_device(): landed = lax.all_to_all(deal(amplitudes, occ_count), line, 0, 0, tiled=True)]
    all_to_all x1 -> x0, starting transfers between devices: 10.4 us -> none  [per_device(): landed = lax.all_to_all(deal(amplitudes, occ_count), line, 0, 0, tiled=True)]
    reduce_scatter x1, waiting for transfers between devices: 47.9 us -> 39.2 us  [contract(): by_z = lax.psum_scatter(partial, 'z', scatter_dimension=0, tiled=True)]
    all_gather x1, waiting for transfers between devices: 3.38 us -> 7.03 us  [contract(): w_rows = lax.all_gather(w_cycle, line, axis=0, tiled=True)]
  transfers between devices with their start and end apart: 3 -> 2, of which waited for: 3 -> 2; matrix products, arithmetic and copies ran while one was open for 0% -> 0% of each run, Pallas kernels for 5% -> 5%
where the time goes in v4:
time: 159 us; the launch traced here: 158 us
  blocking collectives  77.1 us (48%)
  waiting for transfers between devices  47 us (30%)
  Pallas kernels  15.4 us (10%)
  between operations  15.3 us (10%)
  local copies, waits for them, and re-layouts  1.63 us (1%)
    all_to_all x1, blocking collectives, contract(): landed = lax.all_to_all(dealt, line, 0, 0, tiled=True)  44.7 us
    reduce_scatter x1, waiting for transfers between devices, contract(): by_z = lax.psum_scatter(partial, 'z', scatter_dimension=0, tiled=True)  39.2 us
    all_to_all x1, blocking collectives, contract(): got = lax.all_to_all(send_out(by_x, *masks), line, 0, 0, tiled=True)  23 us
    all_to_all x1, blocking collectives, contract(): lax.all_to_all(by_z, 'x', 0, 0, tiled=True).reshape(4, BLOCK, turns * VCAP)  9.42 us
    all_gather x1, waiting for transfers between devices, contract(): w_rows = lax.all_gather(w_cycle, line, axis=0, tiled=True)  7.03 us
    pallas_call x1, Pallas kernels, product(): pl.pallas_call(product_kernel, in_specs=[pl.BlockSpec(memory_space=pl.ANY...  5.7 us
    pallas_call x1, Pallas kernels, deal(): pl.pallas_call(deal_kernel, in_specs=[scalars()] * 3 + [pl.BlockSpec(memo...  5.65 us
  transfers between devices with their start and end apart: 2, of which 2 were waited for; matrix products, arithmetic and copies ran while one was open for 0% of the time, Pallas kernels for 5%

profile of v4, /device:TPU:1, one launch (start us, length us, event | category | flops | bytes accessed | tf_op | source)
XLA Modules:
  0.0 158.1 jit_solution(8998177288833571241)
XLA Ops:
  7.2 0.1 pad_add_fusion
  7.3 1.4 select_reduce_fusion
  9.9 140.7 %conditional.1 = (bf16[48,1536]{1,0:T(8,128)(2,1)S(1)}) conditional(s32[]{:T(128)} %clamp.3, (bf16[96,768]{1,0:T(8,128)(2,1)}, s32[8]{0:T(128)}, s32[8]{0:T(128)}, s32[1]{0:T(128)}, bf16[6,192,8,128]{3,2,1,0:T(8,128)(2,1)}, /*index=5*/s32[2]{0:T(128)S(1)}) %tuple.14, (bf16[96,768]{1,0:T(8,128)(2,1)}, s32[8]{0:T(128)}, s32[8]{0:T(128)}, ...), branch_computations={%region_1.3_spmd, %region_3.5_spmd, %region_5.7_spmd} | conditional | bytes 28754348 | solution.py:251
  10.0 0.0 all-gather.4.cloned.1.call-start
  10.0 0.7 all-gather.4.cloned.1.call-update
  10.7 0.0 reduce-scatter.4.cloned.1.call-start
  10.7 0.0 copy-start.4
  10.8 0.0 copy-start.7
  10.8 5.7 %deal.3 = bf16[16,6,5,8,128]{4,3,2,1,0:T(8,128)(2,1)} custom-call(s32[8]{0:T(128)} %get-tuple-element.46.occ, s32[8]{0:T(128)} %get-tuple-element.47.virt, s32[1]{0:T(128)} %get-tuple-element.48.target, bf16[6,192,8,128]{3,2,1,0:T(8,128)(2,1)} %get-tuple-element.73.t_ref), custom_call_target="tpu_custom_call" | custom-call | tf_op jit(solution)/shard_map/cond/branch_0_fun/deal/pallas_call | solution.py:78
  16.4 44.7 %all_to_all.45 = bf16[16,6,5,8,128]{4,3,2,1,0:T(8,128)(2,1)S(1)} all-to-all(bf16[16,6,5,8,128]{4,3,2,1,0:T(8,128)(2,1)} %deal.3), channel_id=1, replica_groups=mesh['y'=8,'core'=2,'x'=4,'z'=8] {'y','core'}, dimensions={0} | all-to-all | bytes 1966080 | tf_op jit(solution)/shard_map/cond/branch_0_fun/all_to_all | solution.py:234
  61.1 0.0 copy-done.4
  61.1 0.0 copy-done.7
  61.1 1.5 repack.3.t_ref
  62.6 0.0 copy-start.2
  62.6 1.0 copy-done.2
  63.6 7.0 %all-gather.4.cloned.1.call-done.w_ref = bf16[1536,768]{1,0:T(8,128)(2,1)} async-done(((bf16[96,768]{1,0:T(8,128)(2,1)}), bf16[1536,768]{1,0:T(8,128)(2,1)}) %all-gather.4.cloned.1.call-update) | async-done | bytes 2359312 | tf_op jit(solution)/shard_map/cond/branch_0_fun/all_gather | solution.py:232
  70.6 5.7 %product.3 = bf16[8,4,48,640]{3,2,1,0:T(8,128)(2,1)} custom-call(bf16[1536,768]{1,0:T(8,128)(2,1)} %all-gather.4.cloned.1.call-done.w_ref, bf16[768,640]{1,0:T(8,128)(2,1)} %copy-done.2), custom_call_target="tpu_custom_call" | custom-call | tf_op jit(solution)/shard_map/cond/branch_0_fun/product/pallas_call | solution.py:147
  76.3 0.0 reduce-scatter.4.cloned.1.call-update
  76.3 39.2 %reduce-scatter.4.cloned.1.call-done = bf16[192,640]{1,0:T(8,128)(2,1)} async-done(((bf16[1536,640]{1,0:T(8,128)(2,1)}), bf16[192,640]{1,0:T(8,128)(2,1)}) %reduce-scatter.4.cloned.1.call-update) | async-done | bytes 245776 | tf_op jit(solution)/shard_map/cond/branch_0_fun/reduce_scatter | solution.py:237
  115.6 9.4 %all_to_all.46.parts_ref = bf16[4,48,640]{2,1,0:T(8,128)(2,1)S(1)} all-to-all(bf16[4,48,640]{2,1,0:T(8,128)(2,1)} %bitcast.21), channel_id=1, replica_groups=mesh['y'=8,'core'=2,'x'=4,'z'=8] {'x'}, dimensions={0} | all-to-all | bytes 491520 | tf_op jit(solution)/shard_map/cond/branch_0_fun/all_to_all | solution.py:238
  125.0 1.3 send_out.3
  126.3 23.0 %all_to_all.47.got_ref = bf16[16,48,128]{2,1,0:T(8,128)(2,1)S(1)} all-to-all(bf16[16,48,128]{2,1,0:T(8,128)(2,1)S(1)} %send_out.3), channel_id=1, replica_groups=mesh['y'=8,'core'=2,'x'=4,'z'=8] {'y','core'}, dimensions={0} | all-to-all | bytes 393216 | tf_op jit(solution)/shard_map/cond/branch_0_fun/all_to_all | solution.py:239
  149.3 1.3 place.3
  150.6 0.0 copy-start.3
  150.7 0.7 copy-done.3
  (1 shorter events, 0.0 us)
Async XLA Ops:
  10.0 60.7 %all-gather.4.cloned.1.call-start = ((), (), s32[]{:S(2)}) async-start(), calls=%async_computation.12 | async-start | bytes 2506752 | tf_op jit(solution)/shard_map/cond/branch_0_fun/all_gather | solution.py:232
  10.7 104.9 %reduce-scatter.4.cloned.1.call-start = ((), (), s32[]{:S(2)}) async-start(), calls=%async_computation.13 | async-start | bytes 2211840 | tf_op jit(solution)/shard_map/cond/branch_0_fun/reduce_scatter | solution.py:237
  10.7 50.4 %copy-start.4 = (s32[8]{0:T(128)S(1)}, s32[8]{0:T(128)}, u32[]{:S(2)}) copy-start(s32[8]{0:T(128)} %get-tuple-element.47.virt) | copy-start | bytes 100 | tf_op jit(solution)/shard_map/cond
  10.8 50.3 %copy-start.7 = (s32[8]{0:T(128)S(1)}, s32[8]{0:T(128)}, u32[]{:S(2)}) copy-start(s32[8]{0:T(128)} %get-tuple-element.46.occ) | copy-start | bytes 100 | tf_op jit(solution)/shard_map/cond
  62.6 1.0 copy-start.2
  150.6 0.7 copy-start.3
Sparse Core Ops, SparseCore 0:
  12.9 57.6 all-gather.3
  76.5 39.0 reduce-scatter.3

commit v5 on v4

--- a/solution.py
+++ b/solution.py
@@ -13,7 +13,7 @@
 KO = 192
 ROWS = 16
 SIZES = (5, 6, 8)
-STEP = 6
+STEP = 12
 BLOCK = 48
 BF = jnp.bfloat16
 F32 = jnp.float32
@@ -77,11 +77,11 @@
 def deal(turns, amplitudes, occ_count, virt_count, target):
     return pl.pallas_call(
         deal_kernel,
-        in_specs=[scalars()] * 3 + [pl.BlockSpec(memory_space=pl.ANY)],
+        in_specs=[scalars()] * 3 + [pl.BlockSpec(memory_space=pltpu.HBM)],
         out_specs=pl.BlockSpec(memory_space=pltpu.VMEM),
         out_shape=jax.ShapeDtypeStruct((ROWS, 6, turns, 8, VCAP), BF),
         scratch_shapes=[pltpu.VMEM((6, KO, 8, VCAP), BF), pltpu.SemaphoreType.DMA((IRREPS,))],
-        compiler_params=pltpu.CompilerParams(vmem_limit_bytes=56 << 20),
+        compiler_params=pltpu.CompilerParams(vmem_limit_bytes=24 << 20),
         name="deal",
     )(occ_count, virt_count, target, amplitudes)
 
@@ -113,54 +113,43 @@
     )(where, occ_count, virt_count, target, landed)
 
 
-def product_kernel(w_ref, t_ref, out_ref, w_held, t_held, out_held, w_sem, t_sem, out_sem):
-    tall = w_ref.shape[0] // 4
-    t_copy = pltpu.make_async_copy(t_ref, t_held, t_sem)
-    t_copy.start()
-    w_copies = [
-        pltpu.make_async_copy(
-            w_ref.at[x * tall:(x + 1) * tall], w_held.at[x * tall:(x + 1) * tall], w_sem.at[x]
-        )
-        for x in range(4)
-    ]
-    for copy in w_copies:
-        copy.start()
-    t_copy.wait()
-    out_copies = []
-    for x in range(4):
-        w_copies[x].wait()
-        part = jnp.dot(
-            w_held[x * tall:(x + 1) * tall, :], t_held[...], preferred_element_type=F32
-        )
-        for z in range(8):
-            out_held[x, z] = part[z * BLOCK:(z + 1) * BLOCK].astype(BF)
-        copy = pltpu.make_async_copy(out_held.at[x], out_ref.at[:, x], out_sem.at[x])
-        copy.start()
-        out_copies.append(copy)
-    for copy in out_copies:
+def product_kernel(where, own_ref, other_ref, t_ref, out_ref, held, sem):
+    core = lax.rem(where[0], 2)
+    tall = 8 * BLOCK
+    copies = []
+    for part, (ref, of_core) in enumerate(((own_ref, core), (other_ref, 1 - core))):
+        for pair in range(2):
+            value = jnp.dot(
+                ref[pair * tall:(pair + 1) * tall, :], t_ref[...], preferred_element_type=F32
+            )
+            for n in range(4):
+                at = 4 * (2 * part + pair) + n
+                y = 4 * pair + n
+                for i in range(2):
+                    begin = (2 * n + i) * BLOCK
+                    held[at, i] = value[begin:begin + BLOCK].astype(BF)
+                copy = pltpu.make_async_copy(
+                    held.at[at], out_ref.at[pl.ds(4 * (y % 2) + 2 * of_core, 2), y // 2], sem.at[at]
+                )
+                copy.start()
+                copies.append(copy)
+    for copy in copies:
         copy.wait()
 
 
-def product(w_rows, t_rows):
-    rows, depth = w_rows.shape
+def product(own, other, t_rows, where):
+    rows, depth = own.shape
     width = t_rows.shape[1]
     out = pl.pallas_call(
         product_kernel,
-        in_specs=[pl.BlockSpec(memory_space=pl.ANY)] * 2,
-        out_specs=pl.BlockSpec(memory_space=pl.ANY),
+        in_specs=[scalars()] + [pl.BlockSpec(memory_space=pltpu.VMEM)] * 3,
+        out_specs=pl.BlockSpec(memory_space=pltpu.HBM),
         out_shape=jax.ShapeDtypeStruct((8, 4, BLOCK, width), BF),
-        scratch_shapes=[
-            pltpu.VMEM((rows, depth), BF),
-            pltpu.VMEM((depth, width), BF),
-            pltpu.VMEM((4, 8, BLOCK, width), BF),
-            pltpu.SemaphoreType.DMA((4,)),
-            pltpu.SemaphoreType.DMA,
-            pltpu.SemaphoreType.DMA((4,)),
-        ],
-        compiler_params=pltpu.CompilerParams(vmem_limit_bytes=56 << 20),
+        scratch_shapes=[pltpu.VMEM((16, 2, BLOCK, width), BF), pltpu.SemaphoreType.DMA((16,))],
+        compiler_params=pltpu.CompilerParams(vmem_limit_bytes=24 << 20),
         name="product",
-    )(w_rows, t_rows)
-    return out.reshape(rows, width)
+    )(where, own, other, t_rows)
+    return out.reshape(2 * rows, width)
 
 
 def send_kernel(where, occ, virt, target, parts_ref, out_ref, total):
@@ -221,7 +210,7 @@
         in_specs=[scalars()] * 4 + [pl.BlockSpec(memory_space=pltpu.VMEM)],
         out_specs=pl.BlockSpec(memory_space=pltpu.VMEM),
         out_shape=jax.ShapeDtypeStruct((BLOCK, 12 * VCAP), BF),
-        compiler_params=pltpu.CompilerParams(vmem_limit_bytes=32 << 20),
+        compiler_params=pltpu.CompilerParams(vmem_limit_bytes=24 << 20),
         name="place",
     )(where, occ_count, virt_count, target, got)
 
@@ -229,15 +218,16 @@
 def contract(turns, where, w_cycle, amplitudes, occ_count, virt_count, target):
     masks = (where, occ_count, virt_count, target)
     line = ("y", "core")
-    w_rows = lax.all_gather(w_cycle, line, axis=0, tiled=True)
+    own = lax.all_gather(w_cycle, "y", axis=0, tiled=True)
     dealt = deal(turns, amplitudes, occ_count, virt_count, target)
     landed = lax.all_to_all(dealt, line, 0, 0, tiled=True)
+    own, landed = lax.optimization_barrier((own, landed))
+    other = lax.ppermute(own, "core", [(0, 1), (1, 0)])
     t_rows = repack(landed.reshape(ROWS * 6, turns, 8, VCAP), *masks)
-    partial = product(w_rows, t_rows)
+    partial = product(own, other, t_rows, where)
     by_z = lax.psum_scatter(partial, "z", scatter_dimension=0, tiled=True)
     by_x = lax.all_to_all(by_z, "x", 0, 0, tiled=True).reshape(4, BLOCK, turns * VCAP)
-    got = lax.all_to_all(send_out(by_x, *masks), line, 0, 0, tiled=True)
-    return place(got, *masks)
+    return lax.all_to_all(send_out(by_x, *masks), line, 0, 0, tiled=True)
 
 
 def per_device(w_cycle, amplitudes, occ_count, virt_count, target):
@@ -248,11 +238,12 @@
     meets = jnp.bitwise_xor(irreps, target)[:, None] == irreps[None, :]
     pairs = jnp.sum(jnp.where(meets, occ_count[:, None] * virt_count[None, :], 0))
     case = sum((pairs > (ROWS * turns - 1) * VCAP).astype(jnp.int32) for turns in SIZES[:-1])
-    return lax.switch(
+    got = lax.switch(
         case,
         [functools.partial(contract, turns) for turns in SIZES],
         where, w_cycle, amplitudes, occ_count, virt_count, target,
     )
+    return place(got, where, occ_count, virt_count, target)
 
 
 def solution(mesh):

time: 159 us -> 170 us (1.069)
  blocking collectives: 77.1 us -> 32.8 us
  waiting for transfers between devices: 47 us -> 90.4 us
  starting transfers between devices: 0.08 us -> 16.5 us
  Pallas kernels: 15.4 us -> 12.9 us
    all_to_all x2 -> x1, blocking collectives: 67.7 us -> 23.2 us  [contract(): return lax.all_to_all(send_out(by_x, *masks), line, 0, 0, tiled=True)]
    all_gather x1, waiting for transfers between devices: 7.03 us -> 47 us  [contract(): own = lax.all_gather(w_cycle, 'y', axis=0, tiled=True)]
    all_to_all x0 -> x1, starting transfers between devices: none -> 10.4 us  [contract(): landed = lax.all_to_all(dealt, line, 0, 0, tiled=True)]
    ppermute x0 -> x1, starting transfers between devices: none -> 6.02 us  [contract(): other = lax.ppermute(own, 'core', [(0, 1), (1, 0)])]
    reduce_scatter x1, waiting for transfers between devices: 39.2 us -> 41.7 us  [contract(): by_z = lax.psum_scatter(partial, 'z', scatter_dimension=0, tiled=True)]
    pallas_call x1, Pallas kernels: 5.7 us -> 3.44 us  [product(): pl.pallas_call(product_kernel, in_specs=[scalars()] + [pl.BlockSpec(memor...]
  transfers between devices with their start and end apart: 2 -> 4, of which waited for: 2 -> 3; matrix products, arithmetic and copies ran while one was open for 0% -> 0% of each run, Pallas kernels for 5% -> 1%
where the time goes in v5:
time: 170 us; the launch traced here: 169 us
  waiting for transfers between devices  90.4 us (53%)
  blocking collectives  32.8 us (19%)
  starting transfers between devices  16.5 us (10%)
  between operations  15.3 us (9%)
  Pallas kernels  12.9 us (8%)
    all_gather x1, waiting for transfers between devices, contract(): own = lax.all_gather(w_cycle, 'y', axis=0, tiled=True)  47 us
    reduce_scatter x1, waiting for transfers between devices, contract(): by_z = lax.psum_scatter(partial, 'z', scatter_dimension=0, tiled=True)  41.7 us
    all_to_all x1, blocking collectives, contract(): return lax.all_to_all(send_out(by_x, *masks), line, 0, 0, tiled=True)  23.2 us
    all_to_all x1, starting transfers between devices, contract(): landed = lax.all_to_all(dealt, line, 0, 0, tiled=True)  10.4 us
    all_to_all x1, blocking collectives, contract(): lax.all_to_all(by_z, 'x', 0, 0, tiled=True).reshape(4, BLOCK, turns * VCAP)  9.59 us
    ppermute x1, starting transfers between devices, contract(): other = lax.ppermute(own, 'core', [(0, 1), (1, 0)])  6.02 us
    pallas_call x1, Pallas kernels, deal(): pl.pallas_call(deal_kernel, in_specs=[scalars()] * 3 + [pl.BlockSpec(memo...  5.04 us
    pallas_call x1, Pallas kernels, product(): pl.pallas_call(product_kernel, in_specs=[scalars()] + [pl.BlockSpec(memor...  3.44 us
  transfers between devices with their start and end apart: 4, of which 3 were waited for; matrix products, arithmetic and copies ran while one was open for 0% of the time, Pallas kernels for 1%

profile of v5, /device:TPU:1, one launch (start us, length us, event | category | flops | bytes accessed | tf_op | source)
XLA Modules:
  0.0 169.5 jit_solution(4185491338731963713)
XLA Ops:
  7.2 0.1 pad_add_fusion.where
  7.3 1.4 select_reduce_fusion
  9.9 151.2 %conditional.1 = (bf16[16,48,128]{2,1,0:T(8,128)(2,1)S(1)}) conditional(s32[]{:T(128)} %clamp.3, (bf16[96,768]{1,0:T(8,128)(2,1)}, s32[8]{0:T(128)}, s32[8]{0:T(128)}, s32[1]{0:T(128)}, bf16[6,192,8,128]{3,2,1,0:T(8,128)(2,1)}, /*index=5*/s32[2]{0:T(128)S(1)}) %tuple.17, (bf16[96,768]{1,0:T(8,128)(2,1)}, s32[8]{0:T(128)}, ...), branch_computations={%region_1.3_spmd, %region_3.5_spmd, %region_5.7_spmd} | conditional | bytes 29934068 | solution.py:241
  10.0 5.0 %deal.4 = bf16[16,6,6,8,128]{4,3,2,1,0:T(8,128)(2,1)} custom-call(s32[8]{0:T(128)} %get-tuple-element.54.occ, s32[8]{0:T(128)} %get-tuple-element.55.virt, s32[1]{0:T(128)} %get-tuple-element.56.target, bf16[6,192,8,128]{3,2,1,0:T(8,128)(2,1)} %get-tuple-element.58.t_ref), custom_call_target="tpu_custom_call" | custom-call | tf_op jit(solution)/shard_map/cond/branch_1_fun/deal/pallas_call | solution.py:78
  15.0 0.0 copy-start.4
  15.0 0.0 copy-start.7
  15.0 10.4 %all-to-all-start.3 = ((bf16[16,6,6,8,128]{4,3,2,1,0:T(8,128)(2,1)}), bf16[16,6,6,8,128]{4,3,2,1,0:T(8,128)(2,1)S(1)}, u32[]{:S(2)}, u32[]{:S(2)}) async-start(bf16[16,6,6,8,128]{4,3,2,1,0:T(8,128)(2,1)} %deal.4), calls=%async_computation.4 | async-start | bytes 2359296 | tf_op jit(solution)/shard_map/cond/branch_1_fun/all_to_all | solution.py:223
  25.4 0.0 all-gather.6.cloned.1.call-start
  25.5 0.7 all-gather.6.cloned.1.call-update
  26.2 0.0 reduce-scatter.6.cloned.1.call-start
  26.2 47.0 %all-gather.6.cloned.1.call-done.own_ref = bf16[768,768]{1,0:T(8,128)(2,1)} async-done(((bf16[96,768]{1,0:T(8,128)(2,1)}), bf16[768,768]{1,0:T(8,128)(2,1)}) %all-gather.6.cloned.1.call-update) | async-done | bytes 1179664 | tf_op jit(solution)/shard_map/cond/branch_1_fun/all_gather | solution.py:221
  73.2 0.0 all-to-all-done.3
  73.2 6.0 %collective-permute-start.1 = (bf16[768,768]{1,0:T(8,128)(2,1)}, bf16[768,768]{1,0:T(8,128)(2,1)S(1)}, u32[]{:S(2)}, u32[]{:S(2)}) collective-permute-start(bf16[768,768]{1,0:T(8,128)(2,1)} %all-gather.6.cloned.1.call-done.own_ref), channel_id=1, source_target_pairs={{0,32},{32,0},{1,33},{33,1},{2,34},{34,2},{3,35},{35,3},{4,36},{36... | collective-permute-start | bytes 3538952 | tf_op jit(solution)/shard_map/cond/branch_1_fun/ppermute | solution.py:225
  79.2 0.0 copy-done.4
  79.2 0.0 copy-done.7
  79.3 0.0 copy-start.1
  79.3 1.6 repack.4.t_ref
  80.9 1.0 collective-permute-done.1.other_ref
  81.9 0.0 copy-done.1
  81.9 3.4 %product.4 = bf16[8,4,48,768]{3,2,1,0:T(8,128)(2,1)} custom-call(s32[2]{0:T(128)S(1)} %get-tuple-element.53.where, bf16[768,768]{1,0:T(8,128)(2,1)S(1)} %copy-done.1, bf16[768,768]{1,0:T(8,128)(2,1)S(1)} %collective-permute-done.1.other_ref, bf16[768,768]{1,0:T(8,128)(2,1)S(1)} %repack.4.t_ref), custom_call_target="tpu_custom_call" | custom-call | tf_op jit(solution)/shard_map/cond/branch_1_fun/product/pallas_call | solution.py:143
  85.3 0.0 reduce-scatter.6.cloned.1.call-update
  85.4 41.7 %reduce-scatter.6.cloned.1.call-done = bf16[192,768]{1,0:T(8,128)(2,1)} async-done(((bf16[1536,768]{1,0:T(8,128)(2,1)}), bf16[192,768]{1,0:T(8,128)(2,1)}) %reduce-scatter.6.cloned.1.call-update) | async-done | bytes 294928 | tf_op jit(solution)/shard_map/cond/branch_1_fun/reduce_scatter | solution.py:228
  127.0 9.6 %all_to_all.48.parts_ref = bf16[4,48,768]{2,1,0:T(8,128)(2,1)S(1)} all-to-all(bf16[4,48,768]{2,1,0:T(8,128)(2,1)} %bitcast.17), channel_id=1, replica_groups=mesh['y'=8,'core'=2,'x'=4,'z'=8] {'x'}, dimensions={0} | all-to-all | bytes 589824 | tf_op jit(solution)/shard_map/cond/branch_1_fun/all_to_all | solution.py:229
  136.6 1.3 send_out.4
  137.9 23.2 %all_to_all.49 = bf16[16,48,128]{2,1,0:T(8,128)(2,1)S(1)} all-to-all(bf16[16,48,128]{2,1,0:T(8,128)(2,1)S(1)} %send_out.4), channel_id=1, replica_groups=mesh['y'=8,'core'=2,'x'=4,'z'=8] {'y','core'}, dimensions={0} | all-to-all | bytes 393216 | tf_op jit(solution)/shard_map/cond/branch_1_fun/all_to_all | solution.py:230
  161.1 1.5 place.1
  (1 shorter events, 0.0 us)
Async XLA Ops:
  15.0 64.2 %copy-start.4 = (s32[8]{0:T(128)S(1)}, s32[8]{0:T(128)}, u32[]{:S(2)}) copy-start(s32[8]{0:T(128)} %get-tuple-element.54.occ) | copy-start | bytes 100 | tf_op jit(solution)/shard_map/cond
  15.0 64.2 %copy-start.7 = (s32[8]{0:T(128)S(1)}, s32[8]{0:T(128)}, u32[]{:S(2)}) copy-start(s32[8]{0:T(128)} %get-tuple-element.55.virt) | copy-start | bytes 100 | tf_op jit(solution)/shard_map/cond
  15.0 58.2 %all-to-all-start.3 = ((bf16[16,6,6,8,128]{4,3,2,1,0:T(8,128)(2,1)}), bf16[16,6,6,8,128]{4,3,2,1,0:T(8,128)(2,1)S(1)}, u32[]{:S(2)}, u32[]{:S(2)}) async-start(bf16[16,6,6,8,128]{4,3,2,1,0:T(8,128)(2,1)} %deal.4), calls=%async_computation.4 | async-start | bytes 2359296 | tf_op jit(solution)/shard_map/cond/branch_1_fun/all_to_all | solution.py:223
  25.4 47.8 %all-gather.6.cloned.1.call-start = ((), (), s32[]{:S(2)}) async-start(), calls=%async_computation.14 | async-start | bytes 1327104 | tf_op jit(solution)/shard_map/cond/branch_1_fun/all_gather | solution.py:221
  26.2 100.9 %reduce-scatter.6.cloned.1.call-start = ((), (), s32[]{:S(2)}) async-start(), calls=%async_computation.15 | async-start | bytes 2654208 | tf_op jit(solution)/shard_map/cond/branch_1_fun/reduce_scatter | solution.py:228
  73.2 8.7 %collective-permute-start.1 = (bf16[768,768]{1,0:T(8,128)(2,1)}, bf16[768,768]{1,0:T(8,128)(2,1)S(1)}, u32[]{:S(2)}, u32[]{:S(2)}) collective-permute-start(bf16[768,768]{1,0:T(8,128)(2,1)} %all-gather.6.cloned.1.call-done.own_ref), channel_id=1, source_target_pairs={{0,32},{32,0},{1,33},{33,1},{2,34},{34,2},{3,35},{35,3},{4,36},{36... | collective-permute-start | bytes 3538952 | tf_op jit(solution)/shard_map/cond/branch_1_fun/ppermute | solution.py:225
  79.3 2.6 %copy-start.1 = (bf16[768,768]{1,0:T(8,128)(2,1)S(1)}, bf16[768,768]{1,0:T(8,128)(2,1)}, u32[]{:S(2)}) copy-start(bf16[768,768]{1,0:T(8,128)(2,1)} %all-gather.6.cloned.1.call-done.own_ref) | copy-start | bytes 3538948 | tf_op jit(solution)/shard_map/cond
Sparse Core Ops, SparseCore 0:
  28.5 44.6 all-gather.5
  85.5 41.4 reduce-scatter.5

commit v6 on v4

--- a/solution.py
+++ b/solution.py
@@ -13,7 +13,7 @@
 KO = 192
 ROWS = 16
 SIZES = (5, 6, 8)
-STEP = 6
+STEP = 12
 BLOCK = 48
 BF = jnp.bfloat16
 F32 = jnp.float32
@@ -102,12 +102,11 @@
 
 
 def repack(landed, where, occ_count, virt_count, target):
-    turns = landed.shape[1]
     return pl.pallas_call(
         repack_kernel,
         in_specs=[scalars()] * 4 + [pl.BlockSpec(memory_space=pltpu.VMEM)],
         out_specs=pl.BlockSpec(memory_space=pltpu.VMEM),
-        out_shape=jax.ShapeDtypeStruct((6 * VCAP, turns * VCAP), BF),
+        out_shape=jax.ShapeDtypeStruct((6 * VCAP, SIZES[-1] * VCAP), BF),
         compiler_params=pltpu.CompilerParams(vmem_limit_bytes=24 << 20),
         name="repack",
     )(where, occ_count, virt_count, target, landed)
@@ -115,20 +114,22 @@
 
 def product_kernel(w_ref, t_ref, out_ref, w_held, t_held, out_held, w_sem, t_sem, out_sem):
     tall = w_ref.shape[0] // 4
-    t_copy = pltpu.make_async_copy(t_ref, t_held, t_sem)
-    t_copy.start()
+    width = t_held.shape[1]
+    t_copy = pltpu.make_async_copy(t_ref.at[:, :width], t_held, t_sem)
     w_copies = [
         pltpu.make_async_copy(
             w_ref.at[x * tall:(x + 1) * tall], w_held.at[x * tall:(x + 1) * tall], w_sem.at[x]
         )
         for x in range(4)
     ]
-    for copy in w_copies:
-        copy.start()
+    t_copy.start()
+    w_copies[0].start()
     t_copy.wait()
     out_copies = []
     for x in range(4):
         w_copies[x].wait()
+        if x < 3:
+            w_copies[x + 1].start()
         part = jnp.dot(
             w_held[x * tall:(x + 1) * tall, :], t_held[...], preferred_element_type=F32
         )
@@ -141,9 +142,9 @@
         copy.wait()
 
 
-def product(w_rows, t_rows):
+def product(turns, w_rows, t_rows):
     rows, depth = w_rows.shape
-    width = t_rows.shape[1]
+    width = turns * VCAP
     out = pl.pallas_call(
         product_kernel,
         in_specs=[pl.BlockSpec(memory_space=pl.ANY)] * 2,
@@ -221,23 +222,24 @@
         in_specs=[scalars()] * 4 + [pl.BlockSpec(memory_space=pltpu.VMEM)],
         out_specs=pl.BlockSpec(memory_space=pltpu.VMEM),
         out_shape=jax.ShapeDtypeStruct((BLOCK, 12 * VCAP), BF),
-        compiler_params=pltpu.CompilerParams(vmem_limit_bytes=32 << 20),
+        compiler_params=pltpu.CompilerParams(vmem_limit_bytes=24 << 20),
         name="place",
     )(where, occ_count, virt_count, target, got)
 
 
-def contract(turns, where, w_cycle, amplitudes, occ_count, virt_count, target):
-    masks = (where, occ_count, virt_count, target)
-    line = ("y", "core")
-    w_rows = lax.all_gather(w_cycle, line, axis=0, tiled=True)
+def bring(turns, where, amplitudes, occ_count, virt_count, target):
     dealt = deal(turns, amplitudes, occ_count, virt_count, target)
-    landed = lax.all_to_all(dealt, line, 0, 0, tiled=True)
-    t_rows = repack(landed.reshape(ROWS * 6, turns, 8, VCAP), *masks)
-    partial = product(w_rows, t_rows)
+    landed = lax.all_to_all(dealt, ("y", "core"), 0, 0, tiled=True)
+    landed = landed.reshape(ROWS * 6, turns, 8, VCAP)
+    return repack(landed, where, occ_count, virt_count, target)
+
+
+def contract(turns, w_rows, t_rows, where, occ_count, virt_count, target):
+    partial = product(turns, w_rows, t_rows)
     by_z = lax.psum_scatter(partial, "z", scatter_dimension=0, tiled=True)
     by_x = lax.all_to_all(by_z, "x", 0, 0, tiled=True).reshape(4, BLOCK, turns * VCAP)
-    got = lax.all_to_all(send_out(by_x, *masks), line, 0, 0, tiled=True)
-    return place(got, *masks)
+    out = send_out(by_x, where, occ_count, virt_count, target)
+    return lax.all_to_all(out, ("y", "core"), 0, 0, tiled=True)
 
 
 def per_device(w_cycle, amplitudes, occ_count, virt_count, target):
@@ -248,11 +250,16 @@
     meets = jnp.bitwise_xor(irreps, target)[:, None] == irreps[None, :]
     pairs = jnp.sum(jnp.where(meets, occ_count[:, None] * virt_count[None, :], 0))
     case = sum((pairs > (ROWS * turns - 1) * VCAP).astype(jnp.int32) for turns in SIZES[:-1])
-    return lax.switch(
-        case,
-        [functools.partial(contract, turns) for turns in SIZES],
-        where, w_cycle, amplitudes, occ_count, virt_count, target,
+    counts = (occ_count, virt_count, target)
+    w_rows = lax.all_gather(w_cycle, ("y", "core"), axis=0, tiled=True)
+    t_rows = lax.switch(
+        case, [functools.partial(bring, turns) for turns in SIZES], where, amplitudes, *counts
     )
+    got = lax.switch(
+        case, [functools.partial(contract, turns) for turns in SIZES],
+        w_rows, t_rows, where, *counts,
+    )
+    return place(got, where, occ_count, virt_count, target)
 
 
 def solution(mesh):

time: 159 us -> 157 us (0.987)
  local copies, waits for them, and re-layouts: 1.63 us -> 0.03 us
    all_gather x1, waiting for transfers between devices: 7.03 us -> 5.12 us  [per_device(): w_rows = lax.all_gather(w_cycle, ('y', 'core'), axis=0, tiled=True)]
  transfers between devices with their start and end apart: 2 -> 2, of which waited for: 2 -> 2; matrix products, arithmetic and copies ran while one was open for 0% -> 1% of each run, Pallas kernels for 5% -> 4%
where the time goes in v6:
time: 157 us
  blocking collectives  77.8 us (50%)
  waiting for transfers between devices  46.6 us (30%)
  between operations  15.4 us (10%)
  Pallas kernels  15.3 us (10%)
    all_to_all x1, blocking collectives, bring(): landed = lax.all_to_all(dealt, ('y', 'core'), 0, 0, tiled=True)  45.2 us
    reduce_scatter x1, waiting for transfers between devices, contract(): by_z = lax.psum_scatter(partial, 'z', scatter_dimension=0, tiled=True)  40.7 us
    all_to_all x1, blocking collectives, contract(): return lax.all_to_all(out, ('y', 'core'), 0, 0, tiled=True)  23.1 us
    all_to_all x1, blocking collectives, contract(): lax.all_to_all(by_z, 'x', 0, 0, tiled=True).reshape(4, BLOCK, turns * VCAP)  9.5 us
    pallas_call x1, Pallas kernels, product(): pl.pallas_call(product_kernel, in_specs=[pl.BlockSpec(memory_space=pl.ANY...  6.05 us
    all_gather x1, waiting for transfers between devices, per_device(): w_rows = lax.all_gather(w_cycle, ('y', 'core'), axis=0, tiled=True)  5.12 us
    pallas_call x1, Pallas kernels, deal(): pl.pallas_call(deal_kernel, in_specs=[scalars()] * 3 + [pl.BlockSpec(memo...  4.98 us
  transfers between devices with their start and end apart: 2, of which 2 were waited for; matrix products, arithmetic and copies ran while one was open for 1% of the time, Pallas kernels for 4%

profile of v6, /device:TPU:1, one launch (start us, length us, event | category | flops | bytes accessed | tf_op | source)
XLA Modules:
  0.0 156.6 jit_solution(14023290946661140651)
XLA Ops:
  6.5 0.0 all-gather.2.cloned.1.call-start
  6.5 0.7 all-gather.2.cloned.1.call-update
  7.9 1.4 select_reduce_fusion
  10.6 0.1 pad_add_fusion.where
  10.7 51.8 %conditional.2 = (bf16[768,1024]{1,0:T(8,128)(2,1)S(1)}) conditional(s32[]{:T(128)} %clamp.4, (s32[8]{0:T(128)}, s32[8]{0:T(128)}, s32[1]{0:T(128)}, bf16[6,192,8,128]{3,2,1,0:T(8,128)(2,1)}, s32[2]{0:T(128)S(1)}) %tuple.23, (s32[8]{0:T(128)}, s32[8]{0:T(128)}, s32[1]{0:T(128)}, bf16[6,192,8,128]{3,2,1,0:T(8,128)(2,1)}, ...), branch_computations={%region_1.2_spmd, %region_2.3_spmd, %region_3.4_spmd} | conditional | bytes 3146048 | solution.py:255
  10.7 5.0 %deal.3 = bf16[16,6,5,8,128]{4,3,2,1,0:T(8,128)(2,1)} custom-call(s32[8]{0:T(128)} %get-tuple-element.78.occ, s32[8]{0:T(128)} %get-tuple-element.80.virt, s32[1]{0:T(128)} %get-tuple-element.82.target, bf16[6,192,8,128]{3,2,1,0:T(8,128)(2,1)} %get-tuple-element.83.t_ref), custom_call_target="tpu_custom_call" | custom-call | tf_op jit(solution)/shard_map/cond/branch_0_fun/deal/pallas_call | solution.py:78
  15.7 0.0 copy-start
  15.7 0.0 copy-start.6
  15.7 45.2 %all_to_all.45 = bf16[16,6,5,8,128]{4,3,2,1,0:T(8,128)(2,1)S(1)} all-to-all(bf16[16,6,5,8,128]{4,3,2,1,0:T(8,128)(2,1)} %deal.3), channel_id=1, replica_groups=mesh['y'=8,'core'=2,'x'=4,'z'=8] {'y','core'}, dimensions={0} | all-to-all | bytes 1966080 | tf_op jit(solution)/shard_map/cond/branch_0_fun/all_to_all | solution.py:232
  60.9 0.0 copy-done
  60.9 0.0 copy-done.6
  60.9 1.5 repack.3
  62.5 5.1 %all-gather.2.cloned.1.call-done = bf16[1536,768]{1,0:T(8,128)(2,1)} async-done(((bf16[96,768]{1,0:T(8,128)(2,1)}), bf16[1536,768]{1,0:T(8,128)(2,1)}) %all-gather.2.cloned.1.call-update) | async-done | bytes 2359312 | tf_op jit(solution)/shard_map/all_gather | solution.py:254
  67.6 80.7 %conditional.3 = (bf16[16,48,128]{2,1,0:T(8,128)(2,1)S(1)}) conditional(s32[]{:T(128)} %clamp.4, (bf16[1536,768]{1,0:T(8,128)(2,1)}, bf16[768,1024]{1,0:T(8,128)(2,1)S(1)}, s32[2]{0:T(128)S(1)}, s32[8]{0:T(128)}, s32[8]{0:T(128)}, /*index=5*/s32[1]{0:T(128)}) %tuple.24, (bf16[1536,768]{1,0:T(8,128)(2,1)}, ...), branch_computations={%region_4.6_spmd, %region_6.8_spmd, %region_8.10_spmd} | conditional | bytes 11796840 | solution.py:258
  67.6 0.0 reduce-scatter.4.cloned.1.call-start
  67.6 6.0 %product.3 = bf16[8,4,48,640]{3,2,1,0:T(8,128)(2,1)} custom-call(bf16[1536,768]{1,0:T(8,128)(2,1)} %get-tuple-element.98.w_ref, bf16[768,1024]{1,0:T(8,128)(2,1)S(1)} %get-tuple-element.99.t_ref), custom_call_target="tpu_custom_call" | custom-call | tf_op jit(solution)/shard_map/cond/branch_0_fun/product/pallas_call | solution.py:148
  73.7 0.0 copy-start.3
  73.7 0.0 copy-start.9
  73.7 0.0 reduce-scatter.4.cloned.1.call-update
  73.7 40.7 %reduce-scatter.4.cloned.1.call-done = bf16[192,640]{1,0:T(8,128)(2,1)} async-done(((bf16[1536,640]{1,0:T(8,128)(2,1)}), bf16[192,640]{1,0:T(8,128)(2,1)}) %reduce-scatter.4.cloned.1.call-update) | async-done | bytes 245776 | tf_op jit(solution)/shard_map/cond/branch_0_fun/reduce_scatter | solution.py:239
  114.4 9.5 %all_to_all.48.parts_ref = bf16[4,48,640]{2,1,0:T(8,128)(2,1)S(1)} all-to-all(bf16[4,48,640]{2,1,0:T(8,128)(2,1)} %bitcast.21), channel_id=1, replica_groups=mesh['y'=8,'core'=2,'x'=4,'z'=8] {'x'}, dimensions={0} | all-to-all | bytes 491520 | tf_op jit(solution)/shard_map/cond/branch_0_fun/all_to_all | solution.py:240
  123.9 0.0 copy-done.3
  123.9 0.0 copy-done.9
  123.9 1.3 send_out.3
  125.2 23.1 %all_to_all.49 = bf16[16,48,128]{2,1,0:T(8,128)(2,1)S(1)} all-to-all(bf16[16,48,128]{2,1,0:T(8,128)(2,1)S(1)} %send_out.3), channel_id=1, replica_groups=mesh['y'=8,'core'=2,'x'=4,'z'=8] {'y','core'}, dimensions={0} | all-to-all | bytes 393216 | tf_op jit(solution)/shard_map/cond/branch_0_fun/all_to_all | solution.py:242
  148.3 1.5 place.1
  (1 shorter events, 0.0 us)
Async XLA Ops:
  6.5 61.1 %all-gather.2.cloned.1.call-start = ((), (), s32[]{:S(2)}) async-start(), calls=%async_computation.15 | async-start | bytes 2506752 | tf_op jit(solution)/shard_map/all_gather | solution.py:254
  15.7 45.2 %copy-start = (s32[8]{0:T(128)S(1)}, s32[8]{0:T(128)}, u32[]{:S(2)}) copy-start(s32[8]{0:T(128)} %get-tuple-element.78.occ) | copy-start | bytes 100 | tf_op jit(solution)/shard_map/cond
  15.7 45.2 %copy-start.6 = (s32[8]{0:T(128)S(1)}, s32[8]{0:T(128)}, u32[]{:S(2)}) copy-start(s32[8]{0:T(128)} %get-tuple-element.80.virt) | copy-start | bytes 100 | tf_op jit(solution)/shard_map/cond
  67.6 46.8 %reduce-scatter.4.cloned.1.call-start = ((), (), s32[]{:S(2)}) async-start(), calls=%async_computation.12 | async-start | bytes 2211840 | tf_op jit(solution)/shard_map/cond/branch_0_fun/reduce_scatter | solution.py:239
  73.7 50.3 %copy-start.3 = (s32[8]{0:T(128)S(1)}, s32[8]{0:T(128)}, u32[]{:S(2)}) copy-start(s32[8]{0:T(128)} %get-tuple-element.95.occ) | copy-start | bytes 100 | tf_op jit(solution)/shard_map/cond
  73.7 50.3 %copy-start.9 = (s32[8]{0:T(128)S(1)}, s32[8]{0:T(128)}, u32[]{:S(2)}) copy-start(s32[8]{0:T(128)} %get-tuple-element.96.virt) | copy-start | bytes 100 | tf_op jit(solution)/shard_map/cond
Sparse Core Ops, SparseCore 0:
  9.7 57.8 all-gather.1
  73.8 40.5 reduce-scatter.3

commit v7 on v4

--- a/solution.py
+++ b/solution.py
@@ -13,7 +13,7 @@
 KO = 192
 ROWS = 16
 SIZES = (5, 6, 8)
-STEP = 6
+STEP = 12
 BLOCK = 48
 BF = jnp.bfloat16
 F32 = jnp.float32
@@ -34,7 +34,12 @@
     return total
 
 
-def deal_kernel(occ, virt, target, t_ref, out_ref, held, sem):
+def size_class(pairs):
+    return sum((pairs > (ROWS * turns - 1) * VCAP).astype(jnp.int32) for turns in SIZES[:-1])
+
+
+def deal_kernel(occ, virt, target, t_ref, *rest):
+    results, (held, packed, sem, out_sem) = rest[:len(SIZES)], rest[len(SIZES):]
     copies = [
         pltpu.make_async_copy(
             t_ref.at[:, h * OCAP:(h + 1) * OCAP], held.at[:, h * OCAP:(h + 1) * OCAP], sem.at[h]
@@ -46,7 +51,7 @@
     lane = lax.broadcasted_iota(jnp.int32, (48, VCAP), 1)
 
     def put(p, value):
-        out_ref[jnp.bitwise_and(p, 15), :, lax.shift_right_logical(p, 4)] = (
+        packed[jnp.bitwise_and(p, 15), :, lax.shift_right_logical(p, 4)] = (
             value.astype(BF).reshape(6, 8, VCAP)
         )
 
@@ -72,15 +77,27 @@
         current = lax.fori_loop(0, (many + STEP - 1) // STEP, some, current)
         first = first + many * wide
     put(lax.shift_right_logical(first, 7), current)
-
-
-def deal(turns, amplitudes, occ_count, virt_count, target):
+    which = size_class(first)
+    for n, turns in enumerate(SIZES):
+        @pl.when(which == n)
+        def _(n=n, turns=turns):
+            copy = pltpu.make_async_copy(packed.at[:, :, :turns], results[n], out_sem)
+            copy.start()
+            copy.wait()
+
+
+def deal(amplitudes, occ_count, virt_count, target):
     return pl.pallas_call(
         deal_kernel,
         in_specs=[scalars()] * 3 + [pl.BlockSpec(memory_space=pl.ANY)],
-        out_specs=pl.BlockSpec(memory_space=pltpu.VMEM),
-        out_shape=jax.ShapeDtypeStruct((ROWS, 6, turns, 8, VCAP), BF),
-        scratch_shapes=[pltpu.VMEM((6, KO, 8, VCAP), BF), pltpu.SemaphoreType.DMA((IRREPS,))],
+        out_specs=[pl.BlockSpec(memory_space=pl.ANY)] * len(SIZES),
+        out_shape=[jax.ShapeDtypeStruct((ROWS, 6, turns, 8, VCAP), BF) for turns in SIZES],
+        scratch_shapes=[
+            pltpu.VMEM((6, KO, 8, VCAP), BF),
+            pltpu.VMEM((ROWS, 6, SIZES[-1], 8, VCAP), BF),
+            pltpu.SemaphoreType.DMA((IRREPS,)),
+            pltpu.SemaphoreType.DMA,
+        ],
         compiler_params=pltpu.CompilerParams(vmem_limit_bytes=56 << 20),
         name="deal",
     )(occ_count, virt_count, target, amplitudes)
@@ -113,51 +130,33 @@
     )(where, occ_count, virt_count, target, landed)
 
 
-def product_kernel(w_ref, t_ref, out_ref, w_held, t_held, out_held, w_sem, t_sem, out_sem):
-    tall = w_ref.shape[0] // 4
-    t_copy = pltpu.make_async_copy(t_ref, t_held, t_sem)
-    t_copy.start()
-    w_copies = [
-        pltpu.make_async_copy(
-            w_ref.at[x * tall:(x + 1) * tall], w_held.at[x * tall:(x + 1) * tall], w_sem.at[x]
+def product_kernel(w_ref, t_ref, out_ref, held, sem):
+    tall = 4 * BLOCK
+    copies = []
+    for n in range(8):
+        value = jnp.dot(
+            w_ref[n * tall:(n + 1) * tall, :], t_ref[...], preferred_element_type=F32
         )
-        for x in range(4)
-    ]
-    for copy in w_copies:
+        for z in range(4):
+            held[n, z] = value[z * BLOCK:(z + 1) * BLOCK].astype(BF)
+        begin = 4 * (n % 2)
+        copy = pltpu.make_async_copy(held.at[n], out_ref.at[begin:begin + 4, n // 2], sem.at[n])
         copy.start()
-    t_copy.wait()
-    out_copies = []
-    for x in range(4):
-        w_copies[x].wait()
-        part = jnp.dot(
-            w_held[x * tall:(x + 1) * tall, :], t_held[...], preferred_element_type=F32
-        )
-        for z in range(8):
-            out_held[x, z] = part[z * BLOCK:(z + 1) * BLOCK].astype(BF)
-        copy = pltpu.make_async_copy(out_held.at[x], out_ref.at[:, x], out_sem.at[x])
-        copy.start()
-        out_copies.append(copy)
-    for copy in out_copies:
+        copies.append(copy)
+    for copy in copies:
         copy.wait()
 
 
 def product(w_rows, t_rows):
-    rows, depth = w_rows.shape
+    rows = w_rows.shape[0]
     width = t_rows.shape[1]
     out = pl.pallas_call(
         product_kernel,
-        in_specs=[pl.BlockSpec(memory_space=pl.ANY)] * 2,
+        in_specs=[pl.BlockSpec(memory_space=pltpu.VMEM)] * 2,
         out_specs=pl.BlockSpec(memory_space=pl.ANY),
         out_shape=jax.ShapeDtypeStruct((8, 4, BLOCK, width), BF),
-        scratch_shapes=[
-            pltpu.VMEM((rows, depth), BF),
-            pltpu.VMEM((depth, width), BF),
-            pltpu.VMEM((4, 8, BLOCK, width), BF),
-            pltpu.SemaphoreType.DMA((4,)),
-            pltpu.SemaphoreType.DMA,
-            pltpu.SemaphoreType.DMA((4,)),
-        ],
-        compiler_params=pltpu.CompilerParams(vmem_limit_bytes=56 << 20),
+        scratch_shapes=[pltpu.VMEM((8, 4, BLOCK, width), BF), pltpu.SemaphoreType.DMA((8,))],
+        compiler_params=pltpu.CompilerParams(vmem_limit_bytes=24 << 20),
         name="product",
     )(w_rows, t_rows)
     return out.reshape(rows, width)
@@ -226,33 +225,31 @@
     )(where, occ_count, virt_count, target, got)
 
 
-def contract(turns, where, w_cycle, amplitudes, occ_count, virt_count, target):
-    masks = (where, occ_count, virt_count, target)
+def contract(turns, w_cycle, dealt, *masks):
     line = ("y", "core")
     w_rows = lax.all_gather(w_cycle, line, axis=0, tiled=True)
-    dealt = deal(turns, amplitudes, occ_count, virt_count, target)
-    landed = lax.all_to_all(dealt, line, 0, 0, tiled=True)
+    landed = lax.all_to_all(dealt[SIZES.index(turns)], line, 0, 0, tiled=True)
     t_rows = repack(landed.reshape(ROWS * 6, turns, 8, VCAP), *masks)
     partial = product(w_rows, t_rows)
     by_z = lax.psum_scatter(partial, "z", scatter_dimension=0, tiled=True)
     by_x = lax.all_to_all(by_z, "x", 0, 0, tiled=True).reshape(4, BLOCK, turns * VCAP)
-    got = lax.all_to_all(send_out(by_x, *masks), line, 0, 0, tiled=True)
-    return place(got, *masks)
+    return lax.all_to_all(send_out(by_x, *masks), line, 0, 0, tiled=True)
 
 
 def per_device(w_cycle, amplitudes, occ_count, virt_count, target):
     row = lax.axis_index("y") * 2 + lax.axis_index("core")
     col = lax.axis_index("x") * 8 + lax.axis_index("z")
-    where = jnp.stack([row, col]).astype(jnp.int32)
+    masks = (jnp.stack([row, col]).astype(jnp.int32), occ_count, virt_count, target)
     irreps = jnp.arange(IRREPS, dtype=jnp.int32)
     meets = jnp.bitwise_xor(irreps, target)[:, None] == irreps[None, :]
     pairs = jnp.sum(jnp.where(meets, occ_count[:, None] * virt_count[None, :], 0))
-    case = sum((pairs > (ROWS * turns - 1) * VCAP).astype(jnp.int32) for turns in SIZES[:-1])
-    return lax.switch(
-        case,
+    dealt = deal(amplitudes, occ_count, virt_count, target)
+    got = lax.switch(
+        size_class(pairs),
         [functools.partial(contract, turns) for turns in SIZES],
-        where, w_cycle, amplitudes, occ_count, virt_count, target,
+        w_cycle, dealt, *masks,
     )
+    return place(got, *masks)
 
 
 def solution(mesh):

time: 159 us -> 161 us (1.013)
  Pallas kernels: 15.4 us -> 10.6 us
  waiting for transfers between devices: 47 us -> 51.7 us
  blocking collectives: 77.1 us -> 79.8 us
    pallas_call x1, Pallas kernels: 5.7 us -> 2.85 us  [product(): pl.pallas_call(product_kernel, in_specs=[pl.BlockSpec(memory_space=pltpu....]
    reduce_scatter x1, waiting for transfers between devices: 39.2 us -> 41.7 us  [contract(): by_z = lax.psum_scatter(partial, 'z', scatter_dimension=0, tiled=True)]
    all_to_all x2, blocking collectives: 67.7 us -> 70.1 us  [the longest x1 46.9 us: contract(): landed = lax.all_to_all(dealt[SIZES.index(turns)], line, 0, 0, tiled=True)]
    all_gather x1, waiting for transfers between devices: 7.03 us -> 9.35 us  [contract(): w_rows = lax.all_gather(w_cycle, line, axis=0, tiled=True)]
    pallas_call x1, Pallas kernels: 5.65 us -> 3.6 us  [deal(): pl.pallas_call(deal_kernel, in_specs=[scalars()] * 3 + [pl.BlockSpec(memo...]
  transfers between devices with their start and end apart: 2 -> 2, of which waited for: 2 -> 2; matrix products, arithmetic and copies ran while one was open for 0% -> 0% of each run, Pallas kernels for 5% -> 1%
where the time goes in v7:
time: 161 us
  blocking collectives  79.8 us (50%)
  waiting for transfers between devices  51.7 us (32%)
  between operations  15.4 us (10%)
  Pallas kernels  10.6 us (7%)
  local copies, waits for them, and re-layouts  1.67 us (1%)
    all_to_all x1, blocking collectives, contract(): landed = lax.all_to_all(dealt[SIZES.index(turns)], line, 0, 0, tiled=True)  46.9 us
    reduce_scatter x1, waiting for transfers between devices, contract(): by_z = lax.psum_scatter(partial, 'z', scatter_dimension=0, tiled=True)  41.7 us
    all_to_all x1, blocking collectives, contract(): return lax.all_to_all(send_out(by_x, *masks), line, 0, 0, tiled=True)  23.2 us
    all_to_all x1, blocking collectives, contract(): lax.all_to_all(by_z, 'x', 0, 0, tiled=True).reshape(4, BLOCK, turns * VCAP)  9.65 us
    all_gather x1, waiting for transfers between devices, contract(): w_rows = lax.all_gather(w_cycle, line, axis=0, tiled=True)  9.35 us
    pallas_call x1, Pallas kernels, deal(): pl.pallas_call(deal_kernel, in_specs=[scalars()] * 3 + [pl.BlockSpec(memo...  3.6 us
  transfers between devices with their start and end apart: 2, of which 2 were waited for; matrix products, arithmetic and copies ran while one was open for 0% of the time, Pallas kernels for 1%

profile of v7, /device:TPU:1, one launch (start us, length us, event | category | flops | bytes accessed | tf_op | source)
XLA Modules:
  0.0 160.8 jit_solution(10946194057878955535)
XLA Ops:
  6.5 0.0 copy-start.4
  6.5 0.0 copy-start.3
  7.2 0.1 pad_add_fusion.where
  7.3 1.4 select_reduce_fusion
  10.0 3.6 %deal.1 = (bf16[16,6,5,8,128]{4,3,2,1,0:T(8,128)(2,1)}, bf16[16,6,6,8,128]{4,3,2,1,0:T(8,128)(2,1)S(1)}, bf16[16,6,8,8,128]{4,3,2,1,0:T(8,128)(2,1)S(1)}) custom-call(s32[8]{0:T(128)} %occ.3, s32[8]{0:T(128)} %virt.3, s32[1]{0:T(128)} %copy.9.target, bf16[6,192,8,128]{3,2,1,0:T(8,128)(2,1)} %t_ref.1), custom_call_target="tpu_custom_call" | custom-call | tf_op jit(solution)/shard_map/deal/pallas_call | solution.py:90
  13.6 0.0 copy-done.4
  13.6 0.0 copy-done.3
  13.6 139.0 %conditional.1 = (bf16[16,48,128]{2,1,0:T(8,128)(2,1)S(1)}) conditional(s32[]{:T(128)} %clamp.3, (bf16[96,768]{1,0:T(8,128)(2,1)}, bf16[16,6,5,8,128]{4,3,2,1,0:T(8,128)(2,1)}, s32[2]{0:T(128)S(1)}, s32[8]{0:T(128)S(1)}, s32[8]{0:T(128)S(1)}, /*index=5*/s32[1]{0:T(128)}) %tuple.35, (bf16[96,768]{1,0:T(8,128)(2,1)}, ...), branch_computations={%region_1.3_spmd, %region_3.5_spmd, %region_5.7_spmd} | conditional | bytes 31899764 | solution.py:247
  13.6 0.0 all-gather.6.cloned.1.call-start
  13.7 0.7 all-gather.6.cloned.1.call-update
  14.4 0.0 reduce-scatter.6.cloned.1.call-start
  14.4 46.9 %all_to_all.48 = bf16[16,6,6,8,128]{4,3,2,1,0:T(8,128)(2,1)S(1)} all-to-all(bf16[16,6,6,8,128]{4,3,2,1,0:T(8,128)(2,1)S(1)} %get-tuple-element.56), channel_id=1, replica_groups=mesh['y'=8,'core'=2,'x'=4,'z'=8] {'y','core'}, dimensions={0} | all-to-all | bytes 2359296 | tf_op jit(solution)/shard_map/cond/branch_1_fun/all_to_all | solution.py:231
  61.3 1.6 repack.4.t_ref
  62.9 9.3 %all-gather.6.cloned.1.call-done.w_ref = bf16[1536,768]{1,0:T(8,128)(2,1)} async-done(((bf16[96,768]{1,0:T(8,128)(2,1)}), bf16[1536,768]{1,0:T(8,128)(2,1)}) %all-gather.6.cloned.1.call-update) | async-done | bytes 2359312 | tf_op jit(solution)/shard_map/cond/branch_1_fun/all_gather | solution.py:230
  72.2 0.0 copy-start.2
  72.2 1.7 %copy-done.2 = bf16[1536,768]{1,0:T(8,128)(2,1)S(1)} copy-done((bf16[1536,768]{1,0:T(8,128)(2,1)S(1)}, bf16[1536,768]{1,0:T(8,128)(2,1)}, u32[]{:S(2)}) %copy-start.2) | copy-done | bytes 2359320 | tf_op jit(solution)/shard_map/cond
  73.9 2.9 %product.4 = bf16[8,4,48,768]{3,2,1,0:T(8,128)(2,1)} custom-call(bf16[1536,768]{1,0:T(8,128)(2,1)S(1)} %copy-done.2, bf16[768,768]{1,0:T(8,128)(2,1)S(1)} %repack.4.t_ref), custom_call_target="tpu_custom_call" | custom-call | tf_op jit(solution)/shard_map/cond/branch_1_fun/product/pallas_call | solution.py:153
  76.7 0.0 reduce-scatter.6.cloned.1.call-update
  76.8 41.7 %reduce-scatter.6.cloned.1.call-done = bf16[192,768]{1,0:T(8,128)(2,1)} async-done(((bf16[1536,768]{1,0:T(8,128)(2,1)}), bf16[192,768]{1,0:T(8,128)(2,1)}) %reduce-scatter.6.cloned.1.call-update) | async-done | bytes 294928 | tf_op jit(solution)/shard_map/cond/branch_1_fun/reduce_scatter | solution.py:234
  118.4 9.6 %all_to_all.49.parts_ref = bf16[4,48,768]{2,1,0:T(8,128)(2,1)S(1)} all-to-all(bf16[4,48,768]{2,1,0:T(8,128)(2,1)} %bitcast.17), channel_id=1, replica_groups=mesh['y'=8,'core'=2,'x'=4,'z'=8] {'x'}, dimensions={0} | all-to-all | bytes 589824 | tf_op jit(solution)/shard_map/cond/branch_1_fun/all_to_all | solution.py:235
  128.1 1.3 send_out.4
  129.4 23.2 %all_to_all.50 = bf16[16,48,128]{2,1,0:T(8,128)(2,1)S(1)} all-to-all(bf16[16,48,128]{2,1,0:T(8,128)(2,1)S(1)} %send_out.4), channel_id=1, replica_groups=mesh['y'=8,'core'=2,'x'=4,'z'=8] {'y','core'}, dimensions={0} | all-to-all | bytes 393216 | tf_op jit(solution)/shard_map/cond/branch_1_fun/all_to_all | solution.py:236
  152.6 1.4 place.1
  (1 shorter events, 0.0 us)
Async XLA Ops:
  6.5 7.1 %copy-start.4 = (s32[8]{0:T(128)S(1)}, s32[8]{0:T(128)}, u32[]{:S(2)}) copy-start(s32[8]{0:T(128)} %virt.3) | copy-start | bytes 100
  6.5 7.1 %copy-start.3 = (s32[8]{0:T(128)S(1)}, s32[8]{0:T(128)}, u32[]{:S(2)}) copy-start(s32[8]{0:T(128)} %occ.3) | copy-start | bytes 100
  13.6 58.6 %all-gather.6.cloned.1.call-start = ((), (), s32[]{:S(2)}) async-start(), calls=%async_computation.14 | async-start | bytes 2506752 | tf_op jit(solution)/shard_map/cond/branch_1_fun/all_gather | solution.py:230
  14.4 104.1 %reduce-scatter.6.cloned.1.call-start = ((), (), s32[]{:S(2)}) async-start(), calls=%async_computation.15 | async-start | bytes 2654208 | tf_op jit(solution)/shard_map/cond/branch_1_fun/reduce_scatter | solution.py:234
  72.2 1.7 %copy-start.2 = (bf16[1536,768]{1,0:T(8,128)(2,1)S(1)}, bf16[1536,768]{1,0:T(8,128)(2,1)}, u32[]{:S(2)}) copy-start(bf16[1536,768]{1,0:T(8,128)(2,1)} %all-gather.6.cloned.1.call-done.w_ref) | copy-start | bytes 7077892 | tf_op jit(solution)/shard_map/cond
Sparse Core Ops, SparseCore 0:
  16.8 55.3 all-gather.5
  76.9 41.5 reduce-scatter.5

commit v8 on v7

--- a/solution.py
+++ b/solution.py
@@ -34,12 +34,7 @@
     return total
 
 
-def size_class(pairs):
-    return sum((pairs > (ROWS * turns - 1) * VCAP).astype(jnp.int32) for turns in SIZES[:-1])
-
-
-def deal_kernel(occ, virt, target, t_ref, *rest):
-    results, (held, packed, sem, out_sem) = rest[:len(SIZES)], rest[len(SIZES):]
+def deal_kernel(occ, virt, target, t_ref, out_ref, held, sem):
     copies = [
         pltpu.make_async_copy(
             t_ref.at[:, h * OCAP:(h + 1) * OCAP], held.at[:, h * OCAP:(h + 1) * OCAP], sem.at[h]
@@ -51,7 +46,7 @@
     lane = lax.broadcasted_iota(jnp.int32, (48, VCAP), 1)
 
     def put(p, value):
-        packed[jnp.bitwise_and(p, 15), :, lax.shift_right_logical(p, 4)] = (
+        out_ref[jnp.bitwise_and(p, 15), :, lax.shift_right_logical(p, 4)] = (
             value.astype(BF).reshape(6, 8, VCAP)
         )
 
@@ -77,27 +72,15 @@
         current = lax.fori_loop(0, (many + STEP - 1) // STEP, some, current)
         first = first + many * wide
     put(lax.shift_right_logical(first, 7), current)
-    which = size_class(first)
-    for n, turns in enumerate(SIZES):
-        @pl.when(which == n)
-        def _(n=n, turns=turns):
-            copy = pltpu.make_async_copy(packed.at[:, :, :turns], results[n], out_sem)
-            copy.start()
-            copy.wait()
-
-
-def deal(amplitudes, occ_count, virt_count, target):
+
+
+def deal(turns, amplitudes, occ_count, virt_count, target):
     return pl.pallas_call(
         deal_kernel,
         in_specs=[scalars()] * 3 + [pl.BlockSpec(memory_space=pl.ANY)],
-        out_specs=[pl.BlockSpec(memory_space=pl.ANY)] * len(SIZES),
-        out_shape=[jax.ShapeDtypeStruct((ROWS, 6, turns, 8, VCAP), BF) for turns in SIZES],
-        scratch_shapes=[
-            pltpu.VMEM((6, KO, 8, VCAP), BF),
-            pltpu.VMEM((ROWS, 6, SIZES[-1], 8, VCAP), BF),
-            pltpu.SemaphoreType.DMA((IRREPS,)),
-            pltpu.SemaphoreType.DMA,
-        ],
+        out_specs=pl.BlockSpec(memory_space=pltpu.VMEM),
+        out_shape=jax.ShapeDtypeStruct((ROWS, 6, turns, 8, VCAP), BF),
+        scratch_shapes=[pltpu.VMEM((6, KO, 8, VCAP), BF), pltpu.SemaphoreType.DMA((IRREPS,))],
         compiler_params=pltpu.CompilerParams(vmem_limit_bytes=56 << 20),
         name="deal",
     )(occ_count, virt_count, target, amplitudes)
@@ -225,10 +208,25 @@
     )(where, occ_count, virt_count, target, got)
 
 
-def contract(turns, w_cycle, dealt, *masks):
+def class_kernel(occ, virt, target, out):
+    pairs = first_column(occ, virt, target, IRREPS)
+    out[0] = sum((pairs > (ROWS * turns - 1) * VCAP).astype(jnp.int32) for turns in SIZES[:-1])
+
+
+def size_class(occ_count, virt_count, target):
+    return pl.pallas_call(
+        class_kernel,
+        in_specs=[scalars()] * 3,
+        out_specs=scalars(),
+        out_shape=jax.ShapeDtypeStruct((1,), jnp.int32),
+        name="size_class",
+    )(occ_count, virt_count, target)
+
+
+def contract(turns, w_cycle, amplitudes, *masks):
     line = ("y", "core")
     w_rows = lax.all_gather(w_cycle, line, axis=0, tiled=True)
-    landed = lax.all_to_all(dealt[SIZES.index(turns)], line, 0, 0, tiled=True)
+    landed = lax.all_to_all(deal(turns, amplitudes, *masks[1:]), line, 0, 0, tiled=True)
     t_rows = repack(landed.reshape(ROWS * 6, turns, 8, VCAP), *masks)
     partial = product(w_rows, t_rows)
     by_z = lax.psum_scatter(partial, "z", scatter_dimension=0, tiled=True)
@@ -240,14 +238,10 @@
     row = lax.axis_index("y") * 2 + lax.axis_index("core")
     col = lax.axis_index("x") * 8 + lax.axis_index("z")
     masks = (jnp.stack([row, col]).astype(jnp.int32), occ_count, virt_count, target)
-    irreps = jnp.arange(IRREPS, dtype=jnp.int32)
-    meets = jnp.bitwise_xor(irreps, target)[:, None] == irreps[None, :]
-    pairs = jnp.sum(jnp.where(meets, occ_count[:, None] * virt_count[None, :], 0))
-    dealt = deal(amplitudes, occ_count, virt_count, target)
     got = lax.switch(
-        size_class(pairs),
+        size_class(occ_count, virt_count, target)[0],
         [functools.partial(contract, turns) for turns in SIZES],
-        w_cycle, dealt, *masks,
+        w_cycle, amplitudes, *masks,
     )
     return place(got, *masks)
 

time: 161 us -> 156 us (0.969)
  waiting for transfers between devices: 51.7 us -> 47.4 us
  Pallas kernels: 10.6 us -> 13.3 us
  blocking collectives: 79.8 us -> 77.8 us
    reduce_scatter x1, waiting for transfers between devices: 41.7 us -> 38.4 us  [contract(): by_z = lax.psum_scatter(partial, 'z', scatter_dimension=0, tiled=True)]
    all_to_all x1, blocking collectives: 46.9 us -> 44.5 us  [contract(): lax.all_to_all(deal(turns, amplitudes, *masks[1:]), line, 0, 0, tiled=True)]
  transfers between devices with their start and end apart: 2 -> 2, of which waited for: 2 -> 2; matrix products, arithmetic and copies ran while one was open for 0% -> 0% of each run, Pallas kernels for 1% -> 4%
where the time goes in v8:
time: 156 us; the launch traced here: 155 us
  blocking collectives  77.8 us (50%)
  waiting for transfers between devices  47.4 us (30%)
  between operations  14.7 us (9%)
  Pallas kernels  13.3 us (9%)
  local copies, waits for them, and re-layouts  1.68 us (1%)
    all_to_all x1, blocking collectives, contract(): lax.all_to_all(deal(turns, amplitudes, *masks[1:]), line, 0, 0, tiled=True)  44.5 us
    reduce_scatter x1, waiting for transfers between devices, contract(): by_z = lax.psum_scatter(partial, 'z', scatter_dimension=0, tiled=True)  38.4 us
    all_to_all x1, blocking collectives, contract(): return lax.all_to_all(send_out(by_x, *masks), line, 0, 0, tiled=True)  23 us
    all_to_all x1, blocking collectives, contract(): lax.all_to_all(by_z, 'x', 0, 0, tiled=True).reshape(4, BLOCK, turns * VCAP)  10.4 us
    all_gather x1, waiting for transfers between devices, contract(): w_rows = lax.all_gather(w_cycle, line, axis=0, tiled=True)  8.26 us
    pallas_call x1, Pallas kernels, deal(): pl.pallas_call(deal_kernel, in_specs=[scalars()] * 3 + [pl.BlockSpec(memo...  5 us
  transfers between devices with their start and end apart: 2, of which 2 were waited for; matrix products, arithmetic and copies ran while one was open for 0% of the time, Pallas kernels for 4%

profile of v8, /device:TPU:1, one launch (start us, length us, event | category | flops | bytes accessed | tf_op | source)
XLA Modules:
  0.0 155.1 jit_solution(11087502525191403966)
XLA Ops:
  7.2 0.1 pad_add_fusion.where
  7.3 1.2 size_class.1
  9.1 137.6 %conditional.1 = (bf16[16,48,128]{2,1,0:T(8,128)(2,1)S(1)}) conditional(s32[]{:T(128)} %bitcast.11, (bf16[96,768]{1,0:T(8,128)(2,1)}, s32[8]{0:T(128)}, s32[8]{0:T(128)}, s32[1]{0:T(128)}, bf16[6,192,8,128]{3,2,1,0:T(8,128)(2,1)}, /*index=5*/s32[2]{0:T(128)S(1)}) %tuple.14, (bf16[96,768]{1,0:T(8,128)(2,1)}, s32[8]{0:T(128)}, ...), branch_computations={%region_0.0_spmd, %region_2.0_spmd, %region_4.0_spmd} | conditional | bytes 31900076 | solution.py:241
  9.1 0.0 all-gather.4.cloned.1.call-start
  9.2 0.7 all-gather.4.cloned.1.call-update
  9.9 0.0 reduce-scatter.4.cloned.1.call-start
  9.9 0.0 copy-start.3
  9.9 0.0 copy-start.6
  9.9 5.0 %deal.3 = bf16[16,6,5,8,128]{4,3,2,1,0:T(8,128)(2,1)} custom-call(s32[8]{0:T(128)} %get-tuple-element.46.occ, s32[8]{0:T(128)} %get-tuple-element.47.virt, s32[1]{0:T(128)} %get-tuple-element.48.target, bf16[6,192,8,128]{3,2,1,0:T(8,128)(2,1)} %get-tuple-element.50.t_ref), custom_call_target="tpu_custom_call" | custom-call | tf_op jit(solution)/shard_map/cond/branch_0_fun/deal/pallas_call | solution.py:78
  15.0 44.5 %all_to_all.45 = bf16[16,6,5,8,128]{4,3,2,1,0:T(8,128)(2,1)S(1)} all-to-all(bf16[16,6,5,8,128]{4,3,2,1,0:T(8,128)(2,1)} %deal.3), channel_id=1, replica_groups=mesh['y'=8,'core'=2,'x'=4,'z'=8] {'y','core'}, dimensions={0} | all-to-all | bytes 1966080 | tf_op jit(solution)/shard_map/cond/branch_0_fun/all_to_all | solution.py:229
  59.4 0.0 copy-done.3
  59.4 0.0 copy-done.6
  59.4 1.5 repack.3.t_ref
  60.9 8.3 %all-gather.4.cloned.1.call-done.w_ref = bf16[1536,768]{1,0:T(8,128)(2,1)} async-done(((bf16[96,768]{1,0:T(8,128)(2,1)}), bf16[1536,768]{1,0:T(8,128)(2,1)}) %all-gather.4.cloned.1.call-update) | async-done | bytes 2359312 | tf_op jit(solution)/shard_map/cond/branch_0_fun/all_gather | solution.py:228
  69.2 0.0 copy-start.1
  69.2 1.7 %copy-done.1 = bf16[1536,768]{1,0:T(8,128)(2,1)S(1)} copy-done((bf16[1536,768]{1,0:T(8,128)(2,1)S(1)}, bf16[1536,768]{1,0:T(8,128)(2,1)}, u32[]{:S(2)}) %copy-start.1) | copy-done | bytes 2359320 | tf_op jit(solution)/shard_map/cond
  70.9 2.8 %product.3 = bf16[8,4,48,640]{3,2,1,0:T(8,128)(2,1)} custom-call(bf16[1536,768]{1,0:T(8,128)(2,1)S(1)} %copy-done.1, bf16[768,640]{1,0:T(8,128)(2,1)S(1)} %repack.3.t_ref), custom_call_target="tpu_custom_call" | custom-call | tf_op jit(solution)/shard_map/cond/branch_0_fun/product/pallas_call | solution.py:136
  73.7 0.0 reduce-scatter.4.cloned.1.call-update
  73.7 38.4 %reduce-scatter.4.cloned.1.call-done = bf16[192,640]{1,0:T(8,128)(2,1)} async-done(((bf16[1536,640]{1,0:T(8,128)(2,1)}), bf16[192,640]{1,0:T(8,128)(2,1)}) %reduce-scatter.4.cloned.1.call-update) | async-done | bytes 245776 | tf_op jit(solution)/shard_map/cond/branch_0_fun/reduce_scatter | solution.py:232
  112.2 10.4 %all_to_all.46.parts_ref = bf16[4,48,640]{2,1,0:T(8,128)(2,1)S(1)} all-to-all(bf16[4,48,640]{2,1,0:T(8,128)(2,1)} %bitcast.17), channel_id=1, replica_groups=mesh['y'=8,'core'=2,'x'=4,'z'=8] {'x'}, dimensions={0} | all-to-all | bytes 491520 | tf_op jit(solution)/shard_map/cond/branch_0_fun/all_to_all | solution.py:233
  122.5 1.3 send_out.3
  123.8 23.0 %all_to_all.47 = bf16[16,48,128]{2,1,0:T(8,128)(2,1)S(1)} all-to-all(bf16[16,48,128]{2,1,0:T(8,128)(2,1)S(1)} %send_out.3), channel_id=1, replica_groups=mesh['y'=8,'core'=2,'x'=4,'z'=8] {'y','core'}, dimensions={0} | all-to-all | bytes 393216 | tf_op jit(solution)/shard_map/cond/branch_0_fun/all_to_all | solution.py:234
  146.8 1.5 place.1
Async XLA Ops:
  9.1 60.1 %all-gather.4.cloned.1.call-start = ((), (), s32[]{:S(2)}) async-start(), calls=%async_computation.12 | async-start | bytes 2506752 | tf_op jit(solution)/shard_map/cond/branch_0_fun/all_gather | solution.py:228
  9.9 102.3 %reduce-scatter.4.cloned.1.call-start = ((), (), s32[]{:S(2)}) async-start(), calls=%async_computation.13 | async-start | bytes 2211840 | tf_op jit(solution)/shard_map/cond/branch_0_fun/reduce_scatter | solution.py:232
  9.9 49.5 %copy-start.3 = (s32[8]{0:T(128)S(1)}, s32[8]{0:T(128)}, u32[]{:S(2)}) copy-start(s32[8]{0:T(128)} %get-tuple-element.46.occ) | copy-start | bytes 100 | tf_op jit(solution)/shard_map/cond
  9.9 49.5 %copy-start.6 = (s32[8]{0:T(128)S(1)}, s32[8]{0:T(128)}, u32[]{:S(2)}) copy-start(s32[8]{0:T(128)} %get-tuple-element.47.virt) | copy-start | bytes 100 | tf_op jit(solution)/shard_map/cond
  69.2 1.7 %copy-start.1 = (bf16[1536,768]{1,0:T(8,128)(2,1)S(1)}, bf16[1536,768]{1,0:T(8,128)(2,1)}, u32[]{:S(2)}) copy-start(bf16[1536,768]{1,0:T(8,128)(2,1)} %all-gather.4.cloned.1.call-done.w_ref) | copy-start | bytes 7077892 | tf_op jit(solution)/shard_map/cond
Sparse Core Ops, SparseCore 0:
  12.1 57.0 all-gather.3
  73.8 38.2 reduce-scatter.3

commit v9 on v7

--- a/solution.py
+++ b/solution.py
@@ -39,7 +39,7 @@
 
 
 def deal_kernel(occ, virt, target, t_ref, *rest):
-    results, (held, packed, sem, out_sem) = rest[:len(SIZES)], rest[len(SIZES):]
+    results, (class_ref, held, packed, sem, out_sem) = rest[:len(SIZES)], rest[len(SIZES):]
     copies = [
         pltpu.make_async_copy(
             t_ref.at[:, h * OCAP:(h + 1) * OCAP], held.at[:, h * OCAP:(h + 1) * OCAP], sem.at[h]
@@ -78,6 +78,7 @@
         first = first + many * wide
     put(lax.shift_right_logical(first, 7), current)
     which = size_class(first)
+    class_ref[0] = which
     for n, turns in enumerate(SIZES):
         @pl.when(which == n)
         def _(n=n, turns=turns):
@@ -90,8 +91,9 @@
     return pl.pallas_call(
         deal_kernel,
         in_specs=[scalars()] * 3 + [pl.BlockSpec(memory_space=pl.ANY)],
-        out_specs=[pl.BlockSpec(memory_space=pl.ANY)] * len(SIZES),
-        out_shape=[jax.ShapeDtypeStruct((ROWS, 6, turns, 8, VCAP), BF) for turns in SIZES],
+        out_specs=[pl.BlockSpec(memory_space=pl.ANY)] * len(SIZES) + [scalars()],
+        out_shape=[jax.ShapeDtypeStruct((ROWS, 6, turns, 8, VCAP), BF) for turns in SIZES]
+        + [jax.ShapeDtypeStruct((1,), jnp.int32)],
         scratch_shapes=[
             pltpu.VMEM((6, KO, 8, VCAP), BF),
             pltpu.VMEM((ROWS, 6, SIZES[-1], 8, VCAP), BF),
@@ -240,12 +242,9 @@
     row = lax.axis_index("y") * 2 + lax.axis_index("core")
     col = lax.axis_index("x") * 8 + lax.axis_index("z")
     masks = (jnp.stack([row, col]).astype(jnp.int32), occ_count, virt_count, target)
-    irreps = jnp.arange(IRREPS, dtype=jnp.int32)
-    meets = jnp.bitwise_xor(irreps, target)[:, None] == irreps[None, :]
-    pairs = jnp.sum(jnp.where(meets, occ_count[:, None] * virt_count[None, :], 0))
-    dealt = deal(amplitudes, occ_count, virt_count, target)
+    *dealt, which = deal(amplitudes, occ_count, virt_count, target)
     got = lax.switch(
-        size_class(pairs),
+        which[0],
         [functools.partial(contract, turns) for turns in SIZES],
         w_cycle, dealt, *masks,
     )

time: 161 us -> 161 us (level)
  no operation moved by 1% of the time
where the time goes in v9:
time: 161 us; the launch traced here: 160 us
  blocking collectives  81.4 us (51%)
  waiting for transfers between devices  50.2 us (31%)
  between operations  14.7 us (9%)
  Pallas kernels  11.9 us (7%)
  local copies, waits for them, and re-layouts  1.67 us (1%)
    all_to_all x1, blocking collectives, contract(): landed = lax.all_to_all(dealt[SIZES.index(turns)], line, 0, 0, tiled=True)  48.4 us
    reduce_scatter x1, waiting for transfers between devices, contract(): by_z = lax.psum_scatter(partial, 'z', scatter_dimension=0, tiled=True)  40.6 us
    all_to_all x1, blocking collectives, contract(): return lax.all_to_all(send_out(by_x, *masks), line, 0, 0, tiled=True)  23 us
    all_to_all x1, blocking collectives, contract(): lax.all_to_all(by_z, 'x', 0, 0, tiled=True).reshape(4, BLOCK, turns * VCAP)  9.99 us
    all_gather x1, waiting for transfers between devices, contract(): w_rows = lax.all_gather(w_cycle, line, axis=0, tiled=True)  8.83 us
    pallas_call x1, Pallas kernels, deal(): pl.pallas_call(deal_kernel, in_specs=[scalars()] * 3 + [pl.BlockSpec(memo...  4.97 us
  transfers between devices with their start and end apart: 2, of which 2 were waited for; matrix products, arithmetic and copies ran while one was open for 0% of the time, Pallas kernels for 1%

profile of v9, /device:TPU:1, one launch (start us, length us, event | category | flops | bytes accessed | tf_op | source)
XLA Modules:
  0.0 160.1 jit_solution(16565550403657263710)
XLA Ops:
  6.5 0.0 copy-start.4
  6.5 0.0 copy-start.3
  7.2 0.1 pad_add_fusion.where
  7.3 5.0 %deal.1 = (bf16[16,6,5,8,128]{4,3,2,1,0:T(8,128)(2,1)S(1)}, bf16[16,6,6,8,128]{4,3,2,1,0:T(8,128)(2,1)}, bf16[16,6,8,8,128]{4,3,2,1,0:T(8,128)(2,1)S(1)}, s32[1]{0:T(128)}) custom-call(s32[8]{0:T(128)} %occ.3, s32[8]{0:T(128)} %virt.3, s32[1]{0:T(128)S(6)} %copy.9.target, bf16[6,192,8,128]{3,2,1,0:T(8,128)(2,1)} %t_ref.1), custom_call_target="tpu_custom_call" | custom-call | tf_op jit(solution)/shard_map/deal/pallas_call | solution.py:91
  12.9 0.0 copy-done.4
  12.9 0.0 copy-done.3
  12.9 139.0 %conditional.1 = (bf16[16,48,128]{2,1,0:T(8,128)(2,1)S(1)}) conditional(s32[]{:T(128)} %bitcast.11, (bf16[96,768]{1,0:T(8,128)(2,1)}, bf16[16,6,5,8,128]{4,3,2,1,0:T(8,128)(2,1)S(1)}, s32[2]{0:T(128)S(1)}, s32[8]{0:T(128)S(1)}, s32[8]{0:T(128)S(1)}, /*index=5*/s32[1]{0:T(128)}) %tuple.35, (bf16[96,768]{1,0:T(8,128)(2,1)}, ...), branch_computations={%region_0.0_spmd, %region_2.0_spmd, %region_4.0_spmd} | conditional | bytes 31899764 | solution.py:246
  13.0 0.0 all-gather.6.cloned.1.call-start
  13.0 0.7 all-gather.6.cloned.1.call-update
  13.7 0.0 reduce-scatter.6.cloned.1.call-start
  13.7 48.4 %all_to_all.48 = bf16[16,6,6,8,128]{4,3,2,1,0:T(8,128)(2,1)S(1)} all-to-all(bf16[16,6,6,8,128]{4,3,2,1,0:T(8,128)(2,1)} %get-tuple-element.56), channel_id=1, replica_groups=mesh['y'=8,'core'=2,'x'=4,'z'=8] {'y','core'}, dimensions={0} | all-to-all | bytes 2359296 | tf_op jit(solution)/shard_map/cond/branch_1_fun/all_to_all | solution.py:233
  62.1 1.6 repack.4.t_ref
  63.7 8.8 %all-gather.6.cloned.1.call-done.w_ref = bf16[1536,768]{1,0:T(8,128)(2,1)} async-done(((bf16[96,768]{1,0:T(8,128)(2,1)}), bf16[1536,768]{1,0:T(8,128)(2,1)}) %all-gather.6.cloned.1.call-update) | async-done | bytes 2359312 | tf_op jit(solution)/shard_map/cond/branch_1_fun/all_gather | solution.py:232
  72.5 0.0 copy-start.2
  72.5 1.7 %copy-done.2 = bf16[1536,768]{1,0:T(8,128)(2,1)S(1)} copy-done((bf16[1536,768]{1,0:T(8,128)(2,1)S(1)}, bf16[1536,768]{1,0:T(8,128)(2,1)}, u32[]{:S(2)}) %copy-start.2) | copy-done | bytes 2359320 | tf_op jit(solution)/shard_map/cond
  74.2 2.8 %product.4 = bf16[8,4,48,768]{3,2,1,0:T(8,128)(2,1)} custom-call(bf16[1536,768]{1,0:T(8,128)(2,1)S(1)} %copy-done.2, bf16[768,768]{1,0:T(8,128)(2,1)S(1)} %repack.4.t_ref), custom_call_target="tpu_custom_call" | custom-call | tf_op jit(solution)/shard_map/cond/branch_1_fun/product/pallas_call | solution.py:155
  77.0 0.0 reduce-scatter.6.cloned.1.call-update
  77.0 40.6 %reduce-scatter.6.cloned.1.call-done = bf16[192,768]{1,0:T(8,128)(2,1)} async-done(((bf16[1536,768]{1,0:T(8,128)(2,1)}), bf16[192,768]{1,0:T(8,128)(2,1)}) %reduce-scatter.6.cloned.1.call-update) | async-done | bytes 294928 | tf_op jit(solution)/shard_map/cond/branch_1_fun/reduce_scatter | solution.py:236
  117.6 10.0 %all_to_all.49.parts_ref = bf16[4,48,768]{2,1,0:T(8,128)(2,1)S(1)} all-to-all(bf16[4,48,768]{2,1,0:T(8,128)(2,1)} %bitcast.16), channel_id=1, replica_groups=mesh['y'=8,'core'=2,'x'=4,'z'=8] {'x'}, dimensions={0} | all-to-all | bytes 589824 | tf_op jit(solution)/shard_map/cond/branch_1_fun/all_to_all | solution.py:237
  127.6 1.3 send_out.4
  128.9 23.0 %all_to_all.50 = bf16[16,48,128]{2,1,0:T(8,128)(2,1)S(1)} all-to-all(bf16[16,48,128]{2,1,0:T(8,128)(2,1)S(1)} %send_out.4), channel_id=1, replica_groups=mesh['y'=8,'core'=2,'x'=4,'z'=8] {'y','core'}, dimensions={0} | all-to-all | bytes 393216 | tf_op jit(solution)/shard_map/cond/branch_1_fun/all_to_all | solution.py:238
  151.9 1.4 place.1
Async XLA Ops:
  6.5 6.4 %copy-start.4 = (s32[8]{0:T(128)S(1)}, s32[8]{0:T(128)}, u32[]{:S(2)}) copy-start(s32[8]{0:T(128)} %virt.3) | copy-start | bytes 100
  6.5 6.4 %copy-start.3 = (s32[8]{0:T(128)S(1)}, s32[8]{0:T(128)}, u32[]{:S(2)}) copy-start(s32[8]{0:T(128)} %occ.3) | copy-start | bytes 100
  13.0 59.5 %all-gather.6.cloned.1.call-start = ((), (), s32[]{:S(2)}) async-start(), calls=%async_computation.14 | async-start | bytes 2506752 | tf_op jit(solution)/shard_map/cond/branch_1_fun/all_gather | solution.py:232
  13.7 103.9 %reduce-scatter.6.cloned.1.call-start = ((), (), s32[]{:S(2)}) async-start(), calls=%async_computation.15 | async-start | bytes 2654208 | tf_op jit(solution)/shard_map/cond/branch_1_fun/reduce_scatter | solution.py:236
  72.5 1.7 %copy-start.2 = (bf16[1536,768]{1,0:T(8,128)(2,1)S(1)}, bf16[1536,768]{1,0:T(8,128)(2,1)}, u32[]{:S(2)}) copy-start(bf16[1536,768]{1,0:T(8,128)(2,1)} %all-gather.6.cloned.1.call-done.w_ref) | copy-start | bytes 7077892 | tf_op jit(solution)/shard_map/cond
Sparse Core Ops, SparseCore 0:
  16.1 56.3 all-gather.5
  77.1 40.4 reduce-scatter.5

commit v10 on v9

--- a/solution.py
+++ b/solution.py
@@ -121,23 +121,22 @@
 
 
 def repack(landed, where, occ_count, virt_count, target):
-    turns = landed.shape[1]
     return pl.pallas_call(
         repack_kernel,
         in_specs=[scalars()] * 4 + [pl.BlockSpec(memory_space=pltpu.VMEM)],
         out_specs=pl.BlockSpec(memory_space=pltpu.VMEM),
-        out_shape=jax.ShapeDtypeStruct((6 * VCAP, turns * VCAP), BF),
+        out_shape=jax.ShapeDtypeStruct((6 * VCAP, SIZES[-1] * VCAP), BF),
         compiler_params=pltpu.CompilerParams(vmem_limit_bytes=24 << 20),
         name="repack",
     )(where, occ_count, virt_count, target, landed)
 
 
 def product_kernel(w_ref, t_ref, out_ref, held, sem):
-    tall = 4 * BLOCK
+    tall, width = 4 * BLOCK, held.shape[3]
     copies = []
     for n in range(8):
         value = jnp.dot(
-            w_ref[n * tall:(n + 1) * tall, :], t_ref[...], preferred_element_type=F32
+            w_ref[n * tall:(n + 1) * tall, :], t_ref[:, :width], preferred_element_type=F32
         )
         for z in range(4):
             held[n, z] = value[z * BLOCK:(z + 1) * BLOCK].astype(BF)
@@ -149,9 +148,9 @@
         copy.wait()
 
 
-def product(w_rows, t_rows):
+def product(turns, w_rows, t_rows):
     rows = w_rows.shape[0]
-    width = t_rows.shape[1]
+    width = turns * VCAP
     out = pl.pallas_call(
         product_kernel,
         in_specs=[pl.BlockSpec(memory_space=pltpu.VMEM)] * 2,
@@ -227,15 +226,16 @@
     )(where, occ_count, virt_count, target, got)
 
 
-def contract(turns, w_cycle, dealt, *masks):
-    line = ("y", "core")
-    w_rows = lax.all_gather(w_cycle, line, axis=0, tiled=True)
-    landed = lax.all_to_all(dealt[SIZES.index(turns)], line, 0, 0, tiled=True)
-    t_rows = repack(landed.reshape(ROWS * 6, turns, 8, VCAP), *masks)
-    partial = product(w_rows, t_rows)
+def bring(turns, dealt, *masks):
+    landed = lax.all_to_all(dealt[SIZES.index(turns)], ("y", "core"), 0, 0, tiled=True)
+    return repack(landed.reshape(ROWS * 6, turns, 8, VCAP), *masks)
+
+
+def contract(turns, w_rows, t_rows, *masks):
+    partial = product(turns, w_rows, t_rows)
     by_z = lax.psum_scatter(partial, "z", scatter_dimension=0, tiled=True)
     by_x = lax.all_to_all(by_z, "x", 0, 0, tiled=True).reshape(4, BLOCK, turns * VCAP)
-    return lax.all_to_all(send_out(by_x, *masks), line, 0, 0, tiled=True)
+    return lax.all_to_all(send_out(by_x, *masks), ("y", "core"), 0, 0, tiled=True)
 
 
 def per_device(w_cycle, amplitudes, occ_count, virt_count, target):
@@ -243,10 +243,12 @@
     col = lax.axis_index("x") * 8 + lax.axis_index("z")
     masks = (jnp.stack([row, col]).astype(jnp.int32), occ_count, virt_count, target)
     *dealt, which = deal(amplitudes, occ_count, virt_count, target)
+    w_rows = lax.all_gather(w_cycle, ("y", "core"), axis=0, tiled=True)
+    t_rows = lax.switch(
+        which[0], [functools.partial(bring, turns) for turns in SIZES], dealt, *masks
+    )
     got = lax.switch(
-        which[0],
-        [functools.partial(contract, turns) for turns in SIZES],
-        w_cycle, dealt, *masks,
+        which[0], [functools.partial(contract, turns) for turns in SIZES], w_rows, t_rows, *masks
     )
     return place(got, *masks)
 

time: 161 us -> 153 us (0.950)
  blocking collectives: 81.4 us -> 75.3 us
  local copies, waits for them, and re-layouts: 1.67 us -> 0.01 us
    all_to_all x2, blocking collectives: 71.4 us -> 65.8 us  [the longest x1 42.9 us: bring(): lax.all_to_all(dealt[SIZES.index(turns)], ('y', 'core'), 0, 0, tiled=True)]
    pallas_call x1, Pallas kernels: 2.81 us -> 4.5 us  [product(): pl.pallas_call(product_kernel, in_specs=[pl.BlockSpec(memory_space=pltpu....]
    cond x2 -> x0, local copies, waits for them, and re-layouts: 1.66 us -> none
  transfers between devices with their start and end apart: 2 -> 2, of which waited for: 2 -> 2; matrix products, arithmetic and copies ran while one was open for 0% -> 0% of each run, Pallas kernels for 1% -> 4%
where the time goes in v10:
time: 153 us
  blocking collectives  75.3 us (49%)
  waiting for transfers between devices  49.6 us (32%)
  between operations  14.7 us (10%)
  Pallas kernels  12.8 us (8%)
    all_to_all x1, blocking collectives, bring(): lax.all_to_all(dealt[SIZES.index(turns)], ('y', 'core'), 0, 0, tiled=True)  42.9 us
    reduce_scatter x1, waiting for transfers between devices, contract(): by_z = lax.psum_scatter(partial, 'z', scatter_dimension=0, tiled=True)  40.2 us
    all_to_all x1, blocking collectives, contract(): lax.all_to_all(send_out(by_x, *masks), ('y', 'core'), 0, 0, tiled=True)  22.9 us
    all_to_all x1, blocking collectives, contract(): lax.all_to_all(by_z, 'x', 0, 0, tiled=True).reshape(4, BLOCK, turns * VCAP)  9.48 us
    all_gather x1, waiting for transfers between devices, per_device(): w_rows = lax.all_gather(w_cycle, ('y', 'core'), axis=0, tiled=True)  8.67 us
    pallas_call x1, Pallas kernels, product(): pl.pallas_call(product_kernel, in_specs=[pl.BlockSpec(memory_space=pltpu....  4.5 us
    pallas_call x1, Pallas kernels, deal(): pl.pallas_call(deal_kernel, in_specs=[scalars()] * 3 + [pl.BlockSpec(memo...  4.09 us
  transfers between devices with their start and end apart: 2, of which 2 were waited for; matrix products, arithmetic and copies ran while one was open for 0% of the time, Pallas kernels for 4%

profile of v10, /device:TPU:1, one launch (start us, length us, event | category | flops | bytes accessed | tf_op | source)
XLA Modules:
  0.0 152.6 jit_solution(7747442361558759196)
XLA Ops:
  6.5 0.0 copy-start
  6.5 0.0 copy-start.1
  6.5 0.0 all-gather.2.cloned.1.call-start
  6.5 0.7 all-gather.2.cloned.1.call-update
  7.9 4.1 %deal.1 = (bf16[16,6,5,8,128]{4,3,2,1,0:T(8,128)(2,1)S(1)}, bf16[16,6,6,8,128]{4,3,2,1,0:T(8,128)(2,1)S(1)}, bf16[16,6,8,8,128]{4,3,2,1,0:T(8,128)(2,1)S(1)}, s32[1]{0:T(128)}) custom-call(s32[8]{0:T(128)} %occ.3, s32[8]{0:T(128)} %virt.3, s32[1]{0:T(128)S(6)} %copy.12.target, bf16[6,192,8,128]{3,2,1,0:T(8,128)(2,1)} %t_ref.1), custom_call_target="tpu_custom_call" | custom-call | tf_op jit(solution)/shard_map/deal/pallas_call | solution.py:91
  12.0 0.1 pad_add_fusion.where
  12.7 0.0 copy-done
  12.7 0.0 copy-done.1
  12.7 44.5 %conditional.2 = (bf16[768,1024]{1,0:T(8,128)(2,1)S(1)}) conditional(s32[]{:T(128)} %bitcast.11, (bf16[16,6,5,8,128]{4,3,2,1,0:T(8,128)(2,1)S(1)}, s32[2]{0:T(128)S(1)}, s32[8]{0:T(128)S(1)}, s32[8]{0:T(128)S(1)}, s32[1]{0:T(128)}) %tuple.47, (bf16[16,6,6,8,128]{4,3,2,1,0:T(8,128)(2,1)S(1)}, s32[2]{0:T(128)S(1)}, s32[8]{0:T(128)S(1)}, ...), branch_computations={%region_0.0_spmd, %region_1.0_spmd, %region_2.0_spmd} | conditional | bytes 3145736 | solution.py:247
  12.8 42.9 %all_to_all.45 = bf16[16,6,5,8,128]{4,3,2,1,0:T(8,128)(2,1)S(1)} all-to-all(bf16[16,6,5,8,128]{4,3,2,1,0:T(8,128)(2,1)S(1)} %get-tuple-element.83), channel_id=1, replica_groups=mesh['y'=8,'core'=2,'x'=4,'z'=8] {'y','core'}, dimensions={0} | all-to-all | bytes 1966080 | tf_op jit(solution)/shard_map/cond/branch_0_fun/all_to_all | solution.py:230
  55.7 1.5 %repack.3 = bf16[768,1024]{1,0:T(8,128)(2,1)S(1)} custom-call(s32[2]{0:T(128)S(1)} %get-tuple-element.70.where, s32[8]{0:T(128)S(1)} %get-tuple-element.78.occ, s32[8]{0:T(128)S(1)} %get-tuple-element.80.virt, s32[1]{0:T(128)} %get-tuple-element.82.target, bf16[96,5,8,128]{3,2,1,0:T(8,128)(2,1)S(1)} %bitcast.14), custom_call_target="tpu_custom_call" | custom-call | tf_op jit(solution)/shard_map/cond/branch_0_fun/repack/pallas_call | solution.py:124
  57.2 8.7 %all-gather.2.cloned.1.call-done = bf16[1536,768]{1,0:T(8,128)(2,1)} async-done(((bf16[96,768]{1,0:T(8,128)(2,1)}), bf16[1536,768]{1,0:T(8,128)(2,1)}) %all-gather.2.cloned.1.call-update) | async-done | bytes 2359312 | tf_op jit(solution)/shard_map/all_gather | solution.py:246
  65.9 78.4 %conditional.3 = (bf16[16,48,128]{2,1,0:T(8,128)(2,1)S(1)}) conditional(s32[]{:T(128)} %bitcast.11, (bf16[1536,768]{1,0:T(8,128)(2,1)}, bf16[768,1024]{1,0:T(8,128)(2,1)S(1)}, s32[2]{0:T(128)S(1)}, s32[8]{0:T(128)S(1)}, s32[8]{0:T(128)S(1)}, /*index=5*/s32[1]{0:T(128)}) %tuple.50, (bf16[1536,768]{1,0:T(8,128)(2,1)}, ...), branch_computations={%region_3.0_spmd, %region_5.0_spmd, %region_7.0_spmd} | conditional | bytes 11796528 | solution.py:250
  65.9 0.0 reduce-scatter.4.cloned.1.call-start
  65.9 4.5 %product.3 = bf16[8,4,48,640]{3,2,1,0:T(8,128)(2,1)} custom-call(bf16[1536,768]{1,0:T(8,128)(2,1)} %get-tuple-element.98.w_ref, bf16[768,1024]{1,0:T(8,128)(2,1)S(1)} %get-tuple-element.99.t_ref), custom_call_target="tpu_custom_call" | custom-call | tf_op jit(solution)/shard_map/cond/branch_0_fun/product/pallas_call | solution.py:154
  70.4 0.0 reduce-scatter.4.cloned.1.call-update
  70.5 40.2 %reduce-scatter.4.cloned.1.call-done = bf16[192,640]{1,0:T(8,128)(2,1)} async-done(((bf16[1536,640]{1,0:T(8,128)(2,1)}), bf16[192,640]{1,0:T(8,128)(2,1)}) %reduce-scatter.4.cloned.1.call-update) | async-done | bytes 245776 | tf_op jit(solution)/shard_map/cond/branch_0_fun/reduce_scatter | solution.py:236
  110.7 9.5 %all_to_all.48.parts_ref = bf16[4,48,640]{2,1,0:T(8,128)(2,1)S(1)} all-to-all(bf16[4,48,640]{2,1,0:T(8,128)(2,1)} %bitcast.17), channel_id=1, replica_groups=mesh['y'=8,'core'=2,'x'=4,'z'=8] {'x'}, dimensions={0} | all-to-all | bytes 491520 | tf_op jit(solution)/shard_map/cond/branch_0_fun/all_to_all | solution.py:237
  120.2 1.3 send_out.3
  121.4 22.9 %all_to_all.49 = bf16[16,48,128]{2,1,0:T(8,128)(2,1)S(1)} all-to-all(bf16[16,48,128]{2,1,0:T(8,128)(2,1)S(1)} %send_out.3), channel_id=1, replica_groups=mesh['y'=8,'core'=2,'x'=4,'z'=8] {'y','core'}, dimensions={0} | all-to-all | bytes 393216 | tf_op jit(solution)/shard_map/cond/branch_0_fun/all_to_all | solution.py:238
  144.4 1.4 place.1
Async XLA Ops:
  6.5 6.2 %copy-start = (s32[8]{0:T(128)S(1)}, s32[8]{0:T(128)}, u32[]{:S(2)}) copy-start(s32[8]{0:T(128)} %occ.3) | copy-start | bytes 100
  6.5 6.2 %copy-start.1 = (s32[8]{0:T(128)S(1)}, s32[8]{0:T(128)}, u32[]{:S(2)}) copy-start(s32[8]{0:T(128)} %virt.3) | copy-start | bytes 100
  6.5 59.4 %all-gather.2.cloned.1.call-start = ((), (), s32[]{:S(2)}) async-start(), calls=%async_computation.15 | async-start | bytes 2506752 | tf_op jit(solution)/shard_map/all_gather | solution.py:246
  65.9 44.8 %reduce-scatter.4.cloned.1.call-start = ((), (), s32[]{:S(2)}) async-start(), calls=%async_computation.12 | async-start | bytes 2211840 | tf_op jit(solution)/shard_map/cond/branch_0_fun/reduce_scatter | solution.py:236
Sparse Core Ops, SparseCore 0:
  9.7 56.1 all-gather.1
  70.6 40.0 reduce-scatter.3

commit v11 on v10

--- a/solution.py
+++ b/solution.py
@@ -131,12 +131,21 @@
     )(where, occ_count, virt_count, target, landed)
 
 
-def product_kernel(w_ref, t_ref, out_ref, held, sem):
+def product_kernel(w_ref, t_ref, out_ref, w_held, held, w_sem, sem):
     tall, width = 4 * BLOCK, held.shape[3]
+    arrivals = [
+        pltpu.make_async_copy(
+            w_ref.at[n * tall:(n + 1) * tall], w_held.at[n * tall:(n + 1) * tall], w_sem.at[n]
+        )
+        for n in range(8)
+    ]
+    for copy in arrivals:
+        copy.start()
     copies = []
     for n in range(8):
+        arrivals[n].wait()
         value = jnp.dot(
-            w_ref[n * tall:(n + 1) * tall, :], t_ref[:, :width], preferred_element_type=F32
+            w_held[n * tall:(n + 1) * tall, :], t_ref[:, :width], preferred_element_type=F32
         )
         for z in range(4):
             held[n, z] = value[z * BLOCK:(z + 1) * BLOCK].astype(BF)
@@ -149,18 +158,23 @@
 
 
 def product(turns, w_rows, t_rows):
-    rows = w_rows.shape[0]
+    rows, depth = w_rows.shape
     width = turns * VCAP
     out = pl.pallas_call(
         product_kernel,
-        in_specs=[pl.BlockSpec(memory_space=pltpu.VMEM)] * 2,
+        in_specs=[pl.BlockSpec(memory_space=pl.ANY), pl.BlockSpec(memory_space=pltpu.VMEM)],
         out_specs=pl.BlockSpec(memory_space=pl.ANY),
         out_shape=jax.ShapeDtypeStruct((8, 4, BLOCK, width), BF),
-        scratch_shapes=[pltpu.VMEM((8, 4, BLOCK, width), BF), pltpu.SemaphoreType.DMA((8,))],
-        compiler_params=pltpu.CompilerParams(vmem_limit_bytes=24 << 20),
+        scratch_shapes=[
+            pltpu.VMEM((rows, depth), BF),
+            pltpu.VMEM((8, 4, BLOCK, width), BF),
+            pltpu.SemaphoreType.DMA((8,)),
+            pltpu.SemaphoreType.DMA((8,)),
+        ],
+        compiler_params=pltpu.CompilerParams(vmem_limit_bytes=56 << 20),
         name="product",
     )(w_rows, t_rows)
-    return out.reshape(rows, width)
+    return out.reshape(8, rows // 8, width)
 
 
 def send_kernel(where, occ, virt, target, parts_ref, out_ref, total):
@@ -234,7 +248,8 @@
 def contract(turns, w_rows, t_rows, *masks):
     partial = product(turns, w_rows, t_rows)
     by_z = lax.psum_scatter(partial, "z", scatter_dimension=0, tiled=True)
-    by_x = lax.all_to_all(by_z, "x", 0, 0, tiled=True).reshape(4, BLOCK, turns * VCAP)
+    by_z = by_z.reshape(4, BLOCK, turns * VCAP)
+    by_x = lax.all_to_all(by_z, "x", 0, 0, tiled=True)
     return lax.all_to_all(send_out(by_x, *masks), ("y", "core"), 0, 0, tiled=True)
 
 

time: 153 us -> 159 us (1.039)
  blocking collectives: 75.3 us -> 82.2 us
  waiting for transfers between devices: 49.6 us -> 47.3 us
    all_to_all x1, blocking collectives: 42.9 us -> 48.8 us  [bring(): lax.all_to_all(dealt[SIZES.index(turns)], ('y', 'core'), 0, 0, tiled=True)]
    all_gather x1, waiting for transfers between devices: 8.67 us -> 4.61 us  [per_device(): w_rows = lax.all_gather(w_cycle, ('y', 'core'), axis=0, tiled=True)]
    reduce_scatter x1, waiting for transfers between devices: 40.2 us -> 42 us  [contract(): by_z = lax.psum_scatter(partial, 'z', scatter_dimension=0, tiled=True)]
where the time goes in v11:
time: 159 us; the launch traced here: 158 us
  blocking collectives  82.2 us (52%)
  waiting for transfers between devices  47.3 us (30%)
  between operations  14.7 us (9%)
  Pallas kernels  14 us (9%)
    all_to_all x1, blocking collectives, bring(): lax.all_to_all(dealt[SIZES.index(turns)], ('y', 'core'), 0, 0, tiled=True)  48.8 us
    reduce_scatter x1, waiting for transfers between devices, contract(): by_z = lax.psum_scatter(partial, 'z', scatter_dimension=0, tiled=True)  42 us
    all_to_all x1, blocking collectives, contract(): lax.all_to_all(send_out(by_x, *masks), ('y', 'core'), 0, 0, tiled=True)  23.3 us
    all_to_all x1, blocking collectives, contract(): by_x = lax.all_to_all(by_z, 'x', 0, 0, tiled=True)  10 us
    pallas_call x1, Pallas kernels, product(): pl.pallas_call(product_kernel, in_specs=[pl.BlockSpec(memory_space=pl.ANY...  5.7 us
    all_gather x1, waiting for transfers between devices, per_device(): w_rows = lax.all_gather(w_cycle, ('y', 'core'), axis=0, tiled=True)  4.61 us
    pallas_call x1, Pallas kernels, deal(): pl.pallas_call(deal_kernel, in_specs=[scalars()] * 3 + [pl.BlockSpec(memo...  4.12 us
  transfers between devices with their start and end apart: 2, of which 2 were waited for; matrix products, arithmetic and copies ran while one was open for 0% of the time, Pallas kernels for 4%

profile of v11, /device:TPU:1, one launch (start us, length us, event | category | flops | bytes accessed | tf_op | source)
XLA Modules:
  0.0 158.4 jit_solution(10090255586246363987)
XLA Ops:
  6.5 0.0 copy-start
  6.5 0.0 copy-start.1
  6.5 0.0 all-gather.2.cloned.1.call-start
  6.5 0.7 all-gather.2.cloned.1.call-update
  7.9 4.1 %deal.1 = (bf16[16,6,5,8,128]{4,3,2,1,0:T(8,128)(2,1)S(1)}, bf16[16,6,6,8,128]{4,3,2,1,0:T(8,128)(2,1)S(1)}, bf16[16,6,8,8,128]{4,3,2,1,0:T(8,128)(2,1)S(1)}, s32[1]{0:T(128)}) custom-call(s32[8]{0:T(128)} %occ.3, s32[8]{0:T(128)} %virt.3, s32[1]{0:T(128)S(6)} %copy.12.target, bf16[6,192,8,128]{3,2,1,0:T(8,128)(2,1)} %t_ref.1), custom_call_target="tpu_custom_call" | custom-call | tf_op jit(solution)/shard_map/deal/pallas_call | solution.py:91
  12.0 0.1 pad_add_fusion.where
  12.8 0.0 copy-done
  12.8 0.0 copy-done.1
  12.8 50.4 %conditional.2 = (bf16[768,1024]{1,0:T(8,128)(2,1)S(1)}) conditional(s32[]{:T(128)} %bitcast.11, (bf16[16,6,5,8,128]{4,3,2,1,0:T(8,128)(2,1)S(1)}, s32[2]{0:T(128)S(1)}, s32[8]{0:T(128)S(1)}, s32[8]{0:T(128)S(1)}, s32[1]{0:T(128)}) %tuple.47, (bf16[16,6,6,8,128]{4,3,2,1,0:T(8,128)(2,1)S(1)}, s32[2]{0:T(128)S(1)}, s32[8]{0:T(128)S(1)}, ...), branch_computations={%region_0.0_spmd, %region_1.0_spmd, %region_2.0_spmd} | conditional | bytes 3145736 | solution.py:262
  12.8 48.8 %all_to_all.37 = bf16[16,6,6,8,128]{4,3,2,1,0:T(8,128)(2,1)S(1)} all-to-all(bf16[16,6,6,8,128]{4,3,2,1,0:T(8,128)(2,1)S(1)} %get-tuple-element.88), channel_id=1, replica_groups=mesh['y'=8,'core'=2,'x'=4,'z'=8] {'y','core'}, dimensions={0} | all-to-all | bytes 2359296 | tf_op jit(solution)/shard_map/cond/branch_1_fun/all_to_all | solution.py:244
  61.6 1.6 %repack.4 = bf16[768,1024]{1,0:T(8,128)(2,1)S(1)} custom-call(s32[2]{0:T(128)S(1)} %get-tuple-element.84.where, s32[8]{0:T(128)S(1)} %get-tuple-element.85.occ, s32[8]{0:T(128)S(1)} %get-tuple-element.86.virt, s32[1]{0:T(128)} %get-tuple-element.87.target, bf16[96,6,8,128]{3,2,1,0:T(8,128)(2,1)S(1)} %bitcast.13), custom_call_target="tpu_custom_call" | custom-call | tf_op jit(solution)/shard_map/cond/branch_1_fun/repack/pallas_call | solution.py:124
  63.2 4.6 %all-gather.2.cloned.1.call-done = bf16[1536,768]{1,0:T(8,128)(2,1)} async-done(((bf16[96,768]{1,0:T(8,128)(2,1)}), bf16[1536,768]{1,0:T(8,128)(2,1)}) %all-gather.2.cloned.1.call-update) | async-done | bytes 2359312 | tf_op jit(solution)/shard_map/all_gather | solution.py:261
  67.8 82.3 %conditional.3 = (bf16[16,48,128]{2,1,0:T(8,128)(2,1)S(1)}) conditional(s32[]{:T(128)} %bitcast.11, (bf16[1536,768]{1,0:T(8,128)(2,1)}, bf16[768,1024]{1,0:T(8,128)(2,1)S(1)}, s32[2]{0:T(128)S(1)}, s32[8]{0:T(128)S(1)}, s32[8]{0:T(128)S(1)}, /*index=5*/s32[1]{0:T(128)}) %tuple.50, (bf16[1536,768]{1,0:T(8,128)(2,1)}, ...), branch_computations={%region_3.0_spmd, %region_5.0_spmd, %region_7.0_spmd} | conditional | bytes 11796528 | solution.py:265
  67.8 0.0 reduce-scatter.6.cloned.1.call-start
  67.8 5.7 %product.4 = bf16[8,4,48,768]{3,2,1,0:T(8,128)(2,1)} custom-call(bf16[1536,768]{1,0:T(8,128)(2,1)} %get-tuple-element.104.w_ref, bf16[768,1024]{1,0:T(8,128)(2,1)S(1)} %get-tuple-element.105.t_ref), custom_call_target="tpu_custom_call" | custom-call | tf_op jit(solution)/shard_map/cond/branch_1_fun/product/pallas_call | solution.py:163
  73.5 0.0 reduce-scatter.6.cloned.1.call-update
  73.6 42.0 %reduce-scatter.6.cloned.1.call-done = bf16[1,192,768]{2,1,0:T(8,128)(2,1)} async-done(((bf16[8,192,768]{2,1,0:T(8,128)(2,1)}), bf16[1,192,768]{2,1,0:T(8,128)(2,1)}) %reduce-scatter.6.cloned.1.call-update) | async-done | bytes 294928 | tf_op jit(solution)/shard_map/cond/branch_1_fun/reduce_scatter | solution.py:250
  115.5 10.0 %all_to_all.41.parts_ref = bf16[4,48,768]{2,1,0:T(8,128)(2,1)S(1)} all-to-all(bf16[4,48,768]{2,1,0:T(8,128)(2,1)} %bitcast.19), channel_id=1, replica_groups=mesh['y'=8,'core'=2,'x'=4,'z'=8] {'x'}, dimensions={0} | all-to-all | bytes 589824 | tf_op jit(solution)/shard_map/cond/branch_1_fun/all_to_all | solution.py:252
  125.6 1.3 send_out.4
  126.8 23.3 %all_to_all.42 = bf16[16,48,128]{2,1,0:T(8,128)(2,1)S(1)} all-to-all(bf16[16,48,128]{2,1,0:T(8,128)(2,1)S(1)} %send_out.4), channel_id=1, replica_groups=mesh['y'=8,'core'=2,'x'=4,'z'=8] {'y','core'}, dimensions={0} | all-to-all | bytes 393216 | tf_op jit(solution)/shard_map/cond/branch_1_fun/all_to_all | solution.py:253
  150.2 1.4 place.1
Async XLA Ops:
  6.5 6.2 %copy-start = (s32[8]{0:T(128)S(1)}, s32[8]{0:T(128)}, u32[]{:S(2)}) copy-start(s32[8]{0:T(128)} %occ.3) | copy-start | bytes 100
  6.5 6.2 %copy-start.1 = (s32[8]{0:T(128)S(1)}, s32[8]{0:T(128)}, u32[]{:S(2)}) copy-start(s32[8]{0:T(128)} %virt.3) | copy-start | bytes 100
  6.5 61.3 %all-gather.2.cloned.1.call-start = ((), (), s32[]{:S(2)}) async-start(), calls=%async_computation.15 | async-start | bytes 2506752 | tf_op jit(solution)/shard_map/all_gather | solution.py:261
  67.8 47.7 %reduce-scatter.6.cloned.1.call-start = ((), (), s32[]{:S(2)}) async-start(), calls=%async_computation.13 | async-start | bytes 2654208 | tf_op jit(solution)/shard_map/cond/branch_1_fun/reduce_scatter | solution.py:250
Sparse Core Ops, SparseCore 0:
  9.7 58.0 all-gather.1
  73.7 41.8 reduce-scatter.5

commit v12 on v10

--- a/solution.py
+++ b/solution.py
@@ -35,7 +35,7 @@
 
 
 def size_class(pairs):
-    return sum((pairs > (ROWS * turns - 1) * VCAP).astype(jnp.int32) for turns in SIZES[:-1])
+    return sum((pairs > ROWS * turns * VCAP).astype(jnp.int32) for turns in SIZES[:-1])
 
 
 def deal_kernel(occ, virt, target, t_ref, *rest):
@@ -160,7 +160,7 @@
         compiler_params=pltpu.CompilerParams(vmem_limit_bytes=24 << 20),
         name="product",
     )(w_rows, t_rows)
-    return out.reshape(rows, width)
+    return out.reshape(8, rows // 8, width)
 
 
 def send_kernel(where, occ, virt, target, parts_ref, out_ref, total):
@@ -234,7 +234,7 @@
 def contract(turns, w_rows, t_rows, *masks):
     partial = product(turns, w_rows, t_rows)
     by_z = lax.psum_scatter(partial, "z", scatter_dimension=0, tiled=True)
-    by_x = lax.all_to_all(by_z, "x", 0, 0, tiled=True).reshape(4, BLOCK, turns * VCAP)
+    by_x = lax.all_to_all(by_z.reshape(4, BLOCK, turns * VCAP), "x", 0, 0, tiled=True)
     return lax.all_to_all(send_out(by_x, *masks), ("y", "core"), 0, 0, tiled=True)
 
 

time: 153 us -> 153 us (level)
  no operation moved by 1% of the time
where the time goes in v12:
time: 153 us
  blocking collectives  76.5 us (50%)
  waiting for transfers between devices  48.6 us (32%)
  between operations  14.7 us (10%)
  Pallas kernels  12.7 us (8%)
    all_to_all x1, blocking collectives, bring(): lax.all_to_all(dealt[SIZES.index(turns)], ('y', 'core'), 0, 0, tiled=True)  42.9 us
    reduce_scatter x1, waiting for transfers between devices, contract(): by_z = lax.psum_scatter(partial, 'z', scatter_dimension=0, tiled=True)  39.2 us
    all_to_all x1, blocking collectives, contract(): lax.all_to_all(send_out(by_x, *masks), ('y', 'core'), 0, 0, tiled=True)  23.1 us
    all_to_all x1, blocking collectives, contract(): lax.all_to_all(by_z.reshape(4, BLOCK, turns * VCAP), 'x', 0, 0, tiled=True)  10.5 us
    all_gather x1, waiting for transfers between devices, per_device(): w_rows = lax.all_gather(w_cycle, ('y', 'core'), axis=0, tiled=True)  8.67 us
    pallas_call x1, Pallas kernels, product(): pl.pallas_call(product_kernel, in_specs=[pl.BlockSpec(memory_space=pltpu....  4.5 us
    pallas_call x1, Pallas kernels, deal(): pl.pallas_call(deal_kernel, in_specs=[scalars()] * 3 + [pl.BlockSpec(memo...  4.1 us
  transfers between devices with their start and end apart: 2, of which 2 were waited for; matrix products, arithmetic and copies ran while one was open for 0% of the time, Pallas kernels for 4%

profile of v12, /device:TPU:1, one launch (start us, length us, event | category | flops | bytes accessed | tf_op | source)
XLA Modules:
  0.0 152.7 jit_solution(8596358352318767700)
XLA Ops:
  6.5 0.0 copy-start
  6.5 0.0 copy-start.1
  6.5 0.0 all-gather.2.cloned.1.call-start
  6.5 0.7 all-gather.2.cloned.1.call-update
  7.9 4.1 %deal.1 = (bf16[16,6,5,8,128]{4,3,2,1,0:T(8,128)(2,1)S(1)}, bf16[16,6,6,8,128]{4,3,2,1,0:T(8,128)(2,1)S(1)}, bf16[16,6,8,8,128]{4,3,2,1,0:T(8,128)(2,1)S(1)}, s32[1]{0:T(128)}) custom-call(s32[8]{0:T(128)} %occ.3, s32[8]{0:T(128)} %virt.3, s32[1]{0:T(128)S(6)} %copy.12.target, bf16[6,192,8,128]{3,2,1,0:T(8,128)(2,1)} %t_ref.1), custom_call_target="tpu_custom_call" | custom-call | tf_op jit(solution)/shard_map/deal/pallas_call | solution.py:91
  12.0 0.1 pad_add_fusion.where
  12.7 0.0 copy-done
  12.7 0.0 copy-done.1
  12.7 44.5 %conditional.2 = (bf16[768,1024]{1,0:T(8,128)(2,1)S(1)}) conditional(s32[]{:T(128)} %bitcast.11, (bf16[16,6,5,8,128]{4,3,2,1,0:T(8,128)(2,1)S(1)}, s32[2]{0:T(128)S(1)}, s32[8]{0:T(128)S(1)}, s32[8]{0:T(128)S(1)}, s32[1]{0:T(128)}) %tuple.47, (bf16[16,6,6,8,128]{4,3,2,1,0:T(8,128)(2,1)S(1)}, s32[2]{0:T(128)S(1)}, s32[8]{0:T(128)S(1)}, ...), branch_computations={%region_0.0_spmd, %region_1.0_spmd, %region_2.0_spmd} | conditional | bytes 3145736 | solution.py:247
  12.8 42.9 %all_to_all.36 = bf16[16,6,5,8,128]{4,3,2,1,0:T(8,128)(2,1)S(1)} all-to-all(bf16[16,6,5,8,128]{4,3,2,1,0:T(8,128)(2,1)S(1)} %get-tuple-element.83), channel_id=1, replica_groups=mesh['y'=8,'core'=2,'x'=4,'z'=8] {'y','core'}, dimensions={0} | all-to-all | bytes 1966080 | tf_op jit(solution)/shard_map/cond/branch_0_fun/all_to_all | solution.py:230
  55.7 1.5 %repack.3 = bf16[768,1024]{1,0:T(8,128)(2,1)S(1)} custom-call(s32[2]{0:T(128)S(1)} %get-tuple-element.70.where, s32[8]{0:T(128)S(1)} %get-tuple-element.78.occ, s32[8]{0:T(128)S(1)} %get-tuple-element.80.virt, s32[1]{0:T(128)} %get-tuple-element.82.target, bf16[96,5,8,128]{3,2,1,0:T(8,128)(2,1)S(1)} %bitcast.14), custom_call_target="tpu_custom_call" | custom-call | tf_op jit(solution)/shard_map/cond/branch_0_fun/repack/pallas_call | solution.py:124
  57.3 8.7 %all-gather.2.cloned.1.call-done = bf16[1536,768]{1,0:T(8,128)(2,1)} async-done(((bf16[96,768]{1,0:T(8,128)(2,1)}), bf16[1536,768]{1,0:T(8,128)(2,1)}) %all-gather.2.cloned.1.call-update) | async-done | bytes 2359312 | tf_op jit(solution)/shard_map/all_gather | solution.py:246
  65.9 78.6 %conditional.3 = (bf16[16,48,128]{2,1,0:T(8,128)(2,1)S(1)}) conditional(s32[]{:T(128)} %bitcast.11, (bf16[1536,768]{1,0:T(8,128)(2,1)}, bf16[768,1024]{1,0:T(8,128)(2,1)S(1)}, s32[2]{0:T(128)S(1)}, s32[8]{0:T(128)S(1)}, s32[8]{0:T(128)S(1)}, /*index=5*/s32[1]{0:T(128)}) %tuple.50, (bf16[1536,768]{1,0:T(8,128)(2,1)}, ...), branch_computations={%region_3.0_spmd, %region_5.0_spmd, %region_7.0_spmd} | conditional | bytes 11796528 | solution.py:250
  65.9 0.0 reduce-scatter.4.cloned.1.call-start
  65.9 4.5 %product.3 = bf16[8,4,48,640]{3,2,1,0:T(8,128)(2,1)} custom-call(bf16[1536,768]{1,0:T(8,128)(2,1)} %get-tuple-element.98.w_ref, bf16[768,1024]{1,0:T(8,128)(2,1)S(1)} %get-tuple-element.99.t_ref), custom_call_target="tpu_custom_call" | custom-call | tf_op jit(solution)/shard_map/cond/branch_0_fun/product/pallas_call | solution.py:154
  70.4 0.0 reduce-scatter.4.cloned.1.call-update
  70.5 39.2 %reduce-scatter.4.cloned.1.call-done = bf16[1,192,640]{2,1,0:T(8,128)(2,1)} async-done(((bf16[8,192,640]{2,1,0:T(8,128)(2,1)}), bf16[1,192,640]{2,1,0:T(8,128)(2,1)}) %reduce-scatter.4.cloned.1.call-update) | async-done | bytes 245776 | tf_op jit(solution)/shard_map/cond/branch_0_fun/reduce_scatter | solution.py:236
  109.7 10.5 %all_to_all.39.parts_ref = bf16[4,48,640]{2,1,0:T(8,128)(2,1)S(1)} all-to-all(bf16[4,48,640]{2,1,0:T(8,128)(2,1)} %bitcast.17), channel_id=1, replica_groups=mesh['y'=8,'core'=2,'x'=4,'z'=8] {'x'}, dimensions={0} | all-to-all | bytes 491520 | tf_op jit(solution)/shard_map/cond/branch_0_fun/all_to_all | solution.py:237
  120.1 1.3 send_out.3
  121.4 23.1 %all_to_all.40 = bf16[16,48,128]{2,1,0:T(8,128)(2,1)S(1)} all-to-all(bf16[16,48,128]{2,1,0:T(8,128)(2,1)S(1)} %send_out.3), channel_id=1, replica_groups=mesh['y'=8,'core'=2,'x'=4,'z'=8] {'y','core'}, dimensions={0} | all-to-all | bytes 393216 | tf_op jit(solution)/shard_map/cond/branch_0_fun/all_to_all | solution.py:238
  144.5 1.4 place.1
Async XLA Ops:
  6.5 6.2 %copy-start = (s32[8]{0:T(128)S(1)}, s32[8]{0:T(128)}, u32[]{:S(2)}) copy-start(s32[8]{0:T(128)} %occ.3) | copy-start | bytes 100
  6.5 6.2 %copy-start.1 = (s32[8]{0:T(128)S(1)}, s32[8]{0:T(128)}, u32[]{:S(2)}) copy-start(s32[8]{0:T(128)} %virt.3) | copy-start | bytes 100
  6.5 59.4 %all-gather.2.cloned.1.call-start = ((), (), s32[]{:S(2)}) async-start(), calls=%async_computation.15 | async-start | bytes 2506752 | tf_op jit(solution)/shard_map/all_gather | solution.py:246
  65.9 43.7 %reduce-scatter.4.cloned.1.call-start = ((), (), s32[]{:S(2)}) async-start(), calls=%async_computation.12 | async-start | bytes 2211840 | tf_op jit(solution)/shard_map/cond/branch_0_fun/reduce_scatter | solution.py:236
Sparse Core Ops, SparseCore 0:
  9.7 56.1 all-gather.1
  70.6 39.0 reduce-scatter.3

commit v13 on v12

--- a/solution.py
+++ b/solution.py
@@ -35,23 +35,14 @@
 
 
 def size_class(pairs):
-    return sum((pairs > ROWS * turns * VCAP).astype(jnp.int32) for turns in SIZES[:-1])
-
-
-def deal_kernel(occ, virt, target, t_ref, *rest):
-    results, (class_ref, held, packed, sem, out_sem) = rest[:len(SIZES)], rest[len(SIZES):]
-    copies = [
-        pltpu.make_async_copy(
-            t_ref.at[:, h * OCAP:(h + 1) * OCAP], held.at[:, h * OCAP:(h + 1) * OCAP], sem.at[h]
-        )
-        for h in range(IRREPS)
-    ]
-    for copy in copies:
-        copy.start()
+    return sum((pairs >= ROWS * turns * VCAP).astype(jnp.int32) for turns in SIZES[:-1])
+
+
+def pack(occ, virt, target, held, copies, out_ref):
     lane = lax.broadcasted_iota(jnp.int32, (48, VCAP), 1)
 
     def put(p, value):
-        packed[jnp.bitwise_and(p, 15), :, lax.shift_right_logical(p, 4)] = (
+        out_ref[jnp.bitwise_and(p, 15), :, lax.shift_right_logical(p, 4)] = (
             value.astype(BF).reshape(6, 8, VCAP)
         )
 
@@ -77,28 +68,36 @@
         current = lax.fori_loop(0, (many + STEP - 1) // STEP, some, current)
         first = first + many * wide
     put(lax.shift_right_logical(first, 7), current)
-    which = size_class(first)
+
+
+def deal_kernel(occ, virt, target, t_ref, *rest):
+    results, (class_ref, held, sem) = rest[:len(SIZES)], rest[len(SIZES):]
+    copies = [
+        pltpu.make_async_copy(
+            t_ref.at[:, h * OCAP:(h + 1) * OCAP], held.at[:, h * OCAP:(h + 1) * OCAP], sem.at[h]
+        )
+        for h in range(IRREPS)
+    ]
+    for copy in copies:
+        copy.start()
+    which = size_class(first_column(occ, virt, target, IRREPS))
     class_ref[0] = which
-    for n, turns in enumerate(SIZES):
+    for n in range(len(SIZES)):
         @pl.when(which == n)
-        def _(n=n, turns=turns):
-            copy = pltpu.make_async_copy(packed.at[:, :, :turns], results[n], out_sem)
-            copy.start()
-            copy.wait()
+        def _(n=n):
+            pack(occ, virt, target, held, copies, results[n])
 
 
 def deal(amplitudes, occ_count, virt_count, target):
     return pl.pallas_call(
         deal_kernel,
         in_specs=[scalars()] * 3 + [pl.BlockSpec(memory_space=pl.ANY)],
-        out_specs=[pl.BlockSpec(memory_space=pl.ANY)] * len(SIZES) + [scalars()],
+        out_specs=[pl.BlockSpec(memory_space=pltpu.VMEM)] * len(SIZES) + [scalars()],
         out_shape=[jax.ShapeDtypeStruct((ROWS, 6, turns, 8, VCAP), BF) for turns in SIZES]
         + [jax.ShapeDtypeStruct((1,), jnp.int32)],
         scratch_shapes=[
             pltpu.VMEM((6, KO, 8, VCAP), BF),
-            pltpu.VMEM((ROWS, 6, SIZES[-1], 8, VCAP), BF),
             pltpu.SemaphoreType.DMA((IRREPS,)),
-            pltpu.SemaphoreType.DMA,
         ],
         compiler_params=pltpu.CompilerParams(vmem_limit_bytes=56 << 20),
         name="deal",

time: 153 us -> 155 us (1.013); the launches traced: 153 us -> 157 us
  blocking collectives: 76.5 us -> 81.9 us
    all_to_all x1, blocking collectives: 42.9 us -> 48.7 us  [bring(): lax.all_to_all(dealt[SIZES.index(turns)], ('y', 'core'), 0, 0, tiled=True)]
    all_gather x1, waiting for transfers between devices: 8.67 us -> 4.72 us  [per_device(): w_rows = lax.all_gather(w_cycle, ('y', 'core'), axis=0, tiled=True)]
    reduce_scatter x1, waiting for transfers between devices: 39.2 us -> 42.5 us  [contract(): by_z = lax.psum_scatter(partial, 'z', scatter_dimension=0, tiled=True)]
where the time goes in v13:
time: 155 us; the launch traced here: 157 us
  blocking collectives  81.9 us (53%)
  waiting for transfers between devices  47.9 us (31%)
  between operations  14.7 us (9%)
  Pallas kernels  12.6 us (8%)
    all_to_all x1, blocking collectives, bring(): lax.all_to_all(dealt[SIZES.index(turns)], ('y', 'core'), 0, 0, tiled=True)  48.7 us
    reduce_scatter x1, waiting for transfers between devices, contract(): by_z = lax.psum_scatter(partial, 'z', scatter_dimension=0, tiled=True)  42.5 us
    all_to_all x1, blocking collectives, contract(): lax.all_to_all(send_out(by_x, *masks), ('y', 'core'), 0, 0, tiled=True)  23.4 us
    all_to_all x1, blocking collectives, contract(): lax.all_to_all(by_z.reshape(4, BLOCK, turns * VCAP), 'x', 0, 0, tiled=True)  9.79 us
    all_gather x1, waiting for transfers between devices, per_device(): w_rows = lax.all_gather(w_cycle, ('y', 'core'), axis=0, tiled=True)  4.72 us
    pallas_call x1, Pallas kernels, product(): pl.pallas_call(product_kernel, in_specs=[pl.BlockSpec(memory_space=pltpu....  4.52 us
    pallas_call x1, Pallas kernels, deal(): pl.pallas_call(deal_kernel, in_specs=[scalars()] * 3 + [pl.BlockSpec(memo...  3.91 us
  transfers between devices with their start and end apart: 2, of which 2 were waited for; matrix products, arithmetic and copies ran while one was open for 0% of the time, Pallas kernels for 4%

profile of v13, /device:TPU:1, one launch (start us, length us, event | category | flops | bytes accessed | tf_op | source)
XLA Modules:
  0.0 157.3 jit_solution(5234572652090996003)
XLA Ops:
  6.5 0.0 copy-start
  6.5 0.0 copy-start.1
  6.5 0.0 all-gather.2.cloned.1.call-start
  6.5 0.7 all-gather.2.cloned.1.call-update
  7.9 3.9 %deal.1 = (bf16[16,6,5,8,128]{4,3,2,1,0:T(8,128)(2,1)S(1)}, bf16[16,6,6,8,128]{4,3,2,1,0:T(8,128)(2,1)S(1)}, bf16[16,6,8,8,128]{4,3,2,1,0:T(8,128)(2,1)S(1)}, s32[1]{0:T(128)}) custom-call(s32[8]{0:T(128)} %occ.3, s32[8]{0:T(128)} %virt.3, s32[1]{0:T(128)S(6)} %copy.12.target, bf16[6,192,8,128]{3,2,1,0:T(8,128)(2,1)} %t_ref.1), custom_call_target="tpu_custom_call" | custom-call | tf_op jit(solution)/shard_map/deal/pallas_call | solution.py:92
  11.8 0.1 pad_add_fusion.where
  12.5 0.0 copy-done
  12.6 0.0 copy-done.1
  12.6 50.4 %conditional.2 = (bf16[768,1024]{1,0:T(8,128)(2,1)S(1)}) conditional(s32[]{:T(128)} %bitcast.11, (bf16[16,6,5,8,128]{4,3,2,1,0:T(8,128)(2,1)S(1)}, s32[2]{0:T(128)S(1)}, s32[8]{0:T(128)S(1)}, s32[8]{0:T(128)S(1)}, s32[1]{0:T(128)}) %tuple.47, (bf16[16,6,6,8,128]{4,3,2,1,0:T(8,128)(2,1)S(1)}, s32[2]{0:T(128)S(1)}, s32[8]{0:T(128)S(1)}, ...), branch_computations={%region_0.0_spmd, %region_1.0_spmd, %region_2.0_spmd} | conditional | bytes 3145736 | solution.py:246
  12.6 48.7 %all_to_all.37 = bf16[16,6,6,8,128]{4,3,2,1,0:T(8,128)(2,1)S(1)} all-to-all(bf16[16,6,6,8,128]{4,3,2,1,0:T(8,128)(2,1)S(1)} %get-tuple-element.88), channel_id=1, replica_groups=mesh['y'=8,'core'=2,'x'=4,'z'=8] {'y','core'}, dimensions={0} | all-to-all | bytes 2359296 | tf_op jit(solution)/shard_map/cond/branch_1_fun/all_to_all | solution.py:229
  61.3 1.6 %repack.4 = bf16[768,1024]{1,0:T(8,128)(2,1)S(1)} custom-call(s32[2]{0:T(128)S(1)} %get-tuple-element.84.where, s32[8]{0:T(128)S(1)} %get-tuple-element.85.occ, s32[8]{0:T(128)S(1)} %get-tuple-element.86.virt, s32[1]{0:T(128)} %get-tuple-element.87.target, bf16[96,6,8,128]{3,2,1,0:T(8,128)(2,1)S(1)} %bitcast.13), custom_call_target="tpu_custom_call" | custom-call | tf_op jit(solution)/shard_map/cond/branch_1_fun/repack/pallas_call | solution.py:123
  62.9 4.7 %all-gather.2.cloned.1.call-done = bf16[1536,768]{1,0:T(8,128)(2,1)} async-done(((bf16[96,768]{1,0:T(8,128)(2,1)}), bf16[1536,768]{1,0:T(8,128)(2,1)}) %all-gather.2.cloned.1.call-update) | async-done | bytes 2359312 | tf_op jit(solution)/shard_map/all_gather | solution.py:245
  67.7 81.5 %conditional.3 = (bf16[16,48,128]{2,1,0:T(8,128)(2,1)S(1)}) conditional(s32[]{:T(128)} %bitcast.11, (bf16[1536,768]{1,0:T(8,128)(2,1)}, bf16[768,1024]{1,0:T(8,128)(2,1)S(1)}, s32[2]{0:T(128)S(1)}, s32[8]{0:T(128)S(1)}, s32[8]{0:T(128)S(1)}, /*index=5*/s32[1]{0:T(128)}) %tuple.50, (bf16[1536,768]{1,0:T(8,128)(2,1)}, ...), branch_computations={%region_3.0_spmd, %region_5.0_spmd, %region_7.0_spmd} | conditional | bytes 11796528 | solution.py:249
  67.7 0.0 reduce-scatter.6.cloned.1.call-start
  67.7 4.5 %product.4 = bf16[8,4,48,768]{3,2,1,0:T(8,128)(2,1)} custom-call(bf16[1536,768]{1,0:T(8,128)(2,1)} %get-tuple-element.104.w_ref, bf16[768,1024]{1,0:T(8,128)(2,1)S(1)} %get-tuple-element.105.t_ref), custom_call_target="tpu_custom_call" | custom-call | tf_op jit(solution)/shard_map/cond/branch_1_fun/product/pallas_call | solution.py:153
  72.2 0.0 reduce-scatter.6.cloned.1.call-update
  72.2 42.5 %reduce-scatter.6.cloned.1.call-done = bf16[1,192,768]{2,1,0:T(8,128)(2,1)} async-done(((bf16[8,192,768]{2,1,0:T(8,128)(2,1)}), bf16[1,192,768]{2,1,0:T(8,128)(2,1)}) %reduce-scatter.6.cloned.1.call-update) | async-done | bytes 294928 | tf_op jit(solution)/shard_map/cond/branch_1_fun/reduce_scatter | solution.py:235
  114.7 9.8 %all_to_all.41.parts_ref = bf16[4,48,768]{2,1,0:T(8,128)(2,1)S(1)} all-to-all(bf16[4,48,768]{2,1,0:T(8,128)(2,1)} %bitcast.16), channel_id=1, replica_groups=mesh['y'=8,'core'=2,'x'=4,'z'=8] {'x'}, dimensions={0} | all-to-all | bytes 589824 | tf_op jit(solution)/shard_map/cond/branch_1_fun/all_to_all | solution.py:236
  124.5 1.3 send_out.4
  125.7 23.4 %all_to_all.42 = bf16[16,48,128]{2,1,0:T(8,128)(2,1)S(1)} all-to-all(bf16[16,48,128]{2,1,0:T(8,128)(2,1)S(1)} %send_out.4), channel_id=1, replica_groups=mesh['y'=8,'core'=2,'x'=4,'z'=8] {'y','core'}, dimensions={0} | all-to-all | bytes 393216 | tf_op jit(solution)/shard_map/cond/branch_1_fun/all_to_all | solution.py:237
  149.1 1.4 place.1
Async XLA Ops:
  6.5 6.0 %copy-start = (s32[8]{0:T(128)S(1)}, s32[8]{0:T(128)}, u32[]{:S(2)}) copy-start(s32[8]{0:T(128)} %occ.3) | copy-start | bytes 100
  6.5 6.0 %copy-start.1 = (s32[8]{0:T(128)S(1)}, s32[8]{0:T(128)}, u32[]{:S(2)}) copy-start(s32[8]{0:T(128)} %virt.3) | copy-start | bytes 100
  6.5 61.1 %all-gather.2.cloned.1.call-start = ((), (), s32[]{:S(2)}) async-start(), calls=%async_computation.15 | async-start | bytes 2506752 | tf_op jit(solution)/shard_map/all_gather | solution.py:245
  67.7 47.0 %reduce-scatter.6.cloned.1.call-start = ((), (), s32[]{:S(2)}) async-start(), calls=%async_computation.13 | async-start | bytes 2654208 | tf_op jit(solution)/shard_map/cond/branch_1_fun/reduce_scatter | solution.py:235
Sparse Core Ops, SparseCore 0:
  9.7 57.9 all-gather.1
  72.3 42.3 reduce-scatter.5

commit v14 on v12

--- a/solution.py
+++ b/solution.py
@@ -163,14 +163,8 @@
     return out.reshape(8, rows // 8, width)
 
 
-def send_kernel(where, occ, virt, target, parts_ref, out_ref, total):
-    turns = total.shape[0]
-    for turn in range(turns):
-        at = turn * VCAP
-        added = parts_ref[0, :, at:at + VCAP].astype(F32)
-        for x in range(1, 4):
-            added = added + parts_ref[x, :, at:at + VCAP].astype(F32)
-        total[turn] = added.astype(BF)
+def send_kernel(where, occ, virt, target, parts_ref, out_ref):
+    turns = parts_ref.shape[2] // VCAP
     mine = where[0]
     first = jnp.int32(0)
     for h in range(IRREPS):
@@ -178,7 +172,10 @@
         for e in range(2):
             begin = lax.shift_right_logical(first + 12 * e * wide, 7)
             p = begin + jnp.bitwise_and(mine - begin + 16 * ROWS, 15)
-            out_ref[2 * h + e] = total[jnp.minimum(lax.shift_right_logical(p, 4), turns - 1)]
+            turn = jnp.minimum(lax.shift_right_logical(p, 4), turns - 1)
+            at = pl.ds(pl.multiple_of(turn * VCAP, VCAP), VCAP)
+            for x in range(4):
+                out_ref[4 * (2 * h + e) + x] = parts_ref[x, :, at]
         first = first + occ[h] * wide
 
 
@@ -187,14 +184,18 @@
         send_kernel,
         in_specs=[scalars()] * 4 + [pl.BlockSpec(memory_space=pltpu.VMEM)],
         out_specs=pl.BlockSpec(memory_space=pltpu.VMEM),
-        out_shape=jax.ShapeDtypeStruct((ROWS, BLOCK, VCAP), BF),
-        scratch_shapes=[pltpu.VMEM((parts.shape[2] // VCAP, BLOCK, VCAP), BF)],
+        out_shape=jax.ShapeDtypeStruct((4 * ROWS, BLOCK, VCAP), BF),
         compiler_params=pltpu.CompilerParams(vmem_limit_bytes=24 << 20),
         name="send_out",
     )(where, occ_count, virt_count, target, parts)
 
 
-def place_kernel(where, occ, virt, target, got_ref, out_ref):
+def place_kernel(where, occ, virt, target, got_ref, out_ref, total):
+    for q in range(ROWS):
+        added = got_ref[4 * q].astype(F32)
+        for x in range(1, 4):
+            added = added + got_ref[4 * q + x].astype(F32)
+        total[q] = added
     row, col = where[0], where[1]
     irrep, half = row // 2, row % 2
     first = first_column(occ, virt, target, irrep)
@@ -207,8 +208,8 @@
         at = first + s * wide
         p = lax.shift_right_logical(at, 7)
         shift = jnp.bitwise_and(at, 127)
-        here = got_ref[jnp.bitwise_and(p, 15)].astype(F32)
-        after = got_ref[jnp.bitwise_and(p + 1, 15)].astype(F32)
+        here = total[jnp.bitwise_and(p, 15)]
+        after = total[jnp.bitwise_and(p + 1, 15)]
         block = jnp.where(b >= shift, here, after)
         block = pltpu.roll(block, jnp.bitwise_and(VCAP - shift, 127), 1)
         keep = inside & (s < occ[irrep])
@@ -221,6 +222,7 @@
         in_specs=[scalars()] * 4 + [pl.BlockSpec(memory_space=pltpu.VMEM)],
         out_specs=pl.BlockSpec(memory_space=pltpu.VMEM),
         out_shape=jax.ShapeDtypeStruct((BLOCK, 12 * VCAP), BF),
+        scratch_shapes=[pltpu.VMEM((ROWS, BLOCK, VCAP), F32)],
         compiler_params=pltpu.CompilerParams(vmem_limit_bytes=32 << 20),
         name="place",
     )(where, occ_count, virt_count, target, got)
@@ -234,8 +236,8 @@
 def contract(turns, w_rows, t_rows, *masks):
     partial = product(turns, w_rows, t_rows)
     by_z = lax.psum_scatter(partial, "z", scatter_dimension=0, tiled=True)
-    by_x = lax.all_to_all(by_z.reshape(4, BLOCK, turns * VCAP), "x", 0, 0, tiled=True)
-    return lax.all_to_all(send_out(by_x, *masks), ("y", "core"), 0, 0, tiled=True)
+    out = send_out(by_z.reshape(4, BLOCK, turns * VCAP), *masks)
+    return lax.all_to_all(out, ("y", "core", "x"), 0, 0, tiled=True)
 
 
 def per_device(w_cycle, amplitudes, occ_count, virt_count, target):

time: 153 us -> 158 us (1.033)
  blocking collectives: 76.5 us -> 79.6 us
    all_to_all x2 -> x1, blocking collectives: 33.6 us -> 36.6 us  [contract(): return lax.all_to_all(out, ('y', 'core', 'x'), 0, 0, tiled=True)]
where the time goes in v14:
time: 158 us
  blocking collectives  79.6 us (50%)
  waiting for transfers between devices  49.5 us (31%)
  between operations  14.8 us (9%)
  Pallas kernels  12.9 us (8%)
    all_to_all x1, blocking collectives, bring(): lax.all_to_all(dealt[SIZES.index(turns)], ('y', 'core'), 0, 0, tiled=True)  43 us
    reduce_scatter x1, waiting for transfers between devices, contract(): by_z = lax.psum_scatter(partial, 'z', scatter_dimension=0, tiled=True)  40.1 us
    all_to_all x1, blocking collectives, contract(): return lax.all_to_all(out, ('y', 'core', 'x'), 0, 0, tiled=True)  36.6 us
    all_gather x1, waiting for transfers between devices, per_device(): w_rows = lax.all_gather(w_cycle, ('y', 'core'), axis=0, tiled=True)  8.66 us
    pallas_call x1, Pallas kernels, product(): pl.pallas_call(product_kernel, in_specs=[pl.BlockSpec(memory_space=pltpu....  4.49 us
    pallas_call x1, Pallas kernels, deal(): pl.pallas_call(deal_kernel, in_specs=[scalars()] * 3 + [pl.BlockSpec(memo...  4.09 us
  transfers between devices with their start and end apart: 2, of which 2 were waited for; matrix products, arithmetic and copies ran while one was open for 0% of the time, Pallas kernels for 4%

profile of v14, /device:TPU:1, one launch (start us, length us, event | category | flops | bytes accessed | tf_op | source)
XLA Modules:
  0.0 157.9 jit_solution(10017552227327395867)
XLA Ops:
  6.5 0.0 copy-start.3
  6.5 0.0 copy-start.4
  6.5 0.0 all-gather.2.cloned.1.call-start
  6.5 0.7 all-gather.2.cloned.1.call-update
  7.9 4.1 %deal.1 = (bf16[16,6,5,8,128]{4,3,2,1,0:T(8,128)(2,1)S(1)}, bf16[16,6,6,8,128]{4,3,2,1,0:T(8,128)(2,1)S(1)}, bf16[16,6,8,8,128]{4,3,2,1,0:T(8,128)(2,1)S(1)}, s32[1]{0:T(128)}) custom-call(s32[8]{0:T(128)} %occ.3, s32[8]{0:T(128)} %virt.3, s32[1]{0:T(128)S(6)} %copy.12.target, bf16[6,192,8,128]{3,2,1,0:T(8,128)(2,1)} %t_ref.1), custom_call_target="tpu_custom_call" | custom-call | tf_op jit(solution)/shard_map/deal/pallas_call | solution.py:91
  12.0 0.1 pad_add_fusion.where
  12.8 0.0 copy-done.3
  12.8 0.0 copy-done.4
  12.8 44.5 %conditional.2 = (bf16[768,1024]{1,0:T(8,128)(2,1)S(1)}) conditional(s32[]{:T(128)} %bitcast.11, (bf16[16,6,5,8,128]{4,3,2,1,0:T(8,128)(2,1)S(1)}, s32[2]{0:T(128)S(1)}, s32[8]{0:T(128)S(1)}, s32[8]{0:T(128)S(1)}, s32[1]{0:T(128)}) %tuple.47, (bf16[16,6,6,8,128]{4,3,2,1,0:T(8,128)(2,1)S(1)}, s32[2]{0:T(128)S(1)}, s32[8]{0:T(128)S(1)}, ...), branch_computations={%region_0.0_spmd, %region_1.0_spmd, %region_2.0_spmd} | conditional | bytes 3145736 | solution.py:249
  12.8 43.0 %all_to_all.24 = bf16[16,6,5,8,128]{4,3,2,1,0:T(8,128)(2,1)S(1)} all-to-all(bf16[16,6,5,8,128]{4,3,2,1,0:T(8,128)(2,1)S(1)} %get-tuple-element.83), channel_id=1, replica_groups=mesh['y'=8,'core'=2,'x'=4,'z'=8] {'y','core'}, dimensions={0} | all-to-all | bytes 1966080 | tf_op jit(solution)/shard_map/cond/branch_0_fun/all_to_all | solution.py:232
  55.8 1.5 repack.3
  57.4 8.7 %all-gather.2.cloned.1.call-done = bf16[1536,768]{1,0:T(8,128)(2,1)} async-done(((bf16[96,768]{1,0:T(8,128)(2,1)}), bf16[1536,768]{1,0:T(8,128)(2,1)}) %all-gather.2.cloned.1.call-update) | async-done | bytes 2359312 | tf_op jit(solution)/shard_map/all_gather | solution.py:248
  66.0 83.6 %conditional.3 = (bf16[64,48,128]{2,1,0:T(8,128)(2,1)S(1)}) conditional(s32[]{:T(128)} %bitcast.11, (bf16[1536,768]{1,0:T(8,128)(2,1)}, bf16[768,1024]{1,0:T(8,128)(2,1)S(1)}, s32[2]{0:T(128)S(1)}, s32[8]{0:T(128)S(1)}, s32[8]{0:T(128)S(1)}, /*index=5*/s32[1]{0:T(128)}) %tuple.50, (bf16[1536,768]{1,0:T(8,128)(2,1)}, ...), branch_computations={%region_3.0_spmd, %region_5.0_spmd, %region_7.0_spmd} | conditional | bytes 13762636 | solution.py:252
  66.0 0.0 reduce-scatter.4.cloned.1.call-start
  66.0 4.5 %product.3 = bf16[8,4,48,640]{3,2,1,0:T(8,128)(2,1)} custom-call(bf16[1536,768]{1,0:T(8,128)(2,1)} %get-tuple-element.98.w_ref, bf16[768,1024]{1,0:T(8,128)(2,1)S(1)} %get-tuple-element.99.t_ref), custom_call_target="tpu_custom_call" | custom-call | tf_op jit(solution)/shard_map/cond/branch_0_fun/product/pallas_call | solution.py:154
  70.5 0.0 reduce-scatter.4.cloned.1.call-update
  70.6 40.1 %reduce-scatter.4.cloned.1.call-done = bf16[1,192,640]{2,1,0:T(8,128)(2,1)} async-done(((bf16[8,192,640]{2,1,0:T(8,128)(2,1)}), bf16[1,192,640]{2,1,0:T(8,128)(2,1)}) %reduce-scatter.4.cloned.1.call-update) | async-done | bytes 245776 | tf_op jit(solution)/shard_map/cond/branch_0_fun/reduce_scatter | solution.py:238
  110.7 0.0 copy-start.2
  110.7 0.9 copy-done.2
  111.6 1.4 send_out.3
  113.0 36.6 %all_to_all.27 = bf16[64,48,128]{2,1,0:T(8,128)(2,1)S(1)} all-to-all(bf16[64,48,128]{2,1,0:T(8,128)(2,1)S(1)} %send_out.3), channel_id=1, replica_groups=mesh['y'=8,'core'=2,'x'=4,'z'=8] {'y','core','x'}, dimensions={0} | all-to-all | bytes 1572864 | tf_op jit(solution)/shard_map/cond/branch_0_fun/all_to_all | solution.py:240
  149.6 1.4 place.1
Async XLA Ops:
  6.5 6.3 %copy-start.3 = (s32[8]{0:T(128)S(1)}, s32[8]{0:T(128)}, u32[]{:S(2)}) copy-start(s32[8]{0:T(128)} %occ.3) | copy-start | bytes 100
  6.5 6.3 %copy-start.4 = (s32[8]{0:T(128)S(1)}, s32[8]{0:T(128)}, u32[]{:S(2)}) copy-start(s32[8]{0:T(128)} %virt.3) | copy-start | bytes 100
  6.5 59.5 %all-gather.2.cloned.1.call-start = ((), (), s32[]{:S(2)}) async-start(), calls=%async_computation.12 | async-start | bytes 2506752 | tf_op jit(solution)/shard_map/all_gather | solution.py:248
  66.0 44.7 %reduce-scatter.4.cloned.1.call-start = ((), (), s32[]{:S(2)}) async-start(), calls=%async_computation.9 | async-start | bytes 2211840 | tf_op jit(solution)/shard_map/cond/branch_0_fun/reduce_scatter | solution.py:238
  110.7 0.9 copy-start.2
Sparse Core Ops, SparseCore 0:
  9.7 56.2 all-gather.1
  70.7 39.9 reduce-scatter.3
